TPU v7x, 512 devices: a whole 4x4x16 slice. The times are simulated.
512 devices in a mesh: dp: 16 (over y_hi, x, core), fsdp: 32 (over z, y_lo).
Axes of the slice: x: 4, y: 4 (y_hi: 2, y_lo: 2; y = y_hi * 2 + y_lo), z: 16, core: 2. Of those that a mesh axis runs over, the one named last changes fastest.
Arguments:
- attention_output_rows: bfloat16 [131072, 1536], P(('dp', 'fsdp')), may hold values from -24 to 24
- cotangent: bfloat16 [131072, 3072], P(('dp', 'fsdp')), may hold values from -24 to 24
- quantized_weight_codes: bfloat16 [1536, 3072], P('fsdp'), may hold values from -1 to 1
- shard_absolute_maximum: bfloat16 [32], P('fsdp'), may hold values from 0.019897461 to 0.079589844
- adapter_down_weight: bfloat16 [1536, 128], P('fsdp'), may hold values from -0.15625 to 0.15625
- adapter_up_weight: bfloat16 [128, 3072], P(None, 'fsdp'), may hold values from -0.5 to 0.5
- timestep_gate_weight: bfloat16 [256, 3072], P('fsdp'), may hold values from -0.375 to 0.375
- timesteps: int32 [32], replicated, may hold values from 0 to 999
Outputs:
- mixed_update: bfloat16 [131072, 3072], P(('dp', 'fsdp'))
- attention_output_gradient: bfloat16 [131072, 1536], P(('dp', 'fsdp'))
- down_grad: float32 [1536, 128], P('fsdp')
- scaled_up_gradient: float32 [128, 3072], P(None, 'fsdp')
All inputs are finite; a program needn't handle non-finite values.
Results may differ from a plain program's by a relative error of at most 0.0075.
Values may be sent and summed in bfloat16 or wider, within the bound.
No kernel may reach another device: no remote copies, remote signals or barrier semaphores. Data moves between devices by JAX's collectives and lax.ppermute only.
A program may use at most 64 MiB of HBM per device.

v0:
```python
import math

import jax
import jax.numpy as jnp
from jax import lax
from jax.sharding import PartitionSpec as P

FREQ = 256
PATCHES = 4096


adapter_scale_factor = 0.5


def per_device(
    attention_output_rows,
    cotangent,
    quantized_weight_codes,
    shard_absolute_maximum,
    adapter_down_weight,
    adapter_up_weight,
    timestep_gate_weight,
    timesteps,
):
    row_count = attention_output_rows.shape[0]
    dp_count = lax.axis_size("dp")
    fsdp_count = lax.axis_size("fsdp")
    amax_rows = jnp.broadcast_to(shard_absolute_maximum, (quantized_weight_codes.shape[0],))
    all_codes, scales = (
        lax.all_gather(quantized_weight_codes, "fsdp", axis=0, tiled=True),
        lax.all_gather(amax_rows, "fsdp", axis=0, tiled=True),
    )
    weight = (all_codes.astype(jnp.float32) * scales.astype(jnp.float32)[:, None]).astype(
        jnp.bfloat16
    )
    down_all, gathered_up_weight, gate_all = (
        lax.all_gather(adapter_down_weight, "fsdp", axis=0, tiled=True),
        lax.all_gather(adapter_up_weight, "fsdp", axis=1, tiled=True),
        lax.all_gather(timestep_gate_weight, "fsdp", axis=0, tiled=True),
    )
    sample_index = (
        (lax.axis_index("dp") * fsdp_count + lax.axis_index("fsdp")) * row_count // PATCHES
    )
    step_value = lax.dynamic_slice_in_dim(timesteps, sample_index, 1)
    half_freq = FREQ // 2
    frequency = jnp.exp(-math.log(10000.0) * jnp.arange(half_freq, dtype=jnp.float32) / half_freq)
    phase_angle = step_value.astype(jnp.float32)[:, None] * frequency[None, :]
    features = jnp.concatenate([jnp.cos(phase_angle), jnp.sin(phase_angle)], axis=1).astype(
        jnp.bfloat16
    )
    gate_row = jnp.dot(features, gate_all, preferred_element_type=jnp.float32)
    bottleneck_activation = jnp.dot(
        attention_output_rows, down_all, preferred_element_type=jnp.float32
    ).astype(jnp.bfloat16)
    projection_output = jnp.dot(attention_output_rows, weight, preferred_element_type=jnp.float32)
    projection_output = projection_output + adapter_scale_factor * jnp.dot(
        bottleneck_activation, gathered_up_weight, preferred_element_type=jnp.float32
    )
    mixed_update = (projection_output * gate_row).astype(jnp.bfloat16)
    gated_branch_gradient = (cotangent.astype(jnp.float32) * gate_row).astype(jnp.bfloat16)
    bottleneck_gradient = (
        adapter_scale_factor
        * jnp.dot(gated_branch_gradient, gathered_up_weight.T, preferred_element_type=jnp.float32)
    ).astype(jnp.bfloat16)
    attention_output_gradient = jnp.dot(
        gated_branch_gradient, weight.T, preferred_element_type=jnp.float32
    )
    attention_output_gradient = (
        attention_output_gradient
        + jnp.dot(bottleneck_gradient, down_all.T, preferred_element_type=jnp.float32)
    ).astype(jnp.bfloat16)
    term_down = jnp.dot(
        attention_output_rows.T, bottleneck_gradient, preferred_element_type=jnp.float32
    )
    term_up = jnp.dot(
        bottleneck_activation.T, gated_branch_gradient, preferred_element_type=jnp.float32
    )
    gradient_scale_factor = (row_count * dp_count * fsdp_count) ** (-0.5)
    shard_terms = (
        lax.psum_scatter(term_down, "fsdp", scatter_dimension=0, tiled=True),
        lax.psum_scatter(term_up, "fsdp", scatter_dimension=1, tiled=True),
    )
    summed_down, reduced_up_gradient = lax.psum((shard_terms[0], shard_terms[1]), "dp")
    down_grad = summed_down * gradient_scale_factor
    scaled_up_gradient = reduced_up_gradient * (adapter_scale_factor * gradient_scale_factor)
    return (mixed_update, attention_output_gradient, down_grad, scaled_up_gradient)


def solution(mesh):
    in_specs = (
        P(("dp", "fsdp"), None),
        P(("dp", "fsdp"), None),
        P("fsdp", None),
        P("fsdp"),
        P("fsdp", None),
        P(None, "fsdp"),
        P("fsdp", None),
        P(),
    )
    out_specs = (P(("dp", "fsdp"), None), P(("dp", "fsdp"), None), P("fsdp", None), P(None, "fsdp"))
    return jax.shard_map(
        per_device, mesh=mesh, in_specs=in_specs, out_specs=out_specs, check_vma=False
    )
```

profile of v0, /device:TPU:1, one launch (start us, length us, event | category | flops | bytes accessed | tf_op | source)
XLA Modules:
  0.0 815.9 jit_solution(9475165913116458261)
XLA Ops:
  7.2 0.7 all-gather.5.cloned.1.call-update
  8.0 1.2 dynamic_slice.3
  9.9 0.1 sine_convert_fusion
  10.0 1.7 copy.17
  11.7 62.1 %all_gather.18 = bf16[128,3072]{0,1:T(8,128)(2,1)S(1)} all-gather(bf16[128,96]{0,1:T(8,128)(2,1)S(1)} %copy-done.3), channel_id=1, replica_groups=mesh['dp'=16,'fsdp'=32] {'fsdp'}, dimensions={1}, use_global_device_ids=true | all-gather | bytes 811008 | tf_op jit(solution)/shard_map/all_gather | solution.py:38
  73.8 55.0 %all-gather.5.cloned.1.call-done = bf16[256,3072]{1,0:T(8,128)(2,1)} async-done(((bf16[8,3072]{1,0:T(8,128)(2,1)}), bf16[256,3072]{1,0:T(8,128)(2,1)}) %all-gather.5.cloned.1.call-update) | async-done | bytes 1572880 | tf_op jit(solution)/shard_map/all_gather | solution.py:39
  128.8 1.7 fusion.7
  130.5 1.1 fusion.5
  131.6 0.3 convolution_bitcast_fusion.1
  131.9 1.2 copy.21
  133.1 0.0 reduce-scatter.5.cloned.1.call-start
  133.2 48.7 %all_gather.17 = bf16[1536,128]{1,0:T(8,128)(2,1)S(1)} all-gather(bf16[48,128]{1,0:T(8,128)(2,1)S(1)} %copy-done.4), channel_id=1, replica_groups=mesh['dp'=16,'fsdp'=32] {'fsdp'}, dimensions={0}, use_global_device_ids=true | all-gather | bytes 405504 | tf_op jit(solution)/shard_map/all_gather | solution.py:37
  181.8 0.4 convolution_convert_fusion
  182.2 1.8 fusion.6
  184.0 0.0 all-reduce.4.cloned.1.call-start
  184.1 78.8 %reduce-scatter.7.cloned.1.call-done = f32[48,128]{1,0:T(8,128)} async-done(((f32[1536,128]{1,0:T(8,128)}), f32[48,128]{1,0:T(8,128)}) %reduce-scatter.7.cloned.1.call-update) | async-done | bytes 24592
  262.9 1.5 copy.22
  264.4 138.5 %reduce-scatter.5.cloned.1.call-done = f32[128,96]{0,1:T(8,128)} async-done(((f32[128,3072]{0,1:T(8,128)}), f32[128,96]{0,1:T(8,128)}) %reduce-scatter.5.cloned.1.call-update) | async-done | bytes 49168 | tf_op jit(solution)/shard_map/reduce_scatter | solution.py:81
  402.9 0.5 all-gather.3.cloned.1.call-update
  404.1 1.3 dynamic-slice
  406.1 0.2 dynamic-update-slice
  406.3 47.5 %all-reduce = bf16[1536]{0:T(1024)(128)(2,1)S(1)} all-reduce(bf16[1536]{0:T(1024)(128)(2,1)S(1)} %dynamic-update-slice), channel_id=1, replica_groups=mesh['dp'=16,'fsdp'=32] {'fsdp'}, use_global_device_ids=true, to_apply=%add | all-reduce | flops 1536 | bytes 6144
  453.8 122.0 %all-reduce.4.cloned.1.call-done = (f32[48,128]{0,1:T(8,128)}, f32[128,96]{0,1:T(8,128)}) async-done(((f32[48,128]{0,1:T(8,128)}, f32[128,96]{0,1:T(8,128)}), (f32[48,128]{0,1:T(8,128)}, f32[128,96]{0,1:T(8,128)})) %all-reduce.4.cloned.1.call-update) | async-done | bytes 73744 | tf_op jit(solution)/shard_map/psum | solution.py:83
  575.8 0.8 broadcast_multiply_fusion
  576.7 0.7 copy.19
  577.4 1.4 broadcast_multiply_fusion.1
  578.8 215.7 %all-gather.3.cloned.1.call-done = bf16[1536,3072]{1,0:T(8,128)(2,1)} async-done(((bf16[48,3072]{1,0:T(8,128)(2,1)}), bf16[1536,3072]{1,0:T(8,128)(2,1)}) %all-gather.3.cloned.1.call-update) | async-done | bytes 9437200 | tf_op jit(solution)/shard_map/all_gather | solution.py:30
  794.5 7.2 fusion.3
  801.7 1.2 fusion.4
  803.0 4.0 convolution_bitcast_fusion
  807.0 0.6 fusion.2
  807.7 1.7 copy.18
  (23 shorter events, 0.2 us)
Async XLA Ops:
  7.2 124.4 %copy-start = (bf16[256,1536]{1,0:T(8,128)(2,1)S(1)}, bf16[256,1536]{1,0:T(8,128)(2,1)}, u32[]{:S(2)}) copy-start(bf16[256,1536]{1,0:T(8,128)(2,1)} %param.8) | copy-start | bytes 2359300
  7.2 4.5 copy-start.3
  7.2 121.6 %all-gather.5.cloned.1.call-start = ((), (), s32[]{:S(2)}) async-start(), calls=%async_computation.3 | async-start | bytes 1622016 | tf_op jit(solution)/shard_map/all_gather | solution.py:39
  7.9 255.0 %reduce-scatter.7.cloned.1.call-start = ((), (), s32[]{:S(2)}) async-start(), calls=%async_computation.5 | async-start | bytes 811008
  73.8 56.7 %copy-start.1 = (bf16[128,3072]{0,1:T(8,128)(2,1)}, bf16[128,3072]{0,1:T(8,128)(2,1)S(1)}, u32[]{:S(2)}) copy-start(bf16[128,3072]{0,1:T(8,128)(2,1)S(1)} %all_gather.18) | copy-start | bytes 2359300
  130.5 2.7 copy-start.4
  133.1 269.8 %reduce-scatter.5.cloned.1.call-start = ((), (), s32[]{:S(2)}) async-start(), calls=%async_computation.4 | async-start | bytes 1622016 | tf_op jit(solution)/shard_map/reduce_scatter | solution.py:81
  184.0 391.8 %all-reduce.4.cloned.1.call-start = ((), (), s32[]{:S(2)}) async-start(), calls=%async_computation.6 | async-start | bytes 229376 | tf_op jit(solution)/shard_map/psum | solution.py:83
  402.9 391.6 %all-gather.3.cloned.1.call-start = ((), (), s32[]{:S(2)}) async-start(), calls=%async_computation.2 | async-start | bytes 9732096 | tf_op jit(solution)/shard_map/all_gather | solution.py:30
  794.5 8.5 %copy-start.5 = (bf16[1536,3072]{1,0:T(8,128)(2,1)S(1)}, bf16[1536,3072]{1,0:T(8,128)(2,1)}, u32[]{:S(2)}) copy-start(bf16[1536,3072]{1,0:T(8,128)(2,1)} %all-gather.3.cloned.1.call-done) | copy-start | bytes 28311556
  803.0 4.0 copy-start.2
Sparse Core Ops, SparseCore 0:
  10.1 118.6 all-gather.4
  133.2 129.6 reduce-scatter.6
  266.5 136.2 reduce-scatter.4
  406.3 169.5 all-reduce.3
  578.0 216.5 all-gather.2
where the time goes:
time: 817 us; the launch traced here: 816 us
  waiting for transfers between devices  611 us (75%)
  blocking collectives  158 us (19%)
  matrix products  18.4 us (2%)
  between operations  15.9 us (2%)
  local copies, waits for them, and re-layouts  9.55 us (1%)
    all_gather x1, waiting for transfers between devices, per_device(): lax.all_gather(quantized_weight_codes, 'fsdp', axis=0, tiled=True)  216 us
    reduce_scatter x1, waiting for transfers between devices, per_device(): lax.psum_scatter(term_up, 'fsdp', scatter_dimension=1, tiled=True)  138 us
    psum x1, waiting for transfers between devices, per_device(): lax.psum((shard_terms[0], shard_terms[1]), 'dp')  122 us
    unnamed x6, waiting for transfers between devices  80.1 us
    all_gather x1, blocking collectives, per_device(): lax.all_gather(adapter_up_weight, 'fsdp', axis=1, tiled=True)  62.1 us
    all_gather x1, waiting for transfers between devices, per_device(): lax.all_gather(timestep_gate_weight, 'fsdp', axis=0, tiled=True)  55 us
    all_gather x1, blocking collectives, per_device(): lax.all_gather(adapter_down_weight, 'fsdp', axis=0, tiled=True)  48.7 us
    unnamed x1, blocking collectives  47.5 us
  transfers between devices with their start and end apart: 5, of which 5 were waited for; matrix products, arithmetic and copies ran while one was open for 1% of the time, Pallas kernels for 0%

commit v1 on v0

v1 whole, which is shorter than its diff:
```python
import math

import jax
import jax.numpy as jnp
from jax import lax
from jax.experimental import pallas as pl
from jax.experimental.pallas import tpu as pltpu
from jax.sharding import Mesh
from jax.sharding import PartitionSpec as P

FREQ = 256
SCALE = 0.5
AXES = ("yh", "x", "core", "z", "yl")
SIZES = (2, 4, 2, 16, 2)
PLANE = ("yh", "x", "yl")
BF = jnp.bfloat16
F32 = jnp.float32


def index_of(yh, x, c, z, yl):
    return (((yh * 4 + x) * 2 + c) * 16 + z) * 2 + yl


def plane_pairs(k, swap):
    pairs = []
    for yh in range(2):
        for x in range(4):
            for c in range(2):
                for z in range(16):
                    for yl in range(2):
                        tx, ty = x, yh * 2 + yl
                        if (c == 0) != swap:
                            tx ^= k
                        else:
                            ty ^= k
                        pairs.append((index_of(yh, x, c, z, yl), index_of(ty >> 1, tx, c, z, ty & 1)))
    return pairs


def other_core(v):
    return lax.ppermute(v, "core", [(0, 1), (1, 0)])


def assemble_kernel(at_ref, t0, t1, t2, t3, out_ref, sems):
    copies = []
    for k2, t in enumerate((t0, t1, t2, t3)):
        for k1 in range(4):
            b = k2 * 4 + k1
            col = pl.multiple_of(at_ref[b] * 384, 128)
            copy = pltpu.make_async_copy(
                t.at[k1], out_ref.at[:, at_ref[16 + b], :, pl.ds(col, 384)], sems.at[b]
            )
            copy.start()
            copies.append(copy)
    for copy in copies:
        copy.wait()


def assemble(at, blocks):
    hbm = pl.BlockSpec(memory_space=pl.ANY)
    return pl.pallas_call(
        assemble_kernel,
        out_shape=jax.ShapeDtypeStruct((16, 4, 24, 1536), BF),
        in_specs=[pl.BlockSpec(memory_space=pltpu.SMEM)] + [hbm] * 4,
        out_specs=hbm,
        scratch_shapes=[pltpu.SemaphoreType.DMA((16,))],
        name="assemble_weight",
    )(at, *blocks)


def per_device(rows, cotangent, codes, amax, down, up, gate_weight, timesteps):
    yh, xi, core, z, yl = (lax.axis_index(a) for a in AXES)
    j = yh * 4 + xi
    y = yh * 2 + yl

    upT = up.T
    down_piece = lax.dynamic_slice(down, (6 * j, 0), (6, 128))
    up_piece = lax.dynamic_slice(upT, (12 * j, 0), (12, 128))
    gate_piece = lax.dynamic_slice(gate_weight, (0, core * 1536 + j * 192), (8, 192)).reshape(12, 128)
    small = jnp.concatenate([down_piece, up_piece, gate_piece], axis=0)
    small = lax.all_to_all(jnp.broadcast_to(small[None], (16, 30, 128)), "z", 0, 0, tiled=True)

    weight = (codes.astype(F32) * amax.astype(F32)[0]).astype(BF)
    piece = lax.dynamic_slice(weight, (24 * yh, core * 1536 + xi * 384), (24, 384))
    line = lax.all_to_all(jnp.broadcast_to(piece[None], (16, 24, 384)), "z", 0, 0, tiled=True)
    first = jnp.stack([line] + [lax.ppermute(line, AXES, plane_pairs(k, False)) for k in (1, 2, 3)])
    second = [first] + [lax.ppermute(first, AXES, plane_pairs(k, True)) for k in (2, 1, 3)]
    second = [second[0], second[2], second[1], second[3]]
    k1 = jnp.tile(jnp.arange(4), 4)
    k2 = jnp.repeat(jnp.arange(4), 4)
    bx = xi ^ jnp.where(core == 0, k1, k2)
    by = y ^ jnp.where(core == 0, k2, k1)
    at = jnp.concatenate([bx, (by & 1) * 2 + (by >> 1)]).astype(jnp.int32)

    rows_other = other_core(rows)

    half_freq = FREQ // 2
    frequency = jnp.exp(-math.log(10000.0) * jnp.arange(half_freq, dtype=F32) / half_freq)
    steps = lax.dynamic_slice(timesteps.reshape(16, 2), (0, z // 8), (16, 1))
    phase = steps.astype(F32) * frequency[None, :]
    features = jnp.concatenate([jnp.cos(phase), jnp.sin(phase)], axis=1).astype(BF)
    features = lax.dynamic_slice(features.reshape(16, 16, 2, 8), (0, 0, yl, 0), (16, 16, 1, 8))
    gate_block = small[:, 18:].reshape(16, 8, 192).reshape(128, 192)
    part = jnp.dot(features.reshape(16, 128), gate_block, preferred_element_type=F32)
    high = lax.reduce_precision(part, 8, 7)
    pair = jnp.stack([high.astype(BF), (part - high).astype(BF)])
    pair = pair.reshape(2, 8, 2, 192).transpose(1, 0, 2, 3).reshape(8, 1, 6, 128)
    pair = jnp.broadcast_to(pair, (8, 2, 6, 128)).reshape(16, 6, 128)
    maps = jnp.broadcast_to(small[:, :18].reshape(1, 288, 128), (16, 288, 128))
    got = lax.all_to_all(jnp.concatenate([maps, pair], axis=1), PLANE, 0, 0, tiled=True)
    maps = got[:, :288].reshape(8, 2, 16, 18, 128).transpose(2, 1, 0, 3, 4)
    down_all = maps[:, :, :, :6].reshape(1536, 128)
    upT_all = maps[:, :, :, 6:].reshape(3072, 128)
    gates = got[:, 288:].reshape(8, 2, 2, 2, 192).astype(F32).sum((1, 2))
    gates = gates.transpose(1, 0, 2).reshape(2, 1536)
    gate_own = lax.dynamic_slice(gates, (core, 0), (1, 1536))
    gate_other = lax.dynamic_slice(gates, (1 - core, 0), (1, 1536))
    gate_rest = other_core(gate_other)
    gate_row = jnp.where(
        core == 0,
        jnp.concatenate([gate_own, gate_rest], axis=1),
        jnp.concatenate([gate_rest, gate_own], axis=1),
    )

    branch = (cotangent.astype(F32) * gate_row).astype(BF)
    branch_own = lax.dynamic_slice(branch, (0, core * 1536), (256, 1536))
    branch_other = other_core(lax.dynamic_slice(branch, (0, (1 - core) * 1536), (256, 1536)))
    low = jnp.dot(rows, down_all, preferred_element_type=F32).astype(BF)
    low_grad = (SCALE * jnp.dot(branch, upT_all, preferred_element_type=F32)).astype(BF)
    term_down = jnp.dot(rows.T, low_grad, preferred_element_type=F32).reshape(32, 2, 24, 128)
    term_up = jnp.dot(branch.T, low, preferred_element_type=F32).reshape(32, 2, 48, 128)
    terms = jnp.concatenate([term_down, term_up], axis=2)
    mine = lax.dynamic_slice(terms, (0, core, 0, 0), (32, 1, 72, 128))
    yours = lax.dynamic_slice(terms, (0, 1 - core, 0, 0), (32, 1, 72, 128))
    terms = (mine + other_core(yours)).astype(BF).reshape(16, 2, 8, 9, 128)
    terms = terms.transpose(2, 1, 0, 3, 4).reshape(16, 144, 128)
    terms = lax.all_to_all(terms, PLANE, 0, 0, tiled=True).astype(F32).sum(0).reshape(16, 9, 128)
    terms = lax.all_to_all(terms, "z", 0, 0, tiled=True).sum(0)
    terms = jnp.broadcast_to(terms[None], (16, 9, 128))
    terms = lax.all_to_all(terms, ("yh", "x", "core"), 0, 0, tiled=True)
    terms = terms.reshape(8, 2, 9, 128).transpose(1, 0, 2, 3).reshape(2, 72, 128)
    grad_scale = 131072**-0.5
    down_grad = terms[:, :24].reshape(48, 128) * grad_scale
    up_grad = terms[:, 24:].reshape(96, 128).T * (SCALE * grad_scale)

    low_other = jnp.dot(rows_other, down_all, preferred_element_type=F32).astype(BF)
    upT_half = lax.dynamic_slice(upT_all, (core * 1536, 0), (1536, 128))
    wm = assemble(at, second).reshape(1536, 1536)

    def back(b):
        return lax.dot_general(b, wm, (((1,), (1,)), ((), ())), preferred_element_type=F32)

    def forward(r, lo, g):
        p = jnp.dot(r, wm, preferred_element_type=F32)
        p = p + SCALE * lax.dot_general(lo, upT_half, (((1,), (1,)), ((), ())), preferred_element_type=F32)
        return (p * g).astype(BF)

    dx_rest = other_core(back(branch_other).astype(BF))
    mixed_rest = other_core(forward(rows_other, low_other, gate_other))
    mixed_own = forward(rows, low, gate_own)
    dx = back(branch_own) + lax.dot_general(
        low_grad, down_all, (((1,), (1,)), ((), ())), preferred_element_type=F32
    )
    dx = (dx + dx_rest.astype(F32)).astype(BF)
    mixed = jnp.where(
        core == 0,
        jnp.concatenate([mixed_own, mixed_rest], axis=1),
        jnp.concatenate([mixed_rest, mixed_own], axis=1),
    )
    return mixed, dx, down_grad, up_grad


def solution(mesh):
    fine = Mesh(mesh.devices.reshape(SIZES), AXES)
    dp, fsdp = ("yh", "x", "core"), ("z", "yl")
    every = dp + fsdp
    in_specs = (
        P(every, None),
        P(every, None),
        P(fsdp, None),
        P(fsdp),
        P(fsdp, None),
        P(None, fsdp),
        P(fsdp, None),
        P(),
    )
    out_specs = (P(every, None), P(every, None), P(fsdp, None), P(None, fsdp))
    return jax.shard_map(
        per_device, mesh=fine, in_specs=in_specs, out_specs=out_specs, check_vma=False
    )
```

time: 817 us -> 342 us (0.42)
  waiting for transfers between devices: 611 us -> 35.8 us
  blocking collectives: 158 us -> 0 us
  Pallas kernels: 0 us -> 145 us
  starting transfers between devices: 0.2 us -> 94.6 us
  matrix products: 18.4 us -> 32.7 us
  between operations: 15.9 us -> 1.9 us
  local copies, waits for them, and re-layouts: 9.55 us -> 20.2 us
  other arithmetic: 2.33 us -> 10.7 us
    all_gather x2 -> x0, waiting for transfers between devices: 271 us -> none  [the longest x1 216 us: per_device(): lax.all_gather(quantized_weight_codes, 'fsdp', axis=0, tiled=True)]
    pallas_call x0 -> x1, Pallas kernels: none -> 145 us  [assemble(): pl.pallas_call(assemble_kernel, out_shape=jax.ShapeDtypeStruct((16, 4, 24...]
    reduce_scatter x1 -> x0, waiting for transfers between devices: 138 us -> none  [per_device(): lax.psum_scatter(term_up, 'fsdp', scatter_dimension=1, tiled=True)]
    psum x1 -> x0, waiting for transfers between devices: 122 us -> none  [per_device(): lax.psum((shard_terms[0], shard_terms[1]), 'dp')]
    all_gather x2 -> x0, blocking collectives: 111 us -> none  [the longest x1 62.1 us: per_device(): lax.all_gather(adapter_up_weight, 'fsdp', axis=1, tiled=True)]
    unnamed x6 -> x0, waiting for transfers between devices: 80.1 us -> none
    all_to_all x0 -> x6, starting transfers between devices: none -> 52.6 us  [the longest x1 15.7 us: per_device(): lax.all_to_all(jnp.broadcast_to(small[None], (16, 30, 128)), 'z', 0, 0, t...]
    unnamed x1 -> x0, blocking collectives: 47.5 us -> none
  transfers between devices with their start and end apart: 5 -> 18, of which waited for: 5 -> 6; matrix products, arithmetic and copies ran while one was open for 1% -> 17% of each run, Pallas kernels for 0% -> 43%
where the time goes in v1:
time: 342 us; the launch traced here: 341 us
  Pallas kernels  145 us (42%)
  starting transfers between devices  94.6 us (28%)
  waiting for transfers between devices  35.8 us (10%)
  matrix products  32.7 us (10%)
  local copies, waits for them, and re-layouts  20.2 us (6%)
  other arithmetic  10.7 us (3%)
    pallas_call x1, Pallas kernels, assemble(): pl.pallas_call(assemble_kernel, out_shape=jax.ShapeDtypeStruct((16, 4, 24...  145 us
    ppermute x6, starting transfers between devices, other_core(): return lax.ppermute(v, 'core', [(0, 1), (1, 0)])  24.1 us
    all_to_all x1, starting transfers between devices, per_device(): lax.all_to_all(jnp.broadcast_to(small[None], (16, 30, 128)), 'z', 0, 0, t...  15.7 us
    dot_general x2, matrix products, forward(): p = jnp.dot(r, wm, preferred_element_type=F32)  10.6 us
    all_to_all x1, waiting for transfers between devices, per_device(): lax.all_to_all(jnp.broadcast_to(small[None], (16, 30, 128)), 'z', 0, 0, t...  10.6 us
    dot_general x2, matrix products, back(): lax.dot_general(b, wm, (((1,), (1,)), ((), ())), preferred_element_type=F32)  10.3 us
    all_to_all x1, waiting for transfers between devices, per_device(): lax.all_to_all(jnp.broadcast_to(piece[None], (16, 24, 384)), 'z', 0, 0, t...  10.2 us
    all_to_all x1, starting transfers between devices, per_device(): terms = lax.all_to_all(terms, 'z', 0, 0, tiled=True).sum(0)  10.1 us
  transfers between devices with their start and end apart: 18, of which 6 were waited for; matrix products, arithmetic and copies ran while one was open for 17% of the time, Pallas kernels for 43%

profile of v1, /device:TPU:1, one launch (start us, length us, event | category | flops | bytes accessed | tf_op | source)
XLA Modules:
  0.0 340.8 jit_solution(5827337391787362941)
XLA Ops:
  3.7 15.7 %all-to-all-start.1 = ((bf16[16,30,128]{2,1,0:T(8,128)(2,1)}), bf16[16,30,128]{2,1,0:T(8,128)(2,1)S(1)}, u32[]{:S(2)}, u32[]{:S(2)}) async-start(bf16[16,30,128]{2,1,0:T(8,128)(2,1)} %broadcast_in_dim.41), calls=%async_computation.1 | async-start | bytes 262144 | tf_op jit(solution)/shard_map/all_to_all | solution.py:81
  20.8 10.6 %all-to-all-done.1 = bf16[16,30,128]{2,1,0:T(8,128)(2,1)S(1)} async-done(((bf16[16,30,128]{2,1,0:T(8,128)(2,1)}), bf16[16,30,128]{2,1,0:T(8,128)(2,1)S(1)}, u32[]{:S(2)}, u32[]{:S(2)}) %all-to-all-start.1) | async-done | bytes 122912 | tf_op jit(solution)/shard_map/all_to_all | solution.py:81
  32.2 5.9 %all-to-all-start = ((bf16[16,24,384]{2,1,0:T(8,128)(2,1)}), bf16[16,24,384]{2,1,0:T(8,128)(2,1)S(1)}, u32[]{:S(2)}, u32[]{:S(2)}) async-start(bf16[16,24,384]{2,1,0:T(8,128)(2,1)} %broadcast_in_dim.40), calls=%async_computation | async-start | bytes 589824 | tf_op jit(solution)/shard_map/all_to_all | solution.py:85
  41.2 10.2 %all-to-all-done = bf16[16,24,384]{2,1,0:T(8,128)(2,1)S(1)} async-done(((bf16[16,24,384]{2,1,0:T(8,128)(2,1)}), bf16[16,24,384]{2,1,0:T(8,128)(2,1)S(1)}, u32[]{:S(2)}, u32[]{:S(2)}) %all-to-all-start) | async-done | bytes 294944 | tf_op jit(solution)/shard_map/all_to_all | solution.py:85
  51.4 6.8 %all-to-all-start.2 = ((bf16[16,294,128]{2,1,0:T(8,128)(2,1)}), bf16[16,294,128]{2,1,0:T(8,128)(2,1)S(1)}, u32[]{:S(2)}, u32[]{:S(2)}) async-start(bf16[16,294,128]{2,1,0:T(8,128)(2,1)} %pad_maximum_fusion), calls=%async_computation.2 | async-start | bytes 2424832 | tf_op jit(solution)/shard_map/all_to_all | solution.py:110
  58.2 4.5 %collective-permute-start.2 = (bf16[16,24,384]{2,1,0:T(8,128)(2,1)S(1)}, bf16[16,24,384]{2,1,0:T(8,128)(2,1)S(1)}, u32[]{:S(2)}, u32[]{:S(2)}) collective-permute-start(bf16[16,24,384]{2,1,0:T(8,128)(2,1)S(1)} %all-to-all-done), channel_id=1, source_target_pairs={{0,192},{1,193},{2,194},{3,195},{4,196},{5,197},{6,198},{7,199},{8... | collective-permute-start | bytes 884744 | tf_op jit(solution)/shard_map/ppermute | solution.py:86
  62.7 2.5 collective-permute-start.1
  65.2 2.0 collective-permute-start
  67.2 10.9 %collective-permute-start.6 = (bf16[256,1536]{1,0:T(8,128)(2,1)}, bf16[256,1536]{1,0:T(8,128)(2,1)}, u32[]{:S(2)}, u32[]{:S(2)}) collective-permute-start(bf16[256,1536]{1,0:T(8,128)(2,1)} %param.8), channel_id=1, source_target_pairs={{0,32},{32,0},{1,33},{33,1},{2,34},{34,2},{3,35},{35,3},{4,36},{36... | collective-permute-start | bytes 2359304 | tf_op jit(solution)/shard_map/ppermute | solution.py:41
  78.9 2.8 collective-permute-done.2
  83.9 2.8 collective-permute-start.5
  86.7 2.9 collective-permute-start.4
  89.6 3.3 collective-permute-start.3
  93.8 4.1 %collective-permute-start.8 = (f32[1,1536]{1,0:T(1,128)S(1)}, f32[1,1536]{1,0:T(1,128)S(1)}, u32[]{:S(2)}, u32[]{:S(2)}) collective-permute-start(f32[1,1536]{1,0:T(1,128)S(1)} %get-tuple-element.25), channel_id=1, source_target_pairs={{0,32},{32,0},{1,33},{33,1},{2,34},{34,2},{3,35},{35,3},{4,36},{36... | collective-permute-start | bytes 18440 | tf_op jit(solution)/shard_map/ppermute | solution.py:41
  104.6 2.3 convolution_bitcast_fusion.2
  106.9 2.3 copy.72
  109.2 1.9 collective-permute-start.9
  116.6 2.4 collective-permute-start.11
  120.6 3.4 convolution_multiply_fusion
  125.6 144.9 %assemble_weight.1 = bf16[16,4,24,1536]{3,2,1,0:T(8,128)(2,1)} custom-call(s32[32]{0:T(128)} %pad_add_fusion.at_ref, bf16[4,16,24,384]{3,2,1,0:T(8,128)(2,1)} %pad_maximum_fusion.1.t0, bf16[4,16,24,384]{3,2,1,0:T(8,128)(2,1)} %collective-permute-done.3.t1, bf16[4,16,24,384]{3,2,1,0:T(8,128)(2,1)} %collective-permute-done.4.t2, ...), custom_call_target="tpu_custom_call" | custom-call | tf_op jit(solution)/shard_map/assemble_weight/pallas_call | solution.py:61
  270.4 5.0 %convolution_convert_fusion = bf16[256,1536]{1,0:T(8,128)(2,1)} fusion(bf16[256,1536]{1,0:T(8,128)(2,1)} %collective-permute-done.9, bf16[1536,1536]{1,0:T(8,128)(2,1)} %bitcast.80), kind=kOutput, calls=%fused_computation.14 | convolution fusion | flops 1208352768 | bytes 6291456 | tf_op jit(solution)/shard_map/dot_general | solution.py:151
  275.5 2.1 collective-permute-start.10
  280.5 5.0 %all-to-all-start.3 = ((bf16[16,144,128]{2,1,0:T(8,128)(2,1)}), bf16[16,144,128]{2,1,0:T(8,128)(2,1)S(1)}, u32[]{:S(2)}, u32[]{:S(2)}) async-start(bf16[16,144,128]{2,1,0:T(8,128)(2,1)} %copy.76), calls=%async_computation.3 | async-start | bytes 1179648 | tf_op jit(solution)/shard_map/all_to_all | solution.py:137
  285.6 5.6 %fusion.6 = bf16[256,1536]{0,1:T(8,128)(2,1)} fusion(f32[256,1536]{0,1:T(8,128)} %convolution_multiply_fusion, bf16[1536,1536]{1,0:T(8,128)(2,1)} %bitcast.81, bf16[256,1536]{1,0:T(8,128)(2,1)} %collective-permute-done.6, f32[1536]{0:T(1024)S(1)} %get-tuple-element.24), kind=kOutput, calls=%fused_computation.12 | convolution fusion | flops 1209139200 | bytes 7870464 | tf_op jit(solution)/shard_map/dot_general | solution.py:154
  291.1 2.7 collective-permute-start.7
  293.8 5.0 %fusion.7 = bf16[256,1536]{0,1:T(8,128)(2,1)} fusion(f32[256,1536]{0,1:T(8,128)S(1)} %copy-done.5, bf16[1536,1536]{1,0:T(8,128)(2,1)} %bitcast.82, bf16[256,1536]{1,0:T(8,128)(2,1)} %param.8, f32[1536]{0:T(1024)S(1)} %get-tuple-element.28), kind=kOutput, calls=%fused_computation.13 | convolution fusion | flops 1209139200 | bytes 7870464 | tf_op jit(solution)/shard_map/dot_general | solution.py:154
  299.6 10.1 %all-to-all-start.4 = ((f32[16,9,128]{2,1,0:T(8,128)}), f32[16,9,128]{2,1,0:T(8,128)S(1)}, u32[]{:S(2)}, u32[]{:S(2)}) async-start(f32[16,9,128]{2,1,0:T(8,128)} %reshape.166), calls=%async_computation.4 | async-start | bytes 262144 | tf_op jit(solution)/shard_map/all_to_all | solution.py:138
  309.8 5.3 %fusion.5 = bf16[256,1536]{1,0:T(8,128)(2,1)} fusion(f32[256,1536]{1,0:T(8,128)} %fusion.25, bf16[1536,1536]{1,0:T(8,128)(2,1)} %bitcast.83, bf16[256,1536]{1,0:T(8,128)(2,1)} %collective-permute-done.10, bf16[256,3072]{1,0:T(8,128)(2,1)S(1)} %multiply_convert_fusion, s32[]{:T(128)S(6)} %select_n.88), kind=kOutput, calls=%fused_computation.11 | convolution fusion | flops 1209532416 | bytes 8650756 | tf_op jit(solution)/shard_map/dot_general | solution.py:151
  315.1 7.2 %all-to-all-done.4 = f32[16,9,128]{2,1,0:T(8,128)S(1)} async-done(((f32[16,9,128]{2,1,0:T(8,128)}), f32[16,9,128]{2,1,0:T(8,128)S(1)}, u32[]{:S(2)}, u32[]{:S(2)}) %all-to-all-start.4) | async-done | bytes 73760 | tf_op jit(solution)/shard_map/all_to_all | solution.py:138
  322.9 9.0 %all-to-all-start.5 = ((f32[16,9,128]{2,1,0:T(8,128)}), f32[16,9,128]{2,1,0:T(8,128)S(1)}, u32[]{:S(2)}, u32[]{:S(2)}) async-start(f32[16,9,128]{2,1,0:T(8,128)} %broadcast_in_dim.46), calls=%async_computation.5 | async-start | bytes 262144 | tf_op jit(solution)/shard_map/all_to_all | solution.py:140
  331.9 1.8 maximum_select_fusion
  335.4 4.0 %all-to-all-done.5 = f32[16,9,128]{2,1,0:T(8,128)S(1)} async-done(((f32[16,9,128]{2,1,0:T(8,128)}), f32[16,9,128]{2,1,0:T(8,128)S(1)}, u32[]{:S(2)}, u32[]{:S(2)}) %all-to-all-start.5) | async-done | bytes 73760 | tf_op jit(solution)/shard_map/all_to_all | solution.py:140
  (94 shorter events, 34.0 us)
Async XLA Ops:
  0.6 0.8 copy-start
  3.7 27.8 %all-to-all-start.1 = ((bf16[16,30,128]{2,1,0:T(8,128)(2,1)}), bf16[16,30,128]{2,1,0:T(8,128)(2,1)S(1)}, u32[]{:S(2)}, u32[]{:S(2)}) async-start(bf16[16,30,128]{2,1,0:T(8,128)(2,1)} %broadcast_in_dim.41), calls=%async_computation.1 | async-start | bytes 262144 | tf_op jit(solution)/shard_map/all_to_all | solution.py:81
  32.2 19.2 %all-to-all-start = ((bf16[16,24,384]{2,1,0:T(8,128)(2,1)}), bf16[16,24,384]{2,1,0:T(8,128)(2,1)S(1)}, u32[]{:S(2)}, u32[]{:S(2)}) async-start(bf16[16,24,384]{2,1,0:T(8,128)(2,1)} %broadcast_in_dim.40), calls=%async_computation | async-start | bytes 589824 | tf_op jit(solution)/shard_map/all_to_all | solution.py:85
  51.4 41.5 %all-to-all-start.2 = ((bf16[16,294,128]{2,1,0:T(8,128)(2,1)}), bf16[16,294,128]{2,1,0:T(8,128)(2,1)S(1)}, u32[]{:S(2)}, u32[]{:S(2)}) async-start(bf16[16,294,128]{2,1,0:T(8,128)(2,1)} %pad_maximum_fusion), calls=%async_computation.2 | async-start | bytes 2424832 | tf_op jit(solution)/shard_map/all_to_all | solution.py:110
  58.2 23.5 %collective-permute-start.2 = (bf16[16,24,384]{2,1,0:T(8,128)(2,1)S(1)}, bf16[16,24,384]{2,1,0:T(8,128)(2,1)S(1)}, u32[]{:S(2)}, u32[]{:S(2)}) collective-permute-start(bf16[16,24,384]{2,1,0:T(8,128)(2,1)S(1)} %all-to-all-done), channel_id=1, source_target_pairs={{0,192},{1,193},{2,194},{3,195},{4,196},{5,197},{6,198},{7,199},{8... | collective-permute-start | bytes 884744 | tf_op jit(solution)/shard_map/ppermute | solution.py:86
  62.7 19.0 %collective-permute-start.1 = (bf16[16,24,384]{2,1,0:T(8,128)(2,1)S(1)}, bf16[16,24,384]{2,1,0:T(8,128)(2,1)S(1)}, u32[]{:S(2)}, u32[]{:S(2)}) collective-permute-start(bf16[16,24,384]{2,1,0:T(8,128)(2,1)S(1)} %all-to-all-done), channel_id=1, source_target_pairs={{0,128},{1,129},{2,130},{3,131},{4,132},{5,133},{6,134},{7,135},{8... | collective-permute-start | bytes 884744 | tf_op jit(solution)/shard_map/ppermute | solution.py:86
  65.2 17.6 %collective-permute-start = (bf16[16,24,384]{2,1,0:T(8,128)(2,1)S(1)}, bf16[16,24,384]{2,1,0:T(8,128)(2,1)S(1)}, u32[]{:S(2)}, u32[]{:S(2)}) collective-permute-start(bf16[16,24,384]{2,1,0:T(8,128)(2,1)S(1)} %all-to-all-done), channel_id=1, source_target_pairs={{0,64},{1,65},{2,66},{3,67},{4,68},{5,69},{6,70},{7,71},{8,72},{9,... | collective-permute-start | bytes 884744 | tf_op jit(solution)/shard_map/ppermute | solution.py:86
  67.2 49.5 %collective-permute-start.6 = (bf16[256,1536]{1,0:T(8,128)(2,1)}, bf16[256,1536]{1,0:T(8,128)(2,1)}, u32[]{:S(2)}, u32[]{:S(2)}) collective-permute-start(bf16[256,1536]{1,0:T(8,128)(2,1)} %param.8), channel_id=1, source_target_pairs={{0,32},{32,0},{1,33},{33,1},{2,34},{34,2},{3,35},{35,3},{4,36},{36... | collective-permute-start | bytes 2359304 | tf_op jit(solution)/shard_map/ppermute | solution.py:41
  83.9 41.6 %collective-permute-start.5 = (bf16[4,16,24,384]{3,2,1,0:T(8,128)(2,1)}, bf16[4,16,24,384]{3,2,1,0:T(8,128)(2,1)}, u32[]{:S(2)}, u32[]{:S(2)}) collective-permute-start(bf16[4,16,24,384]{3,2,1,0:T(8,128)(2,1)} %pad_maximum_fusion.1.t0), channel_id=1, source_target_pairs={{0,257},{1,256},{2,259},{3,258},{4,261},{5,260},{6,263},{7,262},{8... | collective-permute-start | bytes 3538952 | tf_op jit(solution)/shard_map/ppermute | solution.py:87
  86.7 38.8 %collective-permute-start.4 = (bf16[4,16,24,384]{3,2,1,0:T(8,128)(2,1)}, bf16[4,16,24,384]{3,2,1,0:T(8,128)(2,1)}, u32[]{:S(2)}, u32[]{:S(2)}) collective-permute-start(bf16[4,16,24,384]{3,2,1,0:T(8,128)(2,1)} %pad_maximum_fusion.1.t0), channel_id=1, source_target_pairs={{0,256},{1,257},{2,258},{3,259},{4,260},{5,261},{6,262},{7,263},{8... | collective-permute-start | bytes 3538952 | tf_op jit(solution)/shard_map/ppermute | solution.py:87
  89.6 35.9 %collective-permute-start.3 = (bf16[4,16,24,384]{3,2,1,0:T(8,128)(2,1)}, bf16[4,16,24,384]{3,2,1,0:T(8,128)(2,1)}, u32[]{:S(2)}, u32[]{:S(2)}) collective-permute-start(bf16[4,16,24,384]{3,2,1,0:T(8,128)(2,1)} %pad_maximum_fusion.1.t0), channel_id=1, source_target_pairs={{0,1},{1,0},{2,3},{3,2},{4,5},{5,4},{6,7},{7,6},{8,9},{9,8},{10,11... | collective-permute-start | bytes 3538952 | tf_op jit(solution)/shard_map/ppermute | solution.py:87
  93.5 4.7 %copy-start.1 = (bf16[16,288,128]{2,0,1:T(8,128)(2,1)}, bf16[16,288,128]{2,0,1:T(8,128)(2,1)S(1)}, u32[]{:S(2)}) copy-start(bf16[16,288,128]{2,0,1:T(8,128)(2,1)S(1)} %copy.84) | copy-start | bytes 3538948
  93.8 7.5 %collective-permute-start.8 = (f32[1,1536]{1,0:T(1,128)S(1)}, f32[1,1536]{1,0:T(1,128)S(1)}, u32[]{:S(2)}, u32[]{:S(2)}) collective-permute-start(f32[1,1536]{1,0:T(1,128)S(1)} %get-tuple-element.25), channel_id=1, source_target_pairs={{0,32},{32,0},{1,33},{33,1},{2,34},{34,2},{3,35},{35,3},{4,36},{36... | collective-permute-start | bytes 18440 | tf_op jit(solution)/shard_map/ppermute | solution.py:41
  98.3 1.8 copy-start.2
  109.2 161.2 %collective-permute-start.9 = (bf16[256,1536]{1,0:T(8,128)(2,1)}, bf16[256,1536]{1,0:T(8,128)(2,1)}, u32[]{:S(2)}, u32[]{:S(2)}) collective-permute-start(bf16[256,1536]{1,0:T(8,128)(2,1)} %constant_dynamic-slice_fusion.1), channel_id=1, source_target_pairs={{0,32},{32,0},{1,33},{33,1},{2,34},{34,2},{3,35},{35,3},{4,36},{36... | collective-permute-start | bytes 2359304 | tf_op jit(solution)/shard_map/ppermute | solution.py:41
  114.1 1.4 copy-start.3
  116.6 160.9 %collective-permute-start.11 = (f32[32,1,72,128]{3,0,2,1:T(8,128)}, f32[32,1,72,128]{3,0,2,1:T(8,128)}, u32[]{:S(2)}, u32[]{:S(2)}) collective-permute-start(f32[32,1,72,128]{3,0,2,1:T(8,128)} %constant_dynamic-slice_fusion), channel_id=1, source_target_pairs={{0,32},{32,0},{1,33},{33,1},{2,34},{34,2},{3,35},{35,3},{4,36},{36... | collective-permute-start | bytes 3538952 | tf_op jit(solution)/shard_map/ppermute | solution.py:41
  270.4 7.1 %copy-start.4 = (f32[32,2,72,128]{3,0,2,1:T(8,128)S(1)}, f32[32,2,72,128]{3,0,2,1:T(8,128)}, u32[]{:S(2)}) copy-start(f32[32,2,72,128]{3,0,2,1:T(8,128)} %copy-done.3) | copy-start | bytes 7077892
  275.5 34.3 %collective-permute-start.10 = (bf16[256,1536]{1,0:T(8,128)(2,1)}, bf16[256,1536]{1,0:T(8,128)(2,1)}, u32[]{:S(2)}, u32[]{:S(2)}) collective-permute-start(bf16[256,1536]{1,0:T(8,128)(2,1)} %convolution_convert_fusion), channel_id=1, source_target_pairs={{0,32},{32,0},{1,33},{33,1},{2,34},{34,2},{3,35},{35,3},{4,36},{36... | collective-permute-start | bytes 2359304 | tf_op jit(solution)/shard_map/ppermute | solution.py:41
  280.5 18.3 %all-to-all-start.3 = ((bf16[16,144,128]{2,1,0:T(8,128)(2,1)}), bf16[16,144,128]{2,1,0:T(8,128)(2,1)S(1)}, u32[]{:S(2)}, u32[]{:S(2)}) async-start(bf16[16,144,128]{2,1,0:T(8,128)(2,1)} %copy.76), calls=%async_computation.3 | async-start | bytes 1179648 | tf_op jit(solution)/shard_map/all_to_all | solution.py:137
  285.6 8.3 %copy-start.5 = (f32[256,1536]{0,1:T(8,128)S(1)}, f32[256,1536]{0,1:T(8,128)}, u32[]{:S(2)}) copy-start(f32[256,1536]{0,1:T(8,128)} %convolution_multiply_fusion.1) | copy-start | bytes 4718596
  291.1 40.8 %collective-permute-start.7 = (bf16[256,1536]{0,1:T(8,128)(2,1)}, bf16[256,1536]{0,1:T(8,128)(2,1)S(1)}, u32[]{:S(2)}, u32[]{:S(2)}) collective-permute-start(bf16[256,1536]{0,1:T(8,128)(2,1)} %fusion.6), channel_id=1, source_target_pairs={{0,32},{32,0},{1,33},{33,1},{2,34},{34,2},{3,35},{35,3},{4,36},{36... | collective-permute-start | bytes 2359304 | tf_op jit(solution)/shard_map/ppermute | solution.py:41
  299.6 22.6 %all-to-all-start.4 = ((f32[16,9,128]{2,1,0:T(8,128)}), f32[16,9,128]{2,1,0:T(8,128)S(1)}, u32[]{:S(2)}, u32[]{:S(2)}) async-start(f32[16,9,128]{2,1,0:T(8,128)} %reshape.166), calls=%async_computation.4 | async-start | bytes 262144 | tf_op jit(solution)/shard_map/all_to_all | solution.py:138
  322.9 16.6 %all-to-all-start.5 = ((f32[16,9,128]{2,1,0:T(8,128)}), f32[16,9,128]{2,1,0:T(8,128)S(1)}, u32[]{:S(2)}, u32[]{:S(2)}) async-start(f32[16,9,128]{2,1,0:T(8,128)} %broadcast_in_dim.46), calls=%async_computation.5 | async-start | bytes 262144 | tf_op jit(solution)/shard_map/all_to_all | solution.py:140

commit v2 on v1

--- a/solution.py
+++ b/solution.py
@@ -41,31 +41,109 @@
     return lax.ppermute(v, "core", [(0, 1), (1, 0)])
 
 
-def assemble_kernel(at_ref, t0, t1, t2, t3, out_ref, sems):
+def nt(a, b):
+    return lax.dot_general(a, b, (((1,), (1,)), ((), ())), preferred_element_type=F32)
+
+
+def nn(a, b):
+    return jnp.dot(a, b, preferred_element_type=F32)
+
+
+STRIP = 256
+
+
+def strips(body):
+    def step(i, carry):
+        body(pl.ds(pl.multiple_of(i * STRIP, STRIP), STRIP))
+        return carry
+
+    lax.fori_loop(0, 1536 // STRIP, step, 0)
+
+
+def products(rows, branch, low, up, gate, wm, mixed, dx):
+    def forward(s):
+        p = nn(rows[...], wm[:, s]) + SCALE * nt(low[...], up[s, :])
+        mixed[:, s] = (p * gate[:, s]).astype(BF)
+
+    def back(s):
+        dx[:, s] = nt(branch[...], wm[s, :]).astype(dx.dtype)
+
+    strips(back)
+    strips(forward)
+
+
+def first_kernel(at, t0, t1, t2, t3, rows, branch, low, up, gate, wm, mixed, dx, blocks, sems):
     copies = []
     for k2, t in enumerate((t0, t1, t2, t3)):
         for k1 in range(4):
             b = k2 * 4 + k1
-            col = pl.multiple_of(at_ref[b] * 384, 128)
+            col = pl.multiple_of(at[b] * 384, 128)
             copy = pltpu.make_async_copy(
-                t.at[k1], out_ref.at[:, at_ref[16 + b], :, pl.ds(col, 384)], sems.at[b]
+                t.at[k1], blocks.at[:, at[16 + b], :, pl.ds(col, 384)], sems.at[b]
             )
             copy.start()
             copies.append(copy)
     for copy in copies:
         copy.wait()
 
-
-def assemble(at, blocks):
-    hbm = pl.BlockSpec(memory_space=pl.ANY)
+    def pack(z, carry):
+        part = blocks[z].astype(F32).reshape(96, 1536).astype(BF)
+        wm[pl.ds(pl.multiple_of(z * 96, 96), 96), :] = part
+        return carry
+
+    lax.fori_loop(0, 16, pack, 0)
+    products(rows, branch, low, up, gate, wm, mixed, dx)
+
+
+def second_kernel(wm, rows, branch, low, up, gate, low_grad, down, mixed, dx):
+    products(rows, branch, low, up, gate, wm, mixed, dx)
+
+    def add(s):
+        dx[:, s] = dx[:, s] + nt(low_grad[...], down[s, :])
+
+    strips(add)
+
+
+def vmem(n):
+    return [pl.BlockSpec(memory_space=pltpu.VMEM)] * n
+
+
+PARAMS = pltpu.CompilerParams(vmem_limit_bytes=48 * 1024 * 1024)
+HALF = 256 * 1536 * 1536 * 2
+
+
+def first_products(at, blocks, rows, branch, low, up, gate):
     return pl.pallas_call(
-        assemble_kernel,
-        out_shape=jax.ShapeDtypeStruct((16, 4, 24, 1536), BF),
-        in_specs=[pl.BlockSpec(memory_space=pltpu.SMEM)] + [hbm] * 4,
-        out_specs=hbm,
-        scratch_shapes=[pltpu.SemaphoreType.DMA((16,))],
-        name="assemble_weight",
-    )(at, *blocks)
+        first_kernel,
+        out_shape=(
+            jax.ShapeDtypeStruct((1536, 1536), BF),
+            jax.ShapeDtypeStruct((256, 1536), BF),
+            jax.ShapeDtypeStruct((256, 1536), BF),
+        ),
+        in_specs=[pl.BlockSpec(memory_space=pltpu.SMEM)]
+        + [pl.BlockSpec(memory_space=pl.ANY)] * 4
+        + vmem(5),
+        out_specs=tuple(vmem(3)),
+        scratch_shapes=[pltpu.VMEM((16, 4, 24, 1536), BF), pltpu.SemaphoreType.DMA((16,))],
+        compiler_params=PARAMS,
+        cost_estimate=pl.CostEstimate(flops=2 * HALF, bytes_accessed=13000000, transcendentals=0),
+        name="other_rows",
+    )(at, *blocks, rows, branch, low, up, gate)
+
+
+def second_products(wm, rows, branch, low, up, gate, low_grad, down):
+    return pl.pallas_call(
+        second_kernel,
+        out_shape=(
+            jax.ShapeDtypeStruct((256, 1536), BF),
+            jax.ShapeDtypeStruct((256, 1536), F32),
+        ),
+        in_specs=vmem(8),
+        out_specs=tuple(vmem(2)),
+        compiler_params=PARAMS,
+        cost_estimate=pl.CostEstimate(flops=2 * HALF, bytes_accessed=10000000, transcendentals=0),
+        name="own_rows",
+    )(wm, rows, branch, low, up, gate, low_grad, down)
 
 
 def per_device(rows, cotangent, codes, amax, down, up, gate_weight, timesteps):
@@ -77,12 +155,15 @@
     down_piece = lax.dynamic_slice(down, (6 * j, 0), (6, 128))
     up_piece = lax.dynamic_slice(upT, (12 * j, 0), (12, 128))
     gate_piece = lax.dynamic_slice(gate_weight, (0, core * 1536 + j * 192), (8, 192)).reshape(12, 128)
-    small = jnp.concatenate([down_piece, up_piece, gate_piece], axis=0)
-    small = lax.all_to_all(jnp.broadcast_to(small[None], (16, 30, 128)), "z", 0, 0, tiled=True)
 
     weight = (codes.astype(F32) * amax.astype(F32)[0]).astype(BF)
     piece = lax.dynamic_slice(weight, (24 * yh, core * 1536 + xi * 384), (24, 384))
-    line = lax.all_to_all(jnp.broadcast_to(piece[None], (16, 24, 384)), "z", 0, 0, tiled=True)
+    pieces = jnp.concatenate(
+        [piece[:, :128], piece[:, 128:256], piece[:, 256:], down_piece, up_piece, gate_piece], axis=0
+    )
+    line = lax.all_to_all(jnp.broadcast_to(pieces[None], (16, 102, 128)), "z", 0, 0, tiled=True)
+    small = line[:, 72:]
+    line = jnp.concatenate([line[:, :24], line[:, 24:48], line[:, 48:72]], axis=2)
     first = jnp.stack([line] + [lax.ppermute(line, AXES, plane_pairs(k, False)) for k in (1, 2, 3)])
     second = [first] + [lax.ppermute(first, AXES, plane_pairs(k, True)) for k in (2, 1, 3)]
     second = [second[0], second[2], second[1], second[3]]
@@ -132,34 +213,28 @@
     terms = jnp.concatenate([term_down, term_up], axis=2)
     mine = lax.dynamic_slice(terms, (0, core, 0, 0), (32, 1, 72, 128))
     yours = lax.dynamic_slice(terms, (0, 1 - core, 0, 0), (32, 1, 72, 128))
-    terms = (mine + other_core(yours)).astype(BF).reshape(16, 2, 8, 9, 128)
-    terms = terms.transpose(2, 1, 0, 3, 4).reshape(16, 144, 128)
-    terms = lax.all_to_all(terms, PLANE, 0, 0, tiled=True).astype(F32).sum(0).reshape(16, 9, 128)
-    terms = lax.all_to_all(terms, "z", 0, 0, tiled=True).sum(0)
-    terms = jnp.broadcast_to(terms[None], (16, 9, 128))
-    terms = lax.all_to_all(terms, ("yh", "x", "core"), 0, 0, tiled=True)
-    terms = terms.reshape(8, 2, 9, 128).transpose(1, 0, 2, 3).reshape(2, 72, 128)
+    terms = (mine + other_core(yours)).astype(BF).reshape(32, 4, 18, 128)
+    terms = lax.all_to_all(terms.transpose(1, 0, 2, 3), "x", 0, 0, tiled=True).astype(F32).sum(0)
+    terms = terms.astype(BF).reshape(16, 36, 128)
+    terms = lax.all_to_all(terms, "z", 0, 0, tiled=True).astype(F32).sum(0)
+    terms = jnp.broadcast_to(terms.reshape(1, 2, 18, 128), (8, 2, 18, 128)).reshape(16, 18, 128)
+    terms = lax.all_to_all(terms, PLANE, 0, 0, tiled=True)
+    terms = terms.reshape(2, 4, 2, 18, 128).sum((0, 2)).reshape(72, 128)
+    rest = other_core(terms)
+    terms = jnp.stack([jnp.where(core == 0, terms, rest), jnp.where(core == 0, rest, terms)])
     grad_scale = 131072**-0.5
     down_grad = terms[:, :24].reshape(48, 128) * grad_scale
     up_grad = terms[:, 24:].reshape(96, 128).T * (SCALE * grad_scale)
 
     low_other = jnp.dot(rows_other, down_all, preferred_element_type=F32).astype(BF)
     upT_half = lax.dynamic_slice(upT_all, (core * 1536, 0), (1536, 128))
-    wm = assemble(at, second).reshape(1536, 1536)
-
-    def back(b):
-        return lax.dot_general(b, wm, (((1,), (1,)), ((), ())), preferred_element_type=F32)
-
-    def forward(r, lo, g):
-        p = jnp.dot(r, wm, preferred_element_type=F32)
-        p = p + SCALE * lax.dot_general(lo, upT_half, (((1,), (1,)), ((), ())), preferred_element_type=F32)
-        return (p * g).astype(BF)
-
-    dx_rest = other_core(back(branch_other).astype(BF))
-    mixed_rest = other_core(forward(rows_other, low_other, gate_other))
-    mixed_own = forward(rows, low, gate_own)
-    dx = back(branch_own) + lax.dot_general(
-        low_grad, down_all, (((1,), (1,)), ((), ())), preferred_element_type=F32
+    wm, mixed_other, dx_other = first_products(
+        at, second, rows_other, branch_other, low_other, upT_half, gate_other
+    )
+    dx_rest = other_core(dx_other)
+    mixed_rest = other_core(mixed_other)
+    mixed_own, dx = second_products(
+        wm, rows, branch_own, low, upT_half, gate_own, low_grad, down_all
     )
     dx = (dx + dx_rest.astype(F32)).astype(BF)
     mixed = jnp.where(

time: 342 us -> 198 us (0.58)
  Pallas kernels: 145 us -> 19.4 us
  matrix products: 32.7 us -> 3.26 us
  waiting for transfers between devices: 35.8 us -> 44.3 us
  other arithmetic: 10.7 us -> 16.8 us
  starting transfers between devices: 94.6 us -> 89 us
    pallas_call x1 -> x2, Pallas kernels: 145 us -> 19.4 us  [the longest x1 11 us: first_products(): pl.pallas_call(first_kernel, out_shape=(jax.ShapeDtypeStruct((1536, 1536)...]
    dot_general x7 -> x1, matrix products: 27.4 us -> 0.35 us  [per_device(): jnp.dot(rows_other, down_all, preferred_element_type=F32).astype(BF)]
    ppermute x3, waiting for transfers between devices: 0.01 us -> 17.3 us  [per_device(): lax.ppermute(first, AXES, plane_pairs(k, True))]
    all_to_all x5 -> x4, starting transfers between devices: 45.9 us -> 34.7 us  [the longest x1 15.7 us: per_device(): lax.all_to_all(jnp.broadcast_to(pieces[None], (16, 102, 128)), 'z', 0, 0,...]
    all_to_all x5 -> x4, waiting for transfers between devices: 32 us -> 23.9 us  [the longest x1 19.3 us: per_device(): lax.all_to_all(jnp.broadcast_to(pieces[None], (16, 102, 128)), 'z', 0, 0,...]
    ppermute x6 -> x7, starting transfers between devices: 24.1 us -> 28.4 us  [other_core(): return lax.ppermute(v, 'core', [(0, 1), (1, 0)])]
    ppermute x3, waiting for transfers between devices: 3.81 us -> 0.01 us  [per_device(): lax.ppermute(line, AXES, plane_pairs(k, False))]
  transfers between devices with their start and end apart: 18 -> 18, of which waited for: 6 -> 5; matrix products, arithmetic and copies ran while one was open for 17% -> 16% of each run, Pallas kernels for 43% -> 10%
where the time goes in v2:
time: 198 us; the launch traced here: 196 us
  starting transfers between devices  89 us (45%)
  waiting for transfers between devices  44.3 us (22%)
  local copies, waits for them, and re-layouts  21.7 us (11%)
  Pallas kernels  19.4 us (10%)
  other arithmetic  16.8 us (8%)
  matrix products  3.26 us (2%)
  between operations  2 us (1%)
    ppermute x7, starting transfers between devices, other_core(): return lax.ppermute(v, 'core', [(0, 1), (1, 0)])  28.4 us
    all_to_all x1, waiting for transfers between devices, per_device(): lax.all_to_all(jnp.broadcast_to(pieces[None], (16, 102, 128)), 'z', 0, 0,...  19.3 us
    ppermute x3, waiting for transfers between devices, per_device(): lax.ppermute(first, AXES, plane_pairs(k, True))  17.3 us
    all_to_all x1, starting transfers between devices, per_device(): lax.all_to_all(jnp.broadcast_to(pieces[None], (16, 102, 128)), 'z', 0, 0,...  15.7 us
    pallas_call x1, Pallas kernels, first_products(): pl.pallas_call(first_kernel, out_shape=(jax.ShapeDtypeStruct((1536, 1536)...  11 us
    all_to_all x1, starting transfers between devices, per_device(): terms = lax.all_to_all(terms, 'z', 0, 0, tiled=True).astype(F32).sum(0)  10.3 us
    ppermute x3, starting transfers between devices, per_device(): lax.ppermute(first, AXES, plane_pairs(k, True))  9.59 us
    ppermute x3, starting transfers between devices, per_device(): lax.ppermute(line, AXES, plane_pairs(k, False))  9.57 us
  transfers between devices with their start and end apart: 18, of which 5 were waited for; matrix products, arithmetic and copies ran while one was open for 16% of the time, Pallas kernels for 10%

profile of v2, /device:TPU:1, one launch (start us, length us, event | category | flops | bytes accessed | tf_op | source)
XLA Modules:
  0.0 196.4 jit_solution(5675135440697908485)
XLA Ops:
  4.7 15.7 %all-to-all-start = ((bf16[16,102,128]{2,1,0:T(8,128)(2,1)}), bf16[16,102,128]{2,1,0:T(8,128)(2,1)S(1)}, u32[]{:S(2)}, u32[]{:S(2)}) async-start(bf16[16,102,128]{2,1,0:T(8,128)(2,1)} %broadcast_in_dim.35), calls=%async_computation | async-start | bytes 851968 | tf_op jit(solution)/shard_map/all_to_all | solution.py:164
  21.1 19.3 %all-to-all-done = bf16[16,102,128]{2,1,0:T(8,128)(2,1)S(1)} async-done(((bf16[16,102,128]{2,1,0:T(8,128)(2,1)}), bf16[16,102,128]{2,1,0:T(8,128)(2,1)S(1)}, u32[]{:S(2)}, u32[]{:S(2)}) %all-to-all-start) | async-done | bytes 417824 | tf_op jit(solution)/shard_map/all_to_all | solution.py:164
  42.3 6.8 %all-to-all-start.1 = ((bf16[16,294,128]{2,1,0:T(8,128)(2,1)}), bf16[16,294,128]{2,1,0:T(8,128)(2,1)S(1)}, u32[]{:S(2)}, u32[]{:S(2)}) async-start(bf16[16,294,128]{2,1,0:T(8,128)(2,1)} %pad_maximum_fusion), calls=%async_computation.1 | async-start | bytes 2424832 | tf_op jit(solution)/shard_map/all_to_all | solution.py:191
  50.0 3.2 %collective-permute-start = (bf16[16,24,384]{2,1,0:T(8,128)(2,1)}, bf16[16,24,384]{2,1,0:T(8,128)(2,1)S(1)}, u32[]{:S(2)}, u32[]{:S(2)}) collective-permute-start(bf16[16,24,384]{2,1,0:T(8,128)(2,1)} %get-tuple-element.22), channel_id=1, source_target_pairs={{0,64},{1,65},{2,66},{3,67},{4,68},{5,69},{6,70},{7,71},{8,72},{9,... | collective-permute-start | bytes 884744 | tf_op jit(solution)/shard_map/ppermute | solution.py:167
  53.2 4.3 %collective-permute-start.1 = (bf16[16,24,384]{2,1,0:T(8,128)(2,1)}, bf16[16,24,384]{2,1,0:T(8,128)(2,1)}, u32[]{:S(2)}, u32[]{:S(2)}) collective-permute-start(bf16[16,24,384]{2,1,0:T(8,128)(2,1)} %get-tuple-element.22), channel_id=1, source_target_pairs={{0,128},{1,129},{2,130},{3,131},{4,132},{5,133},{6,134},{7,135},{8... | collective-permute-start | bytes 884744 | tf_op jit(solution)/shard_map/ppermute | solution.py:167
  57.5 2.0 %collective-permute-start.2 = (bf16[16,24,384]{2,1,0:T(8,128)(2,1)}, bf16[16,24,384]{2,1,0:T(8,128)(2,1)}, u32[]{:S(2)}, u32[]{:S(2)}) collective-permute-start(bf16[16,24,384]{2,1,0:T(8,128)(2,1)} %get-tuple-element.22), channel_id=1, source_target_pairs={{0,192},{1,193},{2,194},{3,195},{4,196},{5,197},{6,198},{7,199},{8... | collective-permute-start | bytes 884744 | tf_op jit(solution)/shard_map/ppermute | solution.py:167
  59.6 3.0 %all-to-all-done.1 = bf16[16,294,128]{2,1,0:T(8,128)(2,1)S(1)} async-done(((bf16[16,294,128]{2,1,0:T(8,128)(2,1)}), bf16[16,294,128]{2,1,0:T(8,128)(2,1)S(1)}, u32[]{:S(2)}, u32[]{:S(2)}) %all-to-all-start.1) | async-done | bytes 1204256 | tf_op jit(solution)/shard_map/all_to_all | solution.py:191
  62.9 9.9 %collective-permute-start.7 = (f32[1,1536]{1,0:T(1,128)S(1)}, f32[1,1536]{1,0:T(1,128)S(1)}, u32[]{:S(2)}, u32[]{:S(2)}) collective-permute-start(f32[1,1536]{1,0:T(1,128)S(1)} %get-tuple-element.30.gate), channel_id=1, source_target_pairs={{0,32},{32,0},{1,33},{33,1},{2,34},{34,2},{3,35},{35,3},{4,36},{36... | collective-permute-start | bytes 18440 | tf_op jit(solution)/shard_map/ppermute | solution.py:41
  77.0 1.8 multiply_convert_fusion
  80.6 2.3 %copy.74 = f32[1536,128]{1,0:T(8,128)} copy(f32[1536,128]{0,1:T(8,128)} %convolution_bitcast_fusion) | data formatting | bytes 1572864 | tf_op jit(solution)/shard_map/dot_general | solution.py:211
  87.6 1.9 collective-permute-start.11
  89.5 2.4 %collective-permute-start.6 = (bf16[256,1536]{1,0:T(8,128)(2,1)S(1)}, bf16[256,1536]{1,0:T(8,128)(2,1)S(1)}, u32[]{:S(2)}, u32[]{:S(2)}) collective-permute-start(bf16[256,1536]{1,0:T(8,128)(2,1)S(1)} %copy-done.1), channel_id=1, source_target_pairs={{0,32},{32,0},{1,33},{33,1},{2,34},{34,2},{3,35},{35,3},{4,36},{36... | collective-permute-start | bytes 2359304 | tf_op jit(solution)/shard_map/ppermute | solution.py:41
  92.7 1.4 pad_maximum_fusion.1.t0
  94.1 1.9 collective-permute-start.3
  96.0 2.3 %collective-permute-start.4 = (bf16[4,16,24,384]{3,2,1,0:T(8,128)(2,1)S(1)}, bf16[4,16,24,384]{3,2,1,0:T(8,128)(2,1)}, u32[]{:S(2)}, u32[]{:S(2)}) collective-permute-start(bf16[4,16,24,384]{3,2,1,0:T(8,128)(2,1)S(1)} %pad_maximum_fusion.1.t0), channel_id=1, source_target_pairs={{0,256},{1,257},{2,258},{3,259},{4,260},{5,261},{6,262},{7,263},{8... | collective-permute-start | bytes 3538952 | tf_op jit(solution)/shard_map/ppermute | solution.py:168
  98.4 5.3 %collective-permute-start.5 = (bf16[4,16,24,384]{3,2,1,0:T(8,128)(2,1)S(1)}, bf16[4,16,24,384]{3,2,1,0:T(8,128)(2,1)}, u32[]{:S(2)}, u32[]{:S(2)}) collective-permute-start(bf16[4,16,24,384]{3,2,1,0:T(8,128)(2,1)S(1)} %pad_maximum_fusion.1.t0), channel_id=1, source_target_pairs={{0,257},{1,256},{2,259},{3,258},{4,261},{5,260},{6,263},{7,262},{8... | collective-permute-start | bytes 3538952 | tf_op jit(solution)/shard_map/ppermute | solution.py:168
  103.9 2.8 %constant_dynamic-slice_fusion.1 = (bf16[256,1536]{1,0:T(8,128)(2,1)}, bf16[256,1536]{1,0:T(8,128)(2,1)}) fusion(bf16[256,3072]{1,0:T(8,128)(2,1)} %copy-done.7, s32[]{:T(128)S(6)} %select_n.105, s32[]{:T(128)S(6)} %select_n.104), kind=kLoop, calls=%fused_computation.41 | loop fusion | bytes 3145736 | tf_op jit(solution)/shard_map/dynamic_slice | solution.py:207
  106.7 2.8 %collective-permute-start.8 = (bf16[256,1536]{1,0:T(8,128)(2,1)}, bf16[256,1536]{1,0:T(8,128)(2,1)}, u32[]{:S(2)}, u32[]{:S(2)}) collective-permute-start(bf16[256,1536]{1,0:T(8,128)(2,1)} %get-tuple-element.17), channel_id=1, source_target_pairs={{0,32},{32,0},{1,33},{33,1},{2,34},{34,2},{3,35},{35,3},{4,36},{36... | collective-permute-start | bytes 2359304 | tf_op jit(solution)/shard_map/ppermute | solution.py:41
  109.9 2.4 %add_convert_fusion.1 = bf16[32,1,72,128]{3,0,2,1:T(8,128)(2,1)} fusion(f32[32,1,72,128]{3,0,2,1:T(8,128)} %collective-permute-done.11, f32[32,2,72,128]{3,0,2,1:T(8,128)S(1)} %copy-done.10, s32[]{:T(128)S(6)} %select_n.101), kind=kLoop, calls=%fused_computation.7 | loop fusion | flops 589824 | bytes 2949124 | tf_op jit(solution)/shard_map/convert_element_type | solution.py:216
  112.3 4.2 %all-to-all-start.2 = ((bf16[4,32,18,128]{3,1,2,0:T(8,128)(2,1)}), bf16[4,32,18,128]{3,1,2,0:T(8,128)(2,1)}, u32[]{:S(2)}, u32[]{:S(2)}) async-start(bf16[4,32,18,128]{3,1,2,0:T(8,128)(2,1)} %bitcast.60), calls=%async_computation.2 | async-start | bytes 1179648 | tf_op jit(solution)/shard_map/all_to_all | solution.py:217
  117.5 7.5 %collective-permute-done.4.t2 = bf16[4,16,24,384]{3,2,1,0:T(8,128)(2,1)} collective-permute-done((bf16[4,16,24,384]{3,2,1,0:T(8,128)(2,1)S(1)}, bf16[4,16,24,384]{3,2,1,0:T(8,128)(2,1)}, u32[]{:S(2)}, u32[]{:S(2)}) %collective-permute-start.4) | collective-permute-done | bytes 1179680 | tf_op jit(solution)/shard_map/ppermute | solution.py:168
  125.0 9.8 %collective-permute-done.5.t3 = bf16[4,16,24,384]{3,2,1,0:T(8,128)(2,1)} collective-permute-done((bf16[4,16,24,384]{3,2,1,0:T(8,128)(2,1)S(1)}, bf16[4,16,24,384]{3,2,1,0:T(8,128)(2,1)}, u32[]{:S(2)}, u32[]{:S(2)}) %collective-permute-start.5) | collective-permute-done | bytes 1179680 | tf_op jit(solution)/shard_map/ppermute | solution.py:168
  134.8 11.0 %other_rows.1 = (bf16[1536,1536]{1,0:T(8,128)(2,1)}, bf16[256,1536]{1,0:T(8,128)(2,1)}, bf16[256,1536]{1,0:T(8,128)(2,1)}) custom-call(s32[32]{0:T(128)S(1)} %pad_add_fusion.at, bf16[4,16,24,384]{3,2,1,0:T(8,128)(2,1)S(1)} %pad_maximum_fusion.1.t0, bf16[4,16,24,384]{3,2,1,0:T(8,128)(2,1)} %collective-permute-done.3.t1, ...), custom_call_target="tpu_custom_call" | custom-call | flops 2415919104 | bytes 13000000 | tf_op jit(solution)/shard_map/other_rows/pallas_call | solution.py:116
  145.8 2.1 %collective-permute-start.10 = (bf16[256,1536]{1,0:T(8,128)(2,1)}, bf16[256,1536]{1,0:T(8,128)(2,1)}, u32[]{:S(2)}, u32[]{:S(2)}) collective-permute-start(bf16[256,1536]{1,0:T(8,128)(2,1)} %get-tuple-element.13), channel_id=1, source_target_pairs={{0,32},{32,0},{1,33},{33,1},{2,34},{34,2},{3,35},{35,3},{4,36},{36... | collective-permute-start | bytes 2359304 | tf_op jit(solution)/shard_map/ppermute | solution.py:41
  149.8 10.3 %all-to-all-start.3 = ((bf16[16,36,128]{2,1,0:T(8,128)(2,1)}), bf16[16,36,128]{2,1,0:T(8,128)(2,1)S(1)}, u32[]{:S(2)}, u32[]{:S(2)}) async-start(bf16[16,36,128]{2,1,0:T(8,128)(2,1)} %reshape.161), calls=%async_computation.3 | async-start | bytes 327680 | tf_op jit(solution)/shard_map/all_to_all | solution.py:219
  160.1 2.7 %collective-permute-start.9 = (bf16[256,1536]{1,0:T(8,128)(2,1)}, bf16[256,1536]{1,0:T(8,128)(2,1)}, u32[]{:S(2)}, u32[]{:S(2)}) collective-permute-start(bf16[256,1536]{1,0:T(8,128)(2,1)} %get-tuple-element.11), channel_id=1, source_target_pairs={{0,32},{32,0},{1,33},{33,1},{2,34},{34,2},{3,35},{35,3},{4,36},{36... | collective-permute-start | bytes 2359304 | tf_op jit(solution)/shard_map/ppermute | solution.py:41
  163.9 8.4 %own_rows.1 = (bf16[256,1536]{1,0:T(8,128)(2,1)S(1)}, f32[256,1536]{1,0:T(8,128)S(1)}) custom-call(bf16[1536,1536]{1,0:T(8,128)(2,1)} %get-tuple-element.9.wm, bf16[256,1536]{1,0:T(8,128)(2,1)S(1)} %copy-done.1, bf16[256,1536]{1,0:T(8,128)(2,1)S(1)} %copy-done.2, bf16[256,128]{1,0:T(8,128)(2,1)S(1)} %bitcast.55, bf16[1536,128]{1,0:T(8,128)(2,1)S(1)} %copy-done.6, ...), custom_call_target="tpu_custom_call" | custom-call | flops 2415919104 | bytes 10000000 | tf_op jit(solution)/shard_map/own_rows/pallas_call | solution.py:135
  174.0 4.5 %all-to-all-start.4 = ((f32[16,18,128]{2,1,0:T(8,128)}), f32[16,18,128]{2,1,0:T(8,128)S(1)}, u32[]{:S(2)}, u32[]{:S(2)}) async-start(f32[16,18,128]{2,1,0:T(8,128)} %bitcast.22), calls=%async_computation.4 | async-start | bytes 393216 | tf_op jit(solution)/shard_map/all_to_all | solution.py:221
  178.5 2.3 %add_convert_fusion = bf16[256,1536]{1,0:T(8,128)(2,1)} fusion(f32[256,1536]{1,0:T(8,128)S(1)} %get-tuple-element.12, bf16[256,1536]{1,0:T(8,128)(2,1)} %collective-permute-done.10), kind=kLoop, calls=%fused_computation.4 | loop fusion | flops 1179648 | bytes 3145728 | tf_op jit(solution)/shard_map/convert_element_type | solution.py:239
  180.8 4.6 %all-to-all-done.4 = f32[16,18,128]{2,1,0:T(8,128)S(1)} async-done(((f32[16,18,128]{2,1,0:T(8,128)}), f32[16,18,128]{2,1,0:T(8,128)S(1)}, u32[]{:S(2)}, u32[]{:S(2)}) %all-to-all-start.4) | async-done | bytes 147488 | tf_op jit(solution)/shard_map/all_to_all | solution.py:221
  185.5 6.7 %collective-permute-start.12 = (f32[72,128]{1,0:T(8,128)S(1)}, f32[72,128]{1,0:T(8,128)S(1)}, u32[]{:S(2)}, u32[]{:S(2)}) collective-permute-start(f32[72,128]{1,0:T(8,128)S(1)} %reshape.164), channel_id=1, source_target_pairs={{0,32},{32,0},{1,33},{33,1},{2,34},{34,2},{3,35},{35,3},{4,36},{36... | collective-permute-start | bytes 110600 | tf_op jit(solution)/shard_map/ppermute | solution.py:41
  192.2 3.0 %maximum_select_fusion = bf16[256,3072]{1,0:T(8,128)(2,1)} fusion(bf16[256,1536]{1,0:T(8,128)(2,1)} %collective-permute-done.9, bf16[256,1536]{1,0:T(8,128)(2,1)S(1)} %copy-done.4, pred[]{:T(512)S(6)} %eq.2), kind=kLoop, calls=%fused_computation.2 | loop fusion | flops 7077888 | bytes 3145729 | tf_op jit(solution)/shard_map/jit(_where)/select_n | solution.py:240
  (105 shorter events, 25.8 us)
Async XLA Ops:
  0.6 1.5 copy-start
  0.6 19.9 %copy-start.12 = (s32[32]{0:T(128)S(1)}, s32[32]{0:T(128)}, u32[]{:S(2)}) copy-start(s32[32]{0:T(128)} %param.15) | copy-start | bytes 388
  4.7 35.7 %all-to-all-start = ((bf16[16,102,128]{2,1,0:T(8,128)(2,1)}), bf16[16,102,128]{2,1,0:T(8,128)(2,1)S(1)}, u32[]{:S(2)}, u32[]{:S(2)}) async-start(bf16[16,102,128]{2,1,0:T(8,128)(2,1)} %broadcast_in_dim.35), calls=%async_computation | async-start | bytes 851968 | tf_op jit(solution)/shard_map/all_to_all | solution.py:164
  42.3 20.4 %all-to-all-start.1 = ((bf16[16,294,128]{2,1,0:T(8,128)(2,1)}), bf16[16,294,128]{2,1,0:T(8,128)(2,1)S(1)}, u32[]{:S(2)}, u32[]{:S(2)}) async-start(bf16[16,294,128]{2,1,0:T(8,128)(2,1)} %pad_maximum_fusion), calls=%async_computation.1 | async-start | bytes 2424832 | tf_op jit(solution)/shard_map/all_to_all | solution.py:191
  50.0 42.0 %collective-permute-start = (bf16[16,24,384]{2,1,0:T(8,128)(2,1)}, bf16[16,24,384]{2,1,0:T(8,128)(2,1)S(1)}, u32[]{:S(2)}, u32[]{:S(2)}) collective-permute-start(bf16[16,24,384]{2,1,0:T(8,128)(2,1)} %get-tuple-element.22), channel_id=1, source_target_pairs={{0,64},{1,65},{2,66},{3,67},{4,68},{5,69},{6,70},{7,71},{8,72},{9,... | collective-permute-start | bytes 884744 | tf_op jit(solution)/shard_map/ppermute | solution.py:167
  53.2 38.7 %collective-permute-start.1 = (bf16[16,24,384]{2,1,0:T(8,128)(2,1)}, bf16[16,24,384]{2,1,0:T(8,128)(2,1)}, u32[]{:S(2)}, u32[]{:S(2)}) collective-permute-start(bf16[16,24,384]{2,1,0:T(8,128)(2,1)} %get-tuple-element.22), channel_id=1, source_target_pairs={{0,128},{1,129},{2,130},{3,131},{4,132},{5,133},{6,134},{7,135},{8... | collective-permute-start | bytes 884744 | tf_op jit(solution)/shard_map/ppermute | solution.py:167
  57.5 34.4 %collective-permute-start.2 = (bf16[16,24,384]{2,1,0:T(8,128)(2,1)}, bf16[16,24,384]{2,1,0:T(8,128)(2,1)}, u32[]{:S(2)}, u32[]{:S(2)}) collective-permute-start(bf16[16,24,384]{2,1,0:T(8,128)(2,1)} %get-tuple-element.22), channel_id=1, source_target_pairs={{0,192},{1,193},{2,194},{3,195},{4,196},{5,197},{6,198},{7,199},{8... | collective-permute-start | bytes 884744 | tf_op jit(solution)/shard_map/ppermute | solution.py:167
  62.9 14.0 %collective-permute-start.7 = (f32[1,1536]{1,0:T(1,128)S(1)}, f32[1,1536]{1,0:T(1,128)S(1)}, u32[]{:S(2)}, u32[]{:S(2)}) collective-permute-start(f32[1,1536]{1,0:T(1,128)S(1)} %get-tuple-element.30.gate), channel_id=1, source_target_pairs={{0,32},{32,0},{1,33},{33,1},{2,34},{34,2},{3,35},{35,3},{4,36},{36... | collective-permute-start | bytes 18440 | tf_op jit(solution)/shard_map/ppermute | solution.py:41
  73.3 1.1 copy-start.1
  77.0 1.8 copy-start.8
  78.8 5.4 %copy-start.7 = (bf16[256,3072]{1,0:T(8,128)(2,1)}, bf16[256,3072]{1,0:T(8,128)(2,1)S(1)}, u32[]{:S(2)}) copy-start(bf16[256,3072]{1,0:T(8,128)(2,1)S(1)} %multiply_convert_fusion) | copy-start | bytes 4718596
  85.8 1.8 copy-start.9
  87.6 22.3 %collective-permute-start.11 = (f32[32,1,72,128]{3,0,2,1:T(8,128)}, f32[32,1,72,128]{3,0,2,1:T(8,128)}, u32[]{:S(2)}, u32[]{:S(2)}) collective-permute-start(f32[32,1,72,128]{3,0,2,1:T(8,128)} %constant_dynamic-slice_fusion), channel_id=1, source_target_pairs={{0,32},{32,0},{1,33},{33,1},{2,34},{34,2},{3,35},{35,3},{4,36},{36... | collective-permute-start | bytes 3538952 | tf_op jit(solution)/shard_map/ppermute | solution.py:41
  89.5 17.1 %collective-permute-start.6 = (bf16[256,1536]{1,0:T(8,128)(2,1)S(1)}, bf16[256,1536]{1,0:T(8,128)(2,1)S(1)}, u32[]{:S(2)}, u32[]{:S(2)}) collective-permute-start(bf16[256,1536]{1,0:T(8,128)(2,1)S(1)} %copy-done.1), channel_id=1, source_target_pairs={{0,32},{32,0},{1,33},{33,1},{2,34},{34,2},{3,35},{35,3},{4,36},{36... | collective-permute-start | bytes 2359304 | tf_op jit(solution)/shard_map/ppermute | solution.py:41
  92.0 0.7 copy-start.11
  94.1 23.4 %collective-permute-start.3 = (bf16[4,16,24,384]{3,2,1,0:T(8,128)(2,1)S(1)}, bf16[4,16,24,384]{3,2,1,0:T(8,128)(2,1)}, u32[]{:S(2)}, u32[]{:S(2)}) collective-permute-start(bf16[4,16,24,384]{3,2,1,0:T(8,128)(2,1)S(1)} %pad_maximum_fusion.1.t0), channel_id=1, source_target_pairs={{0,1},{1,0},{2,3},{3,2},{4,5},{5,4},{6,7},{7,6},{8,9},{9,8},{10,11... | collective-permute-start | bytes 3538952 | tf_op jit(solution)/shard_map/ppermute | solution.py:168
  96.0 29.0 %collective-permute-start.4 = (bf16[4,16,24,384]{3,2,1,0:T(8,128)(2,1)S(1)}, bf16[4,16,24,384]{3,2,1,0:T(8,128)(2,1)}, u32[]{:S(2)}, u32[]{:S(2)}) collective-permute-start(bf16[4,16,24,384]{3,2,1,0:T(8,128)(2,1)S(1)} %pad_maximum_fusion.1.t0), channel_id=1, source_target_pairs={{0,256},{1,257},{2,258},{3,259},{4,260},{5,261},{6,262},{7,263},{8... | collective-permute-start | bytes 3538952 | tf_op jit(solution)/shard_map/ppermute | solution.py:168
  98.4 36.4 %collective-permute-start.5 = (bf16[4,16,24,384]{3,2,1,0:T(8,128)(2,1)S(1)}, bf16[4,16,24,384]{3,2,1,0:T(8,128)(2,1)}, u32[]{:S(2)}, u32[]{:S(2)}) collective-permute-start(bf16[4,16,24,384]{3,2,1,0:T(8,128)(2,1)S(1)} %pad_maximum_fusion.1.t0), channel_id=1, source_target_pairs={{0,257},{1,256},{2,259},{3,258},{4,261},{5,260},{6,263},{7,262},{8... | collective-permute-start | bytes 3538952 | tf_op jit(solution)/shard_map/ppermute | solution.py:168
  103.9 6.0 %copy-start.10 = (f32[32,2,72,128]{3,0,2,1:T(8,128)S(1)}, f32[32,2,72,128]{3,0,2,1:T(8,128)}, u32[]{:S(2)}) copy-start(f32[32,2,72,128]{3,0,2,1:T(8,128)} %copy-done.9) | copy-start | bytes 7077892
  106.7 28.1 %collective-permute-start.8 = (bf16[256,1536]{1,0:T(8,128)(2,1)}, bf16[256,1536]{1,0:T(8,128)(2,1)}, u32[]{:S(2)}, u32[]{:S(2)}) collective-permute-start(bf16[256,1536]{1,0:T(8,128)(2,1)} %get-tuple-element.17), channel_id=1, source_target_pairs={{0,32},{32,0},{1,33},{33,1},{2,34},{34,2},{3,35},{35,3},{4,36},{36... | collective-permute-start | bytes 2359304 | tf_op jit(solution)/shard_map/ppermute | solution.py:41
  112.3 35.6 %all-to-all-start.2 = ((bf16[4,32,18,128]{3,1,2,0:T(8,128)(2,1)}), bf16[4,32,18,128]{3,1,2,0:T(8,128)(2,1)}, u32[]{:S(2)}, u32[]{:S(2)}) async-start(bf16[4,32,18,128]{3,1,2,0:T(8,128)(2,1)} %bitcast.60), calls=%async_computation.2 | async-start | bytes 1179648 | tf_op jit(solution)/shard_map/all_to_all | solution.py:217
  117.5 28.3 %copy-start.5 = (bf16[1536,128]{1,0:T(8,128)(2,1)}, bf16[1536,128]{1,0:T(8,128)(2,1)S(1)}, u32[]{:S(2)}) copy-start(bf16[1536,128]{1,0:T(8,128)(2,1)S(1)} %constant_dynamic-slice_fusion.2.up) | copy-start | bytes 1179652
  145.8 17.0 %copy-start.6 = (bf16[1536,128]{1,0:T(8,128)(2,1)S(1)}, bf16[1536,128]{1,0:T(8,128)(2,1)}, u32[]{:S(2)}) copy-start(bf16[1536,128]{1,0:T(8,128)(2,1)} %copy-done.5) | copy-start | bytes 1179652
  145.8 32.7 %collective-permute-start.10 = (bf16[256,1536]{1,0:T(8,128)(2,1)}, bf16[256,1536]{1,0:T(8,128)(2,1)}, u32[]{:S(2)}, u32[]{:S(2)}) collective-permute-start(bf16[256,1536]{1,0:T(8,128)(2,1)} %get-tuple-element.13), channel_id=1, source_target_pairs={{0,32},{32,0},{1,33},{33,1},{2,34},{34,2},{3,35},{35,3},{4,36},{36... | collective-permute-start | bytes 2359304 | tf_op jit(solution)/shard_map/ppermute | solution.py:41
  149.8 23.5 %all-to-all-start.3 = ((bf16[16,36,128]{2,1,0:T(8,128)(2,1)}), bf16[16,36,128]{2,1,0:T(8,128)(2,1)S(1)}, u32[]{:S(2)}, u32[]{:S(2)}) async-start(bf16[16,36,128]{2,1,0:T(8,128)(2,1)} %reshape.161), calls=%async_computation.3 | async-start | bytes 327680 | tf_op jit(solution)/shard_map/all_to_all | solution.py:219
  160.1 32.1 %collective-permute-start.9 = (bf16[256,1536]{1,0:T(8,128)(2,1)}, bf16[256,1536]{1,0:T(8,128)(2,1)}, u32[]{:S(2)}, u32[]{:S(2)}) collective-permute-start(bf16[256,1536]{1,0:T(8,128)(2,1)} %get-tuple-element.11), channel_id=1, source_target_pairs={{0,32},{32,0},{1,33},{33,1},{2,34},{34,2},{3,35},{35,3},{4,36},{36... | collective-permute-start | bytes 2359304 | tf_op jit(solution)/shard_map/ppermute | solution.py:41
  162.8 1.1 copy-start.2
  172.4 0.9 copy-start.3
  174.0 11.5 %all-to-all-start.4 = ((f32[16,18,128]{2,1,0:T(8,128)}), f32[16,18,128]{2,1,0:T(8,128)S(1)}, u32[]{:S(2)}, u32[]{:S(2)}) async-start(f32[16,18,128]{2,1,0:T(8,128)} %bitcast.22), calls=%async_computation.4 | async-start | bytes 393216 | tf_op jit(solution)/shard_map/all_to_all | solution.py:221
  178.5 13.7 %copy-start.4 = (bf16[256,1536]{1,0:T(8,128)(2,1)S(1)}, bf16[256,1536]{1,0:T(8,128)(2,1)}, u32[]{:S(2)}) copy-start(bf16[256,1536]{1,0:T(8,128)(2,1)} %copy-done.3) | copy-start | bytes 2359300
  185.5 9.7 %collective-permute-start.12 = (f32[72,128]{1,0:T(8,128)S(1)}, f32[72,128]{1,0:T(8,128)S(1)}, u32[]{:S(2)}, u32[]{:S(2)}) collective-permute-start(f32[72,128]{1,0:T(8,128)S(1)} %reshape.164), channel_id=1, source_target_pairs={{0,32},{32,0},{1,33},{33,1},{2,34},{34,2},{3,35},{35,3},{4,36},{36... | collective-permute-start | bytes 110600 | tf_op jit(solution)/shard_map/ppermute | solution.py:41

commit v3 on v2

v3 whole, which is shorter than its diff:
```python
import math

import jax
import jax.numpy as jnp
from jax import lax
from jax.experimental import pallas as pl
from jax.experimental.pallas import tpu as pltpu
from jax.sharding import Mesh
from jax.sharding import PartitionSpec as P

FREQ = 256
SCALE = 0.5
AXES = ("yh", "x", "core", "z", "yl")
SIZES = (2, 4, 2, 16, 2)
PLANE = ("yh", "x", "yl")
BF = jnp.bfloat16
F32 = jnp.float32


def index_of(yh, x, c, z, yl):
    return (((yh * 4 + x) * 2 + c) * 16 + z) * 2 + yl


def plane_pairs(k, swap):
    pairs = []
    for yh in range(2):
        for x in range(4):
            for c in range(2):
                for z in range(16):
                    for yl in range(2):
                        tx, ty = x, yh * 2 + yl
                        if (c == 0) != swap:
                            tx ^= k
                        else:
                            ty ^= k
                        pairs.append((index_of(yh, x, c, z, yl), index_of(ty >> 1, tx, c, z, ty & 1)))
    return pairs


def other_core(v):
    return lax.ppermute(v, "core", [(0, 1), (1, 0)])


def nt(a, b):
    return lax.dot_general(a, b, (((1,), (1,)), ((), ())), preferred_element_type=F32)


def nn(a, b):
    return jnp.dot(a, b, preferred_element_type=F32)


STRIPS = [slice(i, i + 256) for i in range(0, 1536, 256)]


def products_kernel(
    at, t0, t1, t2, t3, rows_other, branch_other, low_other, gate_other,
    rows, branch, low, gate, low_grad, up, down,
    mixed_other, dx_other, mixed, dx, blocks, wm, sems,
):
    copies = []
    for k2, t in enumerate((t0, t1, t2, t3)):
        for k1 in range(4):
            b = k2 * 4 + k1
            col = pl.multiple_of(at[b] * 384, 128)
            copy = pltpu.make_async_copy(
                t.at[k1], blocks.at[:, at[16 + b], :, pl.ds(col, 384)], sems.at[b]
            )
            copy.start()
            copies.append(copy)
    for copy in copies:
        copy.wait()

    def pack(z, carry):
        part = blocks[z].astype(F32).reshape(96, 1536).astype(BF)
        wm[pl.ds(pl.multiple_of(z * 96, 96), 96), :] = part
        return carry

    lax.fori_loop(0, 16, pack, 0)
    for s in STRIPS:
        dx_other[:, s] = nt(branch_other[...], wm[s, :]).astype(BF)
        dx[:, s] = nt(branch[...], wm[s, :]) + nt(low_grad[...], down[s, :])
    for s in STRIPS:
        p = nn(rows_other[...], wm[:, s]) + SCALE * nt(low_other[...], up[s, :])
        mixed_other[:, s] = (p * gate_other[:, s]).astype(BF)
        p = nn(rows[...], wm[:, s]) + SCALE * nt(low[...], up[s, :])
        mixed[:, s] = (p * gate[:, s]).astype(BF)


def finish_kernel(core, mixed_own, mixed_rest, dx_own, dx_rest, mixed, dx):
    own = pl.multiple_of(core[0] * 1536, 128)
    mixed[:, pl.ds(own, 1536)] = mixed_own[...]
    mixed[:, pl.ds(pl.multiple_of(1536 - own, 128), 1536)] = mixed_rest[...]
    dx[...] = (dx_own[...] + dx_rest[...].astype(F32)).astype(BF)


def vmem(n):
    return [pl.BlockSpec(memory_space=pltpu.VMEM)] * n


def adapter_kernel(
    core, got, rows, rows_other, cot,
    own, other, low, low_other, low_grad, down, up_half, gate_own, gate_other, mine, yours,
    wide, down_wide, up_wide, up, gates, branch, td, tu,
):
    for s in range(16):
        wide[s] = got[s].astype(F32)
        j, yl = s // 2, s % 2
        for z in range(16):
            a, b = 96 * z + 48 * yl + 6 * j, 192 * z + 96 * yl + 12 * j
            down_wide[a : a + 6] = wide[s, 18 * z : 18 * z + 6]
            up_wide[b : b + 12] = wide[s, 18 * z + 6 : 18 * z + 18]
    for j in range(8):
        part = wide[2 * j, 288:300] + wide[2 * j + 1, 288:300]
        part = part[:6] + part[6:]
        for r in range(6):
            at = 384 * j + 128 * (r % 3)
            gates[r // 3 : r // 3 + 1, at : at + 128] = part[r : r + 1]
    down[...] = down_wide[...].astype(BF)
    up[...] = up_wide[...].astype(BF)
    at = pl.multiple_of(core[0] * 1536, 128)
    rest = pl.multiple_of(1536 - at, 128)
    up_half[...] = up[pl.ds(at, 1536), :]
    first = core[0] == 0
    gate = jnp.where(first, gates[0:1], gates[1:2])
    gate_own[...] = jnp.where(first, gates[0:1, :1536], gates[1:2, 1536:])
    gate_other[...] = jnp.where(first, gates[1:2, :1536], gates[0:1, 1536:])

    branch[...] = (cot[...].astype(F32) * gate).astype(BF)
    own[...] = branch[:, pl.ds(at, 1536)]
    other[...] = branch[:, pl.ds(rest, 1536)]
    low_other[...] = nn(rows_other[...], down[...]).astype(BF)
    a = nn(rows[...], down[...]).astype(BF)
    low[...] = a
    b = (SCALE * nn(branch[...], up[...])).astype(BF)
    low_grad[...] = b
    a = a.astype(F32).T.astype(BF)
    b = b.astype(F32).T.astype(BF)
    for i in range(0, 1536, 384):
        td[i : i + 384, :] = nn(b, rows[:, i : i + 384]).T
    for i in range(0, 3072, 384):
        tu[i : i + 384, :] = nn(a, branch[:, i : i + 384]).T

    def put(h, ref):
        ref[:, :24] = td[...].reshape(32, 2, 24, 128)[:, h]
        ref[:, 24:] = tu[...].reshape(32, 2, 48, 128)[:, h]

    @pl.when(first)
    def _():
        put(0, mine)
        put(1, yours)

    @pl.when(jnp.logical_not(first))
    def _():
        put(1, mine)
        put(0, yours)


PARAMS = pltpu.CompilerParams(vmem_limit_bytes=28 * 1024 * 1024)
HALF = 256 * 1536 * 1536 * 2


def products(at, blocks, *args):
    half = jax.ShapeDtypeStruct((256, 1536), BF)
    return pl.pallas_call(
        products_kernel,
        out_shape=(half, half, half, jax.ShapeDtypeStruct((256, 1536), F32)),
        in_specs=[pl.BlockSpec(memory_space=pltpu.SMEM)]
        + [pl.BlockSpec(memory_space=pl.ANY)] * 4
        + vmem(11),
        out_specs=tuple(vmem(4)),
        scratch_shapes=[
            pltpu.VMEM((16, 4, 24, 1536), BF),
            pltpu.VMEM((1536, 1536), BF),
            pltpu.SemaphoreType.DMA((16,)),
        ],
        compiler_params=PARAMS,
        cost_estimate=pl.CostEstimate(flops=4 * HALF, bytes_accessed=12000000, transcendentals=0),
        name="products",
    )(at, *blocks, *args)


def finish(core, *args):
    return pl.pallas_call(
        finish_kernel,
        out_shape=(jax.ShapeDtypeStruct((256, 3072), BF), jax.ShapeDtypeStruct((256, 1536), BF)),
        in_specs=[pl.BlockSpec(memory_space=pltpu.SMEM)] + vmem(4),
        out_specs=tuple(vmem(2)),
        compiler_params=pltpu.CompilerParams(vmem_limit_bytes=16 * 1024 * 1024),
        cost_estimate=pl.CostEstimate(flops=1000000, bytes_accessed=7000000, transcendentals=0),
        name="finish",
    )(core.reshape(1), *args)


def adapter_terms(core, got, rows, rows_other, cot):
    def out(*shape):
        return jax.ShapeDtypeStruct(shape, BF)

    half, thin, row = out(256, 1536), out(256, 128), jax.ShapeDtypeStruct((1, 1536), F32)
    term = jax.ShapeDtypeStruct((32, 72, 128), F32)
    tall = out(1536, 128)
    return pl.pallas_call(
        adapter_kernel,
        out_shape=(half, half, thin, thin, thin, tall, tall, row, row, term, term),
        in_specs=[pl.BlockSpec(memory_space=pltpu.SMEM)] + vmem(4),
        out_specs=tuple(vmem(11)),
        scratch_shapes=[
            pltpu.VMEM((16, 300, 128), F32),
            pltpu.VMEM((1536, 128), F32),
            pltpu.VMEM((3072, 128), F32),
            pltpu.VMEM((3072, 128), BF),
            pltpu.VMEM((2, 3072), F32),
            pltpu.VMEM((256, 3072), BF),
            pltpu.VMEM((1536, 128), F32),
            pltpu.VMEM((3072, 128), F32),
        ],
        compiler_params=PARAMS,
        cost_estimate=pl.CostEstimate(flops=700000000, bytes_accessed=12000000, transcendentals=0),
        name="adapter_terms",
    )(core.reshape(1), got, rows, rows_other, cot)


def per_device(rows, cotangent, codes, amax, down, up, gate_weight, timesteps):
    yh, xi, core, z, yl = (lax.axis_index(a) for a in AXES)
    j = yh * 4 + xi
    y = yh * 2 + yl

    upT = up.T
    down_piece = lax.dynamic_slice(down, (6 * j, 0), (6, 128))
    up_piece = lax.dynamic_slice(upT, (12 * j, 0), (12, 128))
    gate_piece = lax.dynamic_slice(gate_weight, (0, j * 384), (8, 384)).reshape(24, 128)

    weight = (codes.astype(F32) * amax.astype(F32)[0]).astype(BF)
    piece = lax.dynamic_slice(weight, (24 * yh, core * 1536 + xi * 384), (24, 384))
    pieces = jnp.concatenate(
        [piece[:, :128], piece[:, 128:256], piece[:, 256:], down_piece, up_piece, gate_piece], axis=0
    )
    line = lax.all_to_all(jnp.broadcast_to(pieces[None], (16, 114, 128)), "z", 0, 0, tiled=True)
    line, rows_other = lax.optimization_barrier((line, other_core(rows)))
    small = line[:, 72:]
    line = jnp.concatenate([line[:, :24], line[:, 24:48], line[:, 48:72]], axis=2)
    first = jnp.stack([line] + [lax.ppermute(line, AXES, plane_pairs(k, False)) for k in (1, 2, 3)])
    k1 = jnp.tile(jnp.arange(4), 4)
    k2 = jnp.repeat(jnp.arange(4), 4)
    bx = xi ^ jnp.where(core == 0, k1, k2)
    by = y ^ jnp.where(core == 0, k2, k1)
    at = jnp.concatenate([bx, (by & 1) * 2 + (by >> 1)]).astype(jnp.int32)

    half_freq = FREQ // 2
    frequency = jnp.exp(-math.log(10000.0) * jnp.arange(half_freq, dtype=F32) / half_freq)
    steps = lax.dynamic_slice(timesteps.reshape(16, 2), (0, z // 8), (16, 1))
    phase = steps.astype(F32) * frequency[None, :]
    features = jnp.concatenate([jnp.cos(phase), jnp.sin(phase)], axis=1).astype(BF)
    features = lax.dynamic_slice(features.reshape(16, 16, 2, 8), (0, 0, yl, 0), (16, 16, 1, 8))
    gate_block = small[:, 18:].reshape(16, 8, 384).reshape(128, 384)
    part = jnp.dot(features.reshape(16, 128), gate_block, preferred_element_type=F32)
    high = lax.reduce_precision(part, 8, 7)
    pair = jnp.stack([high.astype(BF), (part - high).astype(BF)])
    pair = pair.reshape(2, 8, 2, 384).transpose(1, 0, 2, 3).reshape(8, 1, 12, 128)
    pair = jnp.broadcast_to(pair, (8, 2, 12, 128)).reshape(16, 12, 128)
    maps = jnp.broadcast_to(small[:, :18].reshape(1, 288, 128), (16, 288, 128))
    got = lax.all_to_all(jnp.concatenate([maps, pair], axis=1), PLANE, 0, 0, tiled=True)
    got, first = lax.optimization_barrier((got, first))
    second = [first] + [lax.ppermute(first, AXES, plane_pairs(k, True)) for k in (2, 1, 3)]
    second = [second[0], second[2], second[1], second[3]]

    (
        branch_own, branch_send, low, low_other, low_grad, down_all, up_half,
        gate_own, gate_other, mine, yours,
    ) = adapter_terms(core, got, rows, rows_other, cotangent)
    branch_other = other_core(branch_send)
    terms = (mine + other_core(yours)).astype(BF).reshape(16, 144, 128)
    terms, second[1] = lax.optimization_barrier((terms, second[1]))
    terms = lax.all_to_all(terms, "z", 0, 0, tiled=True).astype(F32).sum(0).astype(BF)

    mixed_other, dx_other, mixed_own, dx_own = products(
        at, second, rows_other, branch_other, low_other, gate_other,
        rows, branch_own, low, gate_own, low_grad, up_half, down_all,
    )
    dx_rest = other_core(dx_other)
    mixed_rest = other_core(mixed_other)
    dx_rest, mixed_rest, terms = lax.optimization_barrier((dx_rest, mixed_rest, terms))
    mixed, dx = finish(core, mixed_own, mixed_rest, dx_own, dx_rest)

    terms = jnp.broadcast_to(terms.reshape(1, 2, 72, 128), (8, 2, 72, 128)).reshape(16, 72, 128)
    terms = lax.all_to_all(terms, PLANE, 0, 0, tiled=True).astype(F32).sum(0)
    rest = other_core(terms)
    terms = jnp.stack([jnp.where(core == 0, terms, rest), jnp.where(core == 0, rest, terms)])
    grad_scale = 131072**-0.5
    down_grad = terms[:, :24].reshape(48, 128) * grad_scale
    up_grad = terms[:, 24:].reshape(96, 128).T * (SCALE * grad_scale)
    return mixed, dx, down_grad, up_grad


def solution(mesh):
    fine = Mesh(mesh.devices.reshape(SIZES), AXES)
    dp, fsdp = ("yh", "x", "core"), ("z", "yl")
    every = dp + fsdp
    in_specs = (
        P(every, None),
        P(every, None),
        P(fsdp, None),
        P(fsdp),
        P(fsdp, None),
        P(None, fsdp),
        P(fsdp, None),
        P(),
    )
    out_specs = (P(every, None), P(every, None), P(fsdp, None), P(None, fsdp))
    return jax.shard_map(
        per_device, mesh=fine, in_specs=in_specs, out_specs=out_specs, check_vma=False
    )
```

time: 198 us -> 168 us (0.85)
  starting transfers between devices: 89 us -> 75.2 us
  blocking collectives: 0 us -> 11.1 us
  local copies, waits for them, and re-layouts: 21.7 us -> 11.4 us
  other arithmetic: 16.8 us -> 7.17 us
  Pallas kernels: 19.4 us -> 15.7 us
  matrix products: 3.26 us -> 0.18 us
    ppermute x3, waiting for transfers between devices: 0.01 us -> 14.5 us  [per_device(): lax.ppermute(line, AXES, plane_pairs(k, False))]
    all_to_all x0 -> x1, blocking collectives: none -> 11.1 us  [per_device(): terms = lax.all_to_all(terms, PLANE, 0, 0, tiled=True).astype(F32).sum(0)]
    ppermute x3, waiting for transfers between devices: 17.3 us -> 7.75 us  [per_device(): lax.ppermute(first, AXES, plane_pairs(k, True))]
    all_to_all x4 -> x2, starting transfers between devices: 34.7 us -> 26.4 us  [the longest x1 15.7 us: per_device(): lax.all_to_all(jnp.broadcast_to(pieces[None], (16, 114, 128)), 'z', 0, 0,...]
    all_to_all x4 -> x2, waiting for transfers between devices: 23.9 us -> 16.9 us  [the longest x1 16.9 us: per_device(): lax.all_to_all(jnp.broadcast_to(pieces[None], (16, 114, 128)), 'z', 0, 0,...]
    convert_element_type x4 -> x1, other arithmetic: 6.48 us -> 0.93 us  [per_device(): terms = (mine + other_core(yours)).astype(BF).reshape(16, 144, 128)]
    dynamic_slice x5 -> x1, local copies, waits for them, and re-layouts: 5.2 us -> 0.01 us  [per_device(): lax.dynamic_slice(gate_weight, (0, j * 384), (8, 384)).reshape(24, 128)]
    ppermute x7 -> x6, starting transfers between devices: 28.4 us -> 23.6 us  [other_core(): return lax.ppermute(v, 'core', [(0, 1), (1, 0)])]
  transfers between devices with their start and end apart: 18 -> 15, of which waited for: 5 -> 9; matrix products, arithmetic and copies ran while one was open for 16% -> 3% of each run, Pallas kernels for 10% -> 8%
where the time goes in v3:
time: 168 us; the launch traced here: 166 us
  starting transfers between devices  75.2 us (45%)
  waiting for transfers between devices  43.7 us (26%)
  Pallas kernels  15.7 us (9%)
  local copies, waits for them, and re-layouts  11.4 us (7%)
  blocking collectives  11.1 us (7%)
  other arithmetic  7.17 us (4%)
  between operations  1.83 us (1%)
    ppermute x6, starting transfers between devices, other_core(): return lax.ppermute(v, 'core', [(0, 1), (1, 0)])  23.6 us
    all_to_all x1, waiting for transfers between devices, per_device(): lax.all_to_all(jnp.broadcast_to(pieces[None], (16, 114, 128)), 'z', 0, 0,...  16.9 us
    all_to_all x1, starting transfers between devices, per_device(): lax.all_to_all(jnp.broadcast_to(pieces[None], (16, 114, 128)), 'z', 0, 0,...  15.7 us
    ppermute x3, waiting for transfers between devices, per_device(): lax.ppermute(line, AXES, plane_pairs(k, False))  14.5 us
    all_to_all x1, blocking collectives, per_device(): terms = lax.all_to_all(terms, PLANE, 0, 0, tiled=True).astype(F32).sum(0)  11.1 us
    all_to_all x1, starting transfers between devices, per_device(): lax.all_to_all(terms, 'z', 0, 0, tiled=True).astype(F32).sum(0).astype(BF)  10.6 us
    pallas_call x1, Pallas kernels, products(): pl.pallas_call(products_kernel, out_shape=(half, half, half, jax.ShapeDty...  10.3 us
    ppermute x3, starting transfers between devices, per_device(): lax.ppermute(line, AXES, plane_pairs(k, False))  9.49 us
  transfers between devices with their start and end apart: 15, of which 9 were waited for; matrix products, arithmetic and copies ran while one was open for 3% of the time, Pallas kernels for 8%

profile of v3, /device:TPU:1, one launch (start us, length us, event | category | flops | bytes accessed | tf_op | source)
XLA Modules:
  0.0 166.3 jit_solution(39488500432301498)
XLA Ops:
  4.7 15.7 %all-to-all-start = ((bf16[16,114,128]{2,1,0:T(8,128)(2,1)}), bf16[16,114,128]{2,1,0:T(8,128)(2,1)S(1)}, u32[]{:S(2)}, u32[]{:S(2)}) async-start(bf16[16,114,128]{2,1,0:T(8,128)(2,1)} %broadcast_in_dim.35), calls=%async_computation | async-start | bytes 983040 | tf_op jit(solution)/shard_map/all_to_all | solution.py:237
  20.5 2.9 %collective-permute-start = (bf16[256,1536]{1,0:T(8,128)(2,1)S(1)}, bf16[256,1536]{1,0:T(8,128)(2,1)S(1)}, u32[]{:S(2)}, u32[]{:S(2)}) collective-permute-start(bf16[256,1536]{1,0:T(8,128)(2,1)S(1)} %copy-done.2), channel_id=1, source_target_pairs={{0,32},{32,0},{1,33},{33,1},{2,34},{34,2},{3,35},{35,3},{4,36},{36... | collective-permute-start | bytes 2359304 | tf_op jit(solution)/shard_map/ppermute | solution.py:41
  24.0 1.2 collective-permute-done.rows_other
  25.3 16.9 %all-to-all-done = bf16[16,114,128]{2,1,0:T(8,128)(2,1)S(1)} async-done(((bf16[16,114,128]{2,1,0:T(8,128)(2,1)}), bf16[16,114,128]{2,1,0:T(8,128)(2,1)S(1)}, u32[]{:S(2)}, u32[]{:S(2)}) %all-to-all-start) | async-done | bytes 466976 | tf_op jit(solution)/shard_map/all_to_all | solution.py:237
  43.9 6.8 %all-to-all-start.1 = ((bf16[16,300,128]{2,1,0:T(8,128)(2,1)}), bf16[16,300,128]{2,1,0:T(8,128)(2,1)S(1)}, u32[]{:S(2)}, u32[]{:S(2)}) async-start(bf16[16,300,128]{2,1,0:T(8,128)(2,1)} %pad_maximum_fusion), calls=%async_computation.1 | async-start | bytes 2490368 | tf_op jit(solution)/shard_map/all_to_all | solution.py:261
  50.7 4.8 %collective-permute-start.2 = (bf16[16,24,384]{2,1,0:T(8,128)(2,1)S(1)}, bf16[16,24,384]{2,1,0:T(8,128)(2,1)S(1)}, u32[]{:S(2)}, u32[]{:S(2)}) collective-permute-start(bf16[16,24,384]{2,1,0:T(8,128)(2,1)S(1)} %get-tuple-element.61), channel_id=1, source_target_pairs={{0,128},{1,129},{2,130},{3,131},{4,132},{5,133},{6,134},{7,135},{8... | collective-permute-start | bytes 884744 | tf_op jit(solution)/shard_map/ppermute | solution.py:241
  55.5 2.2 %collective-permute-start.1 = (bf16[16,24,384]{2,1,0:T(8,128)(2,1)S(1)}, bf16[16,24,384]{2,1,0:T(8,128)(2,1)S(1)}, u32[]{:S(2)}, u32[]{:S(2)}) collective-permute-start(bf16[16,24,384]{2,1,0:T(8,128)(2,1)S(1)} %get-tuple-element.61), channel_id=1, source_target_pairs={{0,64},{1,65},{2,66},{3,67},{4,68},{5,69},{6,70},{7,71},{8,72},{9,... | collective-permute-start | bytes 884744 | tf_op jit(solution)/shard_map/ppermute | solution.py:241
  57.7 2.5 %collective-permute-start.3 = (bf16[16,24,384]{2,1,0:T(8,128)(2,1)S(1)}, bf16[16,24,384]{2,1,0:T(8,128)(2,1)S(1)}, u32[]{:S(2)}, u32[]{:S(2)}) collective-permute-start(bf16[16,24,384]{2,1,0:T(8,128)(2,1)S(1)} %get-tuple-element.61), channel_id=1, source_target_pairs={{0,192},{1,193},{2,194},{3,195},{4,196},{5,197},{6,198},{7,199},{8... | collective-permute-start | bytes 884744 | tf_op jit(solution)/shard_map/ppermute | solution.py:241
  60.2 7.7 %collective-permute-done.2 = bf16[16,24,384]{2,1,0:T(8,128)(2,1)S(1)} collective-permute-done((bf16[16,24,384]{2,1,0:T(8,128)(2,1)S(1)}, bf16[16,24,384]{2,1,0:T(8,128)(2,1)S(1)}, u32[]{:S(2)}, u32[]{:S(2)}) %collective-permute-start.2) | collective-permute-done | bytes 294944 | tf_op jit(solution)/shard_map/ppermute | solution.py:241
  68.0 6.6 %collective-permute-done.1 = bf16[16,24,384]{2,1,0:T(8,128)(2,1)S(1)} collective-permute-done((bf16[16,24,384]{2,1,0:T(8,128)(2,1)S(1)}, bf16[16,24,384]{2,1,0:T(8,128)(2,1)S(1)}, u32[]{:S(2)}, u32[]{:S(2)}) %collective-permute-start.1) | collective-permute-done | bytes 294944 | tf_op jit(solution)/shard_map/ppermute | solution.py:241
  74.7 1.2 pad_maximum_fusion.1.t0
  76.6 1.1 copy-done.3
  77.7 1.1 copy-done.6
  78.8 2.6 %adapter_terms.1 = (bf16[256,1536]{1,0:T(8,128)(2,1)S(1)}, bf16[256,1536]{1,0:T(8,128)(2,1)S(1)}, bf16[256,128]{1,0:T(8,128)(2,1)S(1)}, bf16[256,128]{1,0:T(8,12...) custom-call(s32[1]{0:T(128)} %bitcast.core, ...), custom_call_target="tpu_custom_call" | custom-call | flops 700000000 | bytes 12000000 | tf_op jit(solution)/shard_map/adapter_terms/pallas_call | solution.py:201
  81.5 3.7 %collective-permute-start.4 = (f32[32,72,128]{2,1,0:T(8,128)S(1)}, f32[32,72,128]{2,1,0:T(8,128)S(1)}, u32[]{:S(2)}, u32[]{:S(2)}) collective-permute-start(f32[32,72,128]{2,1,0:T(8,128)S(1)} %get-tuple-element.35), channel_id=1, source_target_pairs={{0,32},{32,0},{1,33},{33,1},{2,34},{34,2},{3,35},{35,3},{4,36},{36... | collective-permute-start | bytes 3538952 | tf_op jit(solution)/shard_map/ppermute | solution.py:41
  85.2 2.2 %collective-permute-start.5 = (bf16[4,16,24,384]{3,2,1,0:T(8,128)(2,1)}, bf16[4,16,24,384]{3,2,1,0:T(8,128)(2,1)S(1)}, u32[]{:S(2)}, u32[]{:S(2)}) collective-permute-start(bf16[4,16,24,384]{3,2,1,0:T(8,128)(2,1)} %pad_maximum_fusion.1.t0), channel_id=1, source_target_pairs={{0,1},{1,0},{2,3},{3,2},{4,5},{5,4},{6,7},{7,6},{8,9},{9,8},{10,11... | collective-permute-start | bytes 3538952 | tf_op jit(solution)/shard_map/ppermute | solution.py:263
  87.4 2.8 %collective-permute-start.7 = (bf16[4,16,24,384]{3,2,1,0:T(8,128)(2,1)}, bf16[4,16,24,384]{3,2,1,0:T(8,128)(2,1)}, u32[]{:S(2)}, u32[]{:S(2)}) collective-permute-start(bf16[4,16,24,384]{3,2,1,0:T(8,128)(2,1)} %pad_maximum_fusion.1.t0), channel_id=1, source_target_pairs={{0,257},{1,256},{2,259},{3,258},{4,261},{5,260},{6,263},{7,262},{8... | collective-permute-start | bytes 3538952 | tf_op jit(solution)/shard_map/ppermute | solution.py:263
  90.2 4.0 %collective-permute-start.6 = (bf16[4,16,24,384]{3,2,1,0:T(8,128)(2,1)}, bf16[4,16,24,384]{3,2,1,0:T(8,128)(2,1)}, u32[]{:S(2)}, u32[]{:S(2)}) collective-permute-start(bf16[4,16,24,384]{3,2,1,0:T(8,128)(2,1)} %pad_maximum_fusion.1.t0), channel_id=1, source_target_pairs={{0,256},{1,257},{2,258},{3,259},{4,260},{5,261},{6,262},{7,263},{8... | collective-permute-start | bytes 3538952 | tf_op jit(solution)/shard_map/ppermute | solution.py:263
  95.2 7.6 %collective-permute-done.5.t1 = bf16[4,16,24,384]{3,2,1,0:T(8,128)(2,1)S(1)} collective-permute-done((bf16[4,16,24,384]{3,2,1,0:T(8,128)(2,1)}, bf16[4,16,24,384]{3,2,1,0:T(8,128)(2,1)S(1)}, u32[]{:S(2)}, u32[]{:S(2)}) %collective-permute-start.5) | collective-permute-done | bytes 1179680 | tf_op jit(solution)/shard_map/ppermute | solution.py:263
  102.8 10.6 %all-to-all-start.2 = ((bf16[16,144,128]{2,1,0:T(8,128)(2,1)}), bf16[16,144,128]{2,1,0:T(8,128)(2,1)}, u32[]{:S(2)}, u32[]{:S(2)}) async-start(bf16[16,144,128]{2,1,0:T(8,128)(2,1)} %bitcast.33), calls=%async_computation.2 | async-start | bytes 1179648 | tf_op jit(solution)/shard_map/all_to_all | solution.py:273
  113.4 3.0 %collective-permute-start.8 = (bf16[256,1536]{1,0:T(8,128)(2,1)}, bf16[256,1536]{1,0:T(8,128)(2,1)}, u32[]{:S(2)}, u32[]{:S(2)}) collective-permute-start(bf16[256,1536]{1,0:T(8,128)(2,1)} %copy-done.14), channel_id=1, source_target_pairs={{0,32},{32,0},{1,33},{33,1},{2,34},{34,2},{3,35},{35,3},{4,36},{36... | collective-permute-start | bytes 2359304 | tf_op jit(solution)/shard_map/ppermute | solution.py:41
  116.7 2.0 %collective-permute-done.8.branch_other = bf16[256,1536]{1,0:T(8,128)(2,1)} collective-permute-done((bf16[256,1536]{1,0:T(8,128)(2,1)}, bf16[256,1536]{1,0:T(8,128)(2,1)}, u32[]{:S(2)}, u32[]{:S(2)}) %collective-permute-start.8) | collective-permute-done | bytes 786464 | tf_op jit(solution)/shard_map/ppermute | solution.py:41
  118.9 1.3 copy-done.11
  120.1 1.1 copy-done.13
  123.3 10.3 %products.1 = (bf16[256,1536]{1,0:T(8,128)(2,1)}, bf16[256,1536]{1,0:T(8,128)(2,1)}, bf16[256,1536]{1,0:T(8,128)(2,1)S(1)}, f32[256,1536]{1,0:T(8,128)S(1)}) custom-call(s32[32]{0:T(128)S(1)} %pad_add_fusion.at, bf16[4,16,24,384]{3,2,1,0:T(8,128)(2,1)} %pad_maximum_fusion.1.t0, bf16[4,16,24,384]{3,2,1,0:T(8,128)(2,1)S(1)} %copy-done.11, ...), custom_call_target="tpu_custom_call" | custom-call | flops 4831838208 | bytes 12000000 | tf_op jit(solution)/shard_map/products/pallas_call | solution.py:164
  134.5 4.1 %collective-permute-start.9 = (bf16[256,1536]{1,0:T(8,128)(2,1)}, bf16[256,1536]{1,0:T(8,128)(2,1)S(1)}, u32[]{:S(2)}, u32[]{:S(2)}) collective-permute-start(bf16[256,1536]{1,0:T(8,128)(2,1)} %get-tuple-element.47), channel_id=1, source_target_pairs={{0,32},{32,0},{1,33},{33,1},{2,34},{34,2},{3,35},{35,3},{4,36},{36... | collective-permute-start | bytes 2359304 | tf_op jit(solution)/shard_map/ppermute | solution.py:41
  138.6 1.9 %collective-permute-start.10 = (bf16[256,1536]{1,0:T(8,128)(2,1)}, bf16[256,1536]{1,0:T(8,128)(2,1)}, u32[]{:S(2)}, u32[]{:S(2)}) collective-permute-start(bf16[256,1536]{1,0:T(8,128)(2,1)} %get-tuple-element.48), channel_id=1, source_target_pairs={{0,32},{32,0},{1,33},{33,1},{2,34},{34,2},{3,35},{35,3},{4,36},{36... | collective-permute-start | bytes 2359304 | tf_op jit(solution)/shard_map/ppermute | solution.py:41
  140.5 1.2 reduce_sum.21
  141.7 1.4 collective-permute-done.10.mixed_rest
  143.1 11.1 %all_to_all.20 = bf16[16,72,128]{2,1,0:T(8,128)(2,1)S(1)} all-to-all(bf16[16,72,128]{2,1,0:T(8,128)(2,1)S(1)} %bitcast.34), channel_id=1, replica_groups=mesh['yh'=2,'x'=4,'core'=2,'z'=16,'yl'=2] {'yh','x','yl'}, dimensions={0} | all-to-all | bytes 589824 | tf_op jit(solution)/shard_map/all_to_all | solution.py:285
  154.3 8.0 %collective-permute-start.11 = (f32[72,128]{1,0:T(8,128)S(1)}, f32[72,128]{1,0:T(8,128)S(1)}, u32[]{:S(2)}, u32[]{:S(2)}) collective-permute-start(f32[72,128]{1,0:T(8,128)S(1)} %convert_reduce_fusion), channel_id=1, source_target_pairs={{0,32},{32,0},{1,33},{33,1},{2,34},{34,2},{3,35},{35,3},{4,36},{36... | collective-permute-start | bytes 110600 | tf_op jit(solution)/shard_map/ppermute | solution.py:41
  162.3 2.7 %finish.1 = (bf16[256,3072]{1,0:T(8,128)(2,1)}, bf16[256,1536]{1,0:T(8,128)(2,1)}) custom-call(s32[1]{0:T(128)} %bitcast.core, bf16[256,1536]{1,0:T(8,128)(2,1)S(1)} %copy-done.9, bf16[256,1536]{1,0:T(8,128)(2,1)} %collective-permute-done.10.mixed_rest, f32[256,1536]{1,0:T(8,128)S(1)} %get-tuple-element.51.dx_own, ...), custom_call_target="tpu_custom_call" | custom-call | flops 1000000 | bytes 7000000 | tf_op jit(solution)/shard_map/finish/pallas_call | solution.py:183
  (79 shorter events, 12.0 us)
Async XLA Ops:
  0.6 19.8 %copy-start.2 = (bf16[256,1536]{1,0:T(8,128)(2,1)S(1)}, bf16[256,1536]{1,0:T(8,128)(2,1)}, u32[]{:S(2)}) copy-start(bf16[256,1536]{1,0:T(8,128)(2,1)} %rows.3) | copy-start | bytes 2359300
  0.7 22.7 %copy-start.19 = (s32[32]{0:T(128)S(1)}, s32[32]{0:T(128)}, u32[]{:S(2)}) copy-start(s32[32]{0:T(128)} %param.15) | copy-start | bytes 388
  4.7 37.4 %all-to-all-start = ((bf16[16,114,128]{2,1,0:T(8,128)(2,1)}), bf16[16,114,128]{2,1,0:T(8,128)(2,1)S(1)}, u32[]{:S(2)}, u32[]{:S(2)}) async-start(bf16[16,114,128]{2,1,0:T(8,128)(2,1)} %broadcast_in_dim.35), calls=%async_computation | async-start | bytes 983040 | tf_op jit(solution)/shard_map/all_to_all | solution.py:237
  20.5 4.8 %collective-permute-start = (bf16[256,1536]{1,0:T(8,128)(2,1)S(1)}, bf16[256,1536]{1,0:T(8,128)(2,1)S(1)}, u32[]{:S(2)}, u32[]{:S(2)}) collective-permute-start(bf16[256,1536]{1,0:T(8,128)(2,1)S(1)} %copy-done.2), channel_id=1, source_target_pairs={{0,32},{32,0},{1,33},{33,1},{2,34},{34,2},{3,35},{35,3},{4,36},{36... | collective-permute-start | bytes 2359304 | tf_op jit(solution)/shard_map/ppermute | solution.py:41
  25.3 17.5 %copy-start.5 = (bf16[256,1536]{1,0:T(8,128)(2,1)}, bf16[256,1536]{1,0:T(8,128)(2,1)S(1)}, u32[]{:S(2)}) copy-start(bf16[256,1536]{1,0:T(8,128)(2,1)S(1)} %collective-permute-done.rows_other) | copy-start | bytes 2359300
  43.9 32.0 %all-to-all-start.1 = ((bf16[16,300,128]{2,1,0:T(8,128)(2,1)}), bf16[16,300,128]{2,1,0:T(8,128)(2,1)S(1)}, u32[]{:S(2)}, u32[]{:S(2)}) async-start(bf16[16,300,128]{2,1,0:T(8,128)(2,1)} %pad_maximum_fusion), calls=%async_computation.1 | async-start | bytes 2490368 | tf_op jit(solution)/shard_map/all_to_all | solution.py:261
  50.7 17.2 %collective-permute-start.2 = (bf16[16,24,384]{2,1,0:T(8,128)(2,1)S(1)}, bf16[16,24,384]{2,1,0:T(8,128)(2,1)S(1)}, u32[]{:S(2)}, u32[]{:S(2)}) collective-permute-start(bf16[16,24,384]{2,1,0:T(8,128)(2,1)S(1)} %get-tuple-element.61), channel_id=1, source_target_pairs={{0,128},{1,129},{2,130},{3,131},{4,132},{5,133},{6,134},{7,135},{8... | collective-permute-start | bytes 884744 | tf_op jit(solution)/shard_map/ppermute | solution.py:241
  55.5 19.1 %collective-permute-start.1 = (bf16[16,24,384]{2,1,0:T(8,128)(2,1)S(1)}, bf16[16,24,384]{2,1,0:T(8,128)(2,1)S(1)}, u32[]{:S(2)}, u32[]{:S(2)}) collective-permute-start(bf16[16,24,384]{2,1,0:T(8,128)(2,1)S(1)} %get-tuple-element.61), channel_id=1, source_target_pairs={{0,64},{1,65},{2,66},{3,67},{4,68},{5,69},{6,70},{7,71},{8,72},{9,... | collective-permute-start | bytes 884744 | tf_op jit(solution)/shard_map/ppermute | solution.py:241
  57.7 17.0 %collective-permute-start.3 = (bf16[16,24,384]{2,1,0:T(8,128)(2,1)S(1)}, bf16[16,24,384]{2,1,0:T(8,128)(2,1)S(1)}, u32[]{:S(2)}, u32[]{:S(2)}) collective-permute-start(bf16[16,24,384]{2,1,0:T(8,128)(2,1)S(1)} %get-tuple-element.61), channel_id=1, source_target_pairs={{0,192},{1,193},{2,194},{3,195},{4,196},{5,197},{6,198},{7,199},{8... | collective-permute-start | bytes 884744 | tf_op jit(solution)/shard_map/ppermute | solution.py:241
  74.7 1.8 %copy-start.1 = (bf16[256,3072]{1,0:T(8,128)(2,1)S(1)}, bf16[256,3072]{1,0:T(8,128)(2,1)}, u32[]{:S(2)}) copy-start(bf16[256,3072]{1,0:T(8,128)(2,1)} %cot.1) | copy-start | bytes 4718596
  76.6 1.1 copy-start.3
  77.7 1.1 copy-start.6
  81.5 13.7 %copy-start.12 = (bf16[256,1536]{1,0:T(8,128)(2,1)}, bf16[256,1536]{1,0:T(8,128)(2,1)S(1)}, u32[]{:S(2)}) copy-start(bf16[256,1536]{1,0:T(8,128)(2,1)S(1)} %get-tuple-element.40.branch) | copy-start | bytes 2359300
  81.5 13.7 %copy-start.15 = (bf16[1536,128]{1,0:T(8,128)(2,1)}, bf16[1536,128]{1,0:T(8,128)(2,1)S(1)}, u32[]{:S(2)}) copy-start(bf16[1536,128]{1,0:T(8,128)(2,1)S(1)} %get-tuple-element.45.down) | copy-start | bytes 1179652
  81.5 13.7 %copy-start.17 = (bf16[1536,128]{1,0:T(8,128)(2,1)}, bf16[1536,128]{1,0:T(8,128)(2,1)S(1)}, u32[]{:S(2)}) copy-start(bf16[1536,128]{1,0:T(8,128)(2,1)S(1)} %get-tuple-element.44.up) | copy-start | bytes 1179652
  81.5 21.3 %copy-start.14 = (bf16[256,1536]{1,0:T(8,128)(2,1)}, bf16[256,1536]{1,0:T(8,128)(2,1)S(1)}, u32[]{:S(2)}) copy-start(bf16[256,1536]{1,0:T(8,128)(2,1)S(1)} %get-tuple-element.37) | copy-start | bytes 2359300
  81.5 12.7 %collective-permute-start.4 = (f32[32,72,128]{2,1,0:T(8,128)S(1)}, f32[32,72,128]{2,1,0:T(8,128)S(1)}, u32[]{:S(2)}, u32[]{:S(2)}) collective-permute-start(f32[32,72,128]{2,1,0:T(8,128)S(1)} %get-tuple-element.35), channel_id=1, source_target_pairs={{0,32},{32,0},{1,33},{33,1},{2,34},{34,2},{3,35},{35,3},{4,36},{36... | collective-permute-start | bytes 3538952 | tf_op jit(solution)/shard_map/ppermute | solution.py:41
  85.2 17.6 %collective-permute-start.5 = (bf16[4,16,24,384]{3,2,1,0:T(8,128)(2,1)}, bf16[4,16,24,384]{3,2,1,0:T(8,128)(2,1)S(1)}, u32[]{:S(2)}, u32[]{:S(2)}) collective-permute-start(bf16[4,16,24,384]{3,2,1,0:T(8,128)(2,1)} %pad_maximum_fusion.1.t0), channel_id=1, source_target_pairs={{0,1},{1,0},{2,3},{3,2},{4,5},{5,4},{6,7},{7,6},{8,9},{9,8},{10,11... | collective-permute-start | bytes 3538952 | tf_op jit(solution)/shard_map/ppermute | solution.py:263
  87.4 31.4 %collective-permute-start.7 = (bf16[4,16,24,384]{3,2,1,0:T(8,128)(2,1)}, bf16[4,16,24,384]{3,2,1,0:T(8,128)(2,1)}, u32[]{:S(2)}, u32[]{:S(2)}) collective-permute-start(bf16[4,16,24,384]{3,2,1,0:T(8,128)(2,1)} %pad_maximum_fusion.1.t0), channel_id=1, source_target_pairs={{0,257},{1,256},{2,259},{3,258},{4,261},{5,260},{6,263},{7,262},{8... | collective-permute-start | bytes 3538952 | tf_op jit(solution)/shard_map/ppermute | solution.py:263
  90.2 28.6 %collective-permute-start.6 = (bf16[4,16,24,384]{3,2,1,0:T(8,128)(2,1)}, bf16[4,16,24,384]{3,2,1,0:T(8,128)(2,1)}, u32[]{:S(2)}, u32[]{:S(2)}) collective-permute-start(bf16[4,16,24,384]{3,2,1,0:T(8,128)(2,1)} %pad_maximum_fusion.1.t0), channel_id=1, source_target_pairs={{0,256},{1,257},{2,258},{3,259},{4,260},{5,261},{6,262},{7,263},{8... | collective-permute-start | bytes 3538952 | tf_op jit(solution)/shard_map/ppermute | solution.py:263
  94.2 24.6 %copy-start.7 = (bf16[256,1536]{1,0:T(8,128)(2,1)S(1)}, bf16[256,1536]{1,0:T(8,128)(2,1)}, u32[]{:S(2)}) copy-start(bf16[256,1536]{1,0:T(8,128)(2,1)} %copy-done.5) | copy-start | bytes 2359300
  95.2 23.7 %copy-start.4 = (bf16[256,1536]{1,0:T(8,128)(2,1)S(1)}, bf16[256,1536]{1,0:T(8,128)(2,1)}, u32[]{:S(2)}) copy-start(bf16[256,1536]{1,0:T(8,128)(2,1)} %rows.3) | copy-start | bytes 2359300
  102.8 16.0 %copy-start.10 = (bf16[4,16,24,384]{3,2,1,0:T(8,128)(2,1)}, bf16[4,16,24,384]{3,2,1,0:T(8,128)(2,1)S(1)}, u32[]{:S(2)}) copy-start(bf16[4,16,24,384]{3,2,1,0:T(8,128)(2,1)S(1)} %collective-permute-done.5.t1) | copy-start | bytes 3538948
  102.8 37.7 %all-to-all-start.2 = ((bf16[16,144,128]{2,1,0:T(8,128)(2,1)}), bf16[16,144,128]{2,1,0:T(8,128)(2,1)}, u32[]{:S(2)}, u32[]{:S(2)}) async-start(bf16[16,144,128]{2,1,0:T(8,128)(2,1)} %bitcast.33), calls=%async_computation.2 | async-start | bytes 1179648 | tf_op jit(solution)/shard_map/all_to_all | solution.py:273
  113.4 5.2 %collective-permute-start.8 = (bf16[256,1536]{1,0:T(8,128)(2,1)}, bf16[256,1536]{1,0:T(8,128)(2,1)}, u32[]{:S(2)}, u32[]{:S(2)}) collective-permute-start(bf16[256,1536]{1,0:T(8,128)(2,1)} %copy-done.14), channel_id=1, source_target_pairs={{0,32},{32,0},{1,33},{33,1},{2,34},{34,2},{3,35},{35,3},{4,36},{36... | collective-permute-start | bytes 2359304 | tf_op jit(solution)/shard_map/ppermute | solution.py:41
  118.9 1.3 copy-start.11
  120.1 1.1 copy-start.13
  121.3 1.0 copy-start.16
  134.5 27.8 %copy-start.9 = (bf16[256,1536]{1,0:T(8,128)(2,1)S(1)}, bf16[256,1536]{1,0:T(8,128)(2,1)}, u32[]{:S(2)}) copy-start(bf16[256,1536]{1,0:T(8,128)(2,1)} %copy-done.8) | copy-start | bytes 2359300
  134.5 7.2 %collective-permute-start.9 = (bf16[256,1536]{1,0:T(8,128)(2,1)}, bf16[256,1536]{1,0:T(8,128)(2,1)S(1)}, u32[]{:S(2)}, u32[]{:S(2)}) collective-permute-start(bf16[256,1536]{1,0:T(8,128)(2,1)} %get-tuple-element.47), channel_id=1, source_target_pairs={{0,32},{32,0},{1,33},{33,1},{2,34},{34,2},{3,35},{35,3},{4,36},{36... | collective-permute-start | bytes 2359304 | tf_op jit(solution)/shard_map/ppermute | solution.py:41
  138.6 4.5 %collective-permute-start.10 = (bf16[256,1536]{1,0:T(8,128)(2,1)}, bf16[256,1536]{1,0:T(8,128)(2,1)}, u32[]{:S(2)}, u32[]{:S(2)}) collective-permute-start(bf16[256,1536]{1,0:T(8,128)(2,1)} %get-tuple-element.48), channel_id=1, source_target_pairs={{0,32},{32,0},{1,33},{33,1},{2,34},{34,2},{3,35},{35,3},{4,36},{36... | collective-permute-start | bytes 2359304 | tf_op jit(solution)/shard_map/ppermute | solution.py:41
  154.3 10.8 %collective-permute-start.11 = (f32[72,128]{1,0:T(8,128)S(1)}, f32[72,128]{1,0:T(8,128)S(1)}, u32[]{:S(2)}, u32[]{:S(2)}) collective-permute-start(f32[72,128]{1,0:T(8,128)S(1)} %convert_reduce_fusion), channel_id=1, source_target_pairs={{0,32},{32,0},{1,33},{33,1},{2,34},{34,2},{3,35},{35,3},{4,36},{36... | collective-permute-start | bytes 110600 | tf_op jit(solution)/shard_map/ppermute | solution.py:41
  (3 other events, 2.7 us)

commit v4 on v3

v4 whole, which is shorter than its diff:
```python
import math

import jax
import jax.numpy as jnp
from jax import lax
from jax.experimental import pallas as pl
from jax.experimental.pallas import tpu as pltpu
from jax.sharding import Mesh
from jax.sharding import PartitionSpec as P

FREQ = 256
SCALE = 0.5
AXES = ("yh", "x", "core", "z", "yl")
SIZES = (2, 4, 2, 16, 2)
PLANE = ("yh", "x", "yl")
BF = jnp.bfloat16
F32 = jnp.float32


def index_of(yh, x, c, z, yl):
    return (((yh * 4 + x) * 2 + c) * 16 + z) * 2 + yl


def plane_pairs(k, swap):
    pairs = []
    for yh in range(2):
        for x in range(4):
            for c in range(2):
                for z in range(16):
                    for yl in range(2):
                        tx, ty = x, yh * 2 + yl
                        if (c == 0) != swap:
                            tx ^= k
                        else:
                            ty ^= k
                        pairs.append((index_of(yh, x, c, z, yl), index_of(ty >> 1, tx, c, z, ty & 1)))
    return pairs


def other_core(v):
    return lax.ppermute(v, "core", [(0, 1), (1, 0)])


def nt(a, b):
    return lax.dot_general(a, b, (((1,), (1,)), ((), ())), preferred_element_type=F32)


def nn(a, b):
    return jnp.dot(a, b, preferred_element_type=F32)


STRIPS = [slice(i, i + 256) for i in range(0, 1536, 256)]


def fetch(pairs, sems):
    copies = [pltpu.make_async_copy(a, b, sems.at[i]) for i, (a, b) in enumerate(pairs)]
    for copy in copies:
        copy.start()
    return copies


def products_kernel(
    at, core, low_other, gate_other, low, gate, low_grad,
    up_hbm, down_hbm, t0, t1, t2, t3, rows_hbm, rows_other_hbm, cot_hbm, cot_other_hbm,
    mixed_other_hbm, dx_other_hbm, mixed_hbm, dx_hbm,
    blocks, wm, rows, rows_other, cot, cot_other, branch, branch_other, up, down,
    mixed_other, dx_other, mixed, dx, sems,
):
    pairs = []
    for k2, t in enumerate((t0, t1, t2, t3)):
        for k1 in range(4):
            b = k2 * 4 + k1
            col = pl.multiple_of(at[b] * 384, 128)
            pairs.append((t.at[k1], blocks.at[:, at[16 + b], :, pl.ds(col, 384)]))
    half = pl.ds(pl.multiple_of(core[0] * 1536, 128), 1536)
    pairs.append((cot_other_hbm.at[:, half], cot_other))
    pairs.append((cot_hbm.at[:, half], cot))
    pairs.append((down_hbm, down))
    pairs.append((rows_other_hbm, rows_other))
    pairs.append((rows_hbm, rows))
    pairs.append((up_hbm, up))
    copies = fetch(pairs, sems)
    for copy in copies[:19]:
        copy.wait()
    branch_other[...] = (cot_other[...].astype(F32) * gate_other[...]).astype(BF)
    branch[...] = (cot[...].astype(F32) * gate[...]).astype(BF)

    def pack(z, carry):
        part = blocks[z].astype(F32).reshape(96, 1536).astype(BF)
        wm[pl.ds(pl.multiple_of(z * 96, 96), 96), :] = part
        return carry

    lax.fori_loop(0, 16, pack, 0)
    for s in STRIPS:
        dx_other[:, s] = nt(branch_other[...], wm[s, :]).astype(BF)
    out = fetch([(dx_other, dx_other_hbm)], sems.at[pl.ds(22, 1)])
    for copy in copies[19:]:
        copy.wait()
    for s in STRIPS:
        p = nn(rows_other[...], wm[:, s]) + SCALE * nt(low_other[...], up[s, :])
        mixed_other[:, s] = (p * gate_other[:, s]).astype(BF)
    out += fetch([(mixed_other, mixed_other_hbm)], sems.at[pl.ds(23, 1)])
    for s in STRIPS:
        dx[:, s] = nt(branch[...], wm[s, :]) + nt(low_grad[...], down[s, :])
    out += fetch([(dx, dx_hbm)], sems.at[pl.ds(24, 1)])
    for s in STRIPS:
        p = nn(rows[...], wm[:, s]) + SCALE * nt(low[...], up[s, :])
        mixed[:, s] = (p * gate[:, s]).astype(BF)
    out += fetch([(mixed, mixed_hbm.at[:, half])], sems.at[pl.ds(25, 1)])
    for copy in out:
        copy.wait()


def finish_kernel(
    core, mixed_in, mixed_rest_hbm, dx_own_hbm, dx_rest_hbm, mixed_hbm, dx_hbm,
    mixed_rest, dx_own, dx_rest, dx, sems,
):
    rest = pl.ds(pl.multiple_of(1536 - core[0] * 1536, 128), 1536)
    pairs = [(mixed_rest_hbm, mixed_rest), (dx_rest_hbm, dx_rest), (dx_own_hbm, dx_own)]
    copies = fetch(pairs, sems.at[pl.ds(0, 3)])
    copies[0].wait()
    out = fetch([(mixed_rest, mixed_hbm.at[:, rest])], sems.at[pl.ds(3, 1)])
    copies[1].wait()
    copies[2].wait()
    dx[...] = (dx_own[...] + dx_rest[...].astype(F32)).astype(BF)
    out += fetch([(dx, dx_hbm)], sems.at[pl.ds(4, 1)])
    for copy in out:
        copy.wait()


def vmem(n):
    return [pl.BlockSpec(memory_space=pltpu.VMEM)] * n


def adapter_kernel(
    core, got_hbm, rows_hbm, rows_other_hbm, cot_hbm, cot_other_hbm,
    low, low_other, low_grad, gate_own, gate_other, down_hbm, up_hbm, terms_hbm,
    wide, down_wide, up_wide, down, up, gates, branch, td, tu, kept, terms,
    rows, rows_other, cot, cot_other, got, sems,
):
    load = fetch([(got_hbm, got)], sems.at[pl.ds(7, 1)])
    copies = fetch(
        [(rows_hbm, rows), (rows_other_hbm, rows_other), (cot_hbm, cot), (cot_other_hbm, cot_other)],
        sems.at[pl.ds(0, 4)],
    )
    load[0].wait()
    for s in range(16):
        wide[s] = got[s].astype(F32)
        j, yl = s // 2, s % 2
        for z in range(16):
            a, b = 96 * z + 48 * yl + 6 * j, 192 * z + 96 * yl + 12 * j
            down_wide[a : a + 6] = wide[s, 18 * z : 18 * z + 6]
            up_wide[b : b + 12] = wide[s, 18 * z + 6 : 18 * z + 18]
    for j in range(8):
        part = wide[2 * j, 288:300] + wide[2 * j + 1, 288:300]
        part = part[:6] + part[6:]
        for r in range(6):
            at = 384 * j + 128 * (r % 3)
            gates[r // 3 : r // 3 + 1, at : at + 128] = part[r : r + 1]
    down[...] = down_wide[...].astype(BF)
    up[...] = up_wide[...].astype(BF)
    at = pl.multiple_of(core[0] * 1536, 128)
    out = fetch([(down, down_hbm), (up.at[pl.ds(at, 1536)], up_hbm)], sems.at[pl.ds(4, 2)])
    first = core[0] == 0
    gate = jnp.where(first, gates[0:1], gates[1:2])
    gate_own[...] = jnp.where(first, gates[0:1, :1536], gates[1:2, 1536:])
    gate_other[...] = jnp.where(first, gates[1:2, :1536], gates[0:1, 1536:])

    copies[0].wait()
    low[...] = nn(rows[...], down[...]).astype(BF)
    copies[1].wait()
    low_other[...] = nn(rows_other[...], down[...]).astype(BF)
    copies[2].wait()
    branch[:256] = (cot[...].astype(F32) * gate).astype(BF)
    b0 = (SCALE * nn(branch[:256], up[...])).astype(BF)
    low_grad[...] = b0
    copies[3].wait()
    branch[256:] = (cot_other[...].astype(F32) * jnp.where(first, gates[1:2], gates[0:1])).astype(BF)
    b1 = (SCALE * nn(branch[256:], up[...])).astype(BF)
    b0 = b0.astype(F32).T.astype(BF)
    b1 = b1.astype(F32).T.astype(BF)
    a0 = low[...].astype(F32).T.astype(BF)
    a1 = low_other[...].astype(F32).T.astype(BF)
    for i in range(0, 1536, 384):
        s = slice(i, i + 384)
        td[s, :] = (nn(b0, rows[:, s]) + nn(b1, rows_other[:, s])).T
    for i in range(0, 3072, 384):
        s = slice(i, i + 384)
        tu[s, :] = (nn(a0, branch[:256, s]) + nn(a1, branch[256:, s])).T

    def put(h):
        kept[:, :24] = td[...].reshape(32, 2, 24, 128)[:, h]
        kept[:, 24:] = tu[...].reshape(32, 2, 48, 128)[:, h]

    @pl.when(first)
    def _():
        put(0)

    @pl.when(jnp.logical_not(first))
    def _():
        put(1)

    terms[...] = kept[...].reshape(16, 144, 128).astype(BF)
    out += fetch([(terms, terms_hbm)], sems.at[pl.ds(6, 1)])
    for copy in out:
        copy.wait()


PARAMS = pltpu.CompilerParams(vmem_limit_bytes=60 * 1024 * 1024)
HALF = 256 * 1536 * 1536 * 2


def hbm(n):
    return [pl.BlockSpec(memory_space=pltpu.HBM)] * n


def products(at, core, *args):
    half = jax.ShapeDtypeStruct((256, 1536), BF)
    return pl.pallas_call(
        products_kernel,
        out_shape=(
            half,
            half,
            jax.ShapeDtypeStruct((256, 3072), BF),
            jax.ShapeDtypeStruct((256, 1536), F32),
        ),
        in_specs=[pl.BlockSpec(memory_space=pltpu.SMEM)] * 2 + vmem(5) + hbm(10),
        out_specs=tuple(hbm(4)),
        scratch_shapes=[
            pltpu.VMEM((16, 4, 24, 1536), BF),
            pltpu.VMEM((1536, 1536), BF),
            *[pltpu.VMEM((256, 1536), BF)] * 6,
            *[pltpu.VMEM((1536, 128), BF)] * 2,
            *[pltpu.VMEM((256, 1536), BF)] * 3,
            pltpu.VMEM((256, 1536), F32),
            pltpu.SemaphoreType.DMA((26,)),
        ],
        compiler_params=PARAMS,
        cost_estimate=pl.CostEstimate(flops=4 * HALF, bytes_accessed=200000000, transcendentals=0),
        name="products",
    )(at, core.reshape(1), *args)


def finish(core, *args):
    return pl.pallas_call(
        finish_kernel,
        out_shape=(jax.ShapeDtypeStruct((256, 3072), BF), jax.ShapeDtypeStruct((256, 1536), BF)),
        in_specs=[pl.BlockSpec(memory_space=pltpu.SMEM)] + hbm(4),
        out_specs=tuple(hbm(2)),
        input_output_aliases={1: 0},
        scratch_shapes=[
            pltpu.VMEM((256, 1536), BF),
            pltpu.VMEM((256, 1536), F32),
            *[pltpu.VMEM((256, 1536), BF)] * 2,
            pltpu.SemaphoreType.DMA((5,)),
        ],
        compiler_params=PARAMS,
        cost_estimate=pl.CostEstimate(flops=1000000, bytes_accessed=7000000, transcendentals=0),
        name="finish",
    )(core.reshape(1), *args)


def adapter_terms(core, *args):
    def out(*shape):
        return jax.ShapeDtypeStruct(shape, BF)

    thin, row = out(256, 128), jax.ShapeDtypeStruct((1, 1536), F32)
    tall = out(1536, 128)
    return pl.pallas_call(
        adapter_kernel,
        out_shape=(thin, thin, thin, row, row, tall, tall, out(16, 144, 128)),
        in_specs=[pl.BlockSpec(memory_space=pltpu.SMEM)] + hbm(5),
        out_specs=tuple(vmem(5) + hbm(3)),
        scratch_shapes=[
            pltpu.VMEM((16, 300, 128), F32),
            pltpu.VMEM((1536, 128), F32),
            pltpu.VMEM((3072, 128), F32),
            pltpu.VMEM((1536, 128), BF),
            pltpu.VMEM((3072, 128), BF),
            pltpu.VMEM((2, 3072), F32),
            pltpu.VMEM((512, 3072), BF),
            pltpu.VMEM((1536, 128), F32),
            pltpu.VMEM((3072, 128), F32),
            pltpu.VMEM((32, 72, 128), F32),
            pltpu.VMEM((16, 144, 128), BF),
            *[pltpu.VMEM((256, 1536), BF)] * 2,
            *[pltpu.VMEM((256, 3072), BF)] * 2,
            pltpu.VMEM((16, 300, 128), BF),
            pltpu.SemaphoreType.DMA((8,)),
        ],
        compiler_params=PARAMS,
        cost_estimate=pl.CostEstimate(flops=1400000000, bytes_accessed=200000000, transcendentals=0),
        name="adapter_terms",
    )(core.reshape(1), *args)


def pieces_kernel(at, codes, amax, down, up, gate, out, wide):
    core, xi, yh = at[0], at[1], at[2]
    j = yh * 4 + xi
    col = pl.multiple_of(core * 1536 + xi * 384, 128)
    weight = codes[:, pl.ds(col, 384)].astype(F32) * amax[...].astype(F32)
    weight = jnp.where(yh == 0, weight[:24], weight[24:]).astype(BF).astype(F32)
    gates = gate[:, pl.ds(pl.multiple_of(j * 384, 128), 384)].astype(F32)
    for k in range(3):
        lanes = slice(128 * k, 128 * k + 128)
        wide[24 * k : 24 * k + 24] = weight[:, lanes]
        wide[72 + 8 * k : 80 + 8 * k] = gates[:, lanes]

    def pick(n, size):
        row = lax.broadcasted_iota(jnp.int32, (n, size), 0)
        col = lax.broadcasted_iota(jnp.int32, (n, size), 1)
        return jnp.where(col == row + n * j, 1.0, 0.0).astype(BF)

    wide[96:102] = nn(pick(6, 48), down[...])
    wide[102:114] = nn(pick(12, 96), up[...])
    for d in range(16):
        out[d] = wide[...].astype(BF)


def pieces(at, codes, amax, down, up, gate):
    return pl.pallas_call(
        pieces_kernel,
        out_shape=jax.ShapeDtypeStruct((16, 114, 128), BF),
        in_specs=[pl.BlockSpec(memory_space=pltpu.SMEM)] + vmem(5),
        out_specs=vmem(1)[0],
        scratch_shapes=[pltpu.VMEM((114, 128), F32)],
        compiler_params=PARAMS,
        name="pieces",
    )(at, codes, amax, down, up, gate)


def spread_kernel(line, features, out_hbm, weight_hbm, wide, maps, pair, out, weight, sems):
    for k in range(3):
        weight[:, :, 128 * k : 128 * k + 128] = line[:, 24 * k : 24 * k + 24]
    copies = fetch([(weight, weight_hbm)], sems.at[pl.ds(0, 1)])
    wide[...] = line[...].astype(F32)
    for z in range(16):
        maps[18 * z : 18 * z + 18] = wide[z, 96:114]
    for k in range(3):
        block = wide[:, 72 + 8 * k : 80 + 8 * k].reshape(128, 128).astype(BF)
        part = nn(features[...], block)
        high = part.astype(BF).astype(F32)
        for h, v in enumerate((high, part - high)):
            for c in range(2):
                for j in range(8):
                    r = 6 * h + 3 * c + k
                    row = v[2 * j + c : 2 * j + c + 1]
                    pair[2 * j, r : r + 1] = row
                    pair[2 * j + 1, r : r + 1] = row
    for d in range(16):
        out[d, :288] = maps[...].astype(BF)
        out[d, 288:] = pair[d].astype(BF)
    copies += fetch([(out, out_hbm)], sems.at[pl.ds(1, 1)])
    for copy in copies:
        copy.wait()


def spread(line, features):
    shapes = ((16, 114, 128), (16, 300, 128), (16, 24, 384))
    return pl.pallas_call(
        spread_kernel,
        out_shape=tuple(jax.ShapeDtypeStruct(s, BF) for s in shapes[1:]),
        in_specs=vmem(2),
        out_specs=tuple(hbm(2)),
        scratch_shapes=[
            pltpu.VMEM(shapes[0], F32),
            pltpu.VMEM((288, 128), F32),
            pltpu.VMEM((16, 12, 128), F32),
            pltpu.VMEM(shapes[1], BF),
            pltpu.VMEM(shapes[2], BF),
            pltpu.SemaphoreType.DMA((2,)),
        ],
        compiler_params=pltpu.CompilerParams(vmem_limit_bytes=14 * 1024 * 1024),
        cost_estimate=pl.CostEstimate(flops=20000000, bytes_accessed=2000000, transcendentals=0),
        name="spread",
    )(line, features)


def per_device(rows, cotangent, codes, amax, down, up, gate_weight, timesteps):
    yh, xi, core, z, yl = (lax.axis_index(a) for a in AXES)
    j = yh * 4 + xi
    y = yh * 2 + yl

    place = jnp.stack([core, xi, yh]).astype(jnp.int32)
    line = pieces(place, codes, amax.reshape(1, 1), down, up.T, gate_weight)
    line = lax.all_to_all(line, "z", 0, 0, tiled=True)
    line, rows_other, cot_other = lax.optimization_barrier(
        (line, other_core(rows), other_core(cotangent))
    )
    k1 = jnp.tile(jnp.arange(4), 4)
    k2 = jnp.repeat(jnp.arange(4), 4)
    bx = xi ^ jnp.where(core == 0, k1, k2)
    by = y ^ jnp.where(core == 0, k2, k1)
    at = jnp.concatenate([bx, (by & 1) * 2 + (by >> 1)]).astype(jnp.int32)

    half_freq = FREQ // 2
    frequency = jnp.exp(-math.log(10000.0) * jnp.arange(half_freq, dtype=F32) / half_freq)
    steps = lax.dynamic_slice(timesteps.reshape(16, 2), (0, z // 8), (16, 1))
    phase = steps.astype(F32) * frequency[None, :]
    features = jnp.concatenate([jnp.cos(phase), jnp.sin(phase)], axis=1).astype(BF)
    features = lax.dynamic_slice(features.reshape(16, 16, 2, 8), (0, 0, yl, 0), (16, 16, 1, 8))
    spread_out, line = spread(line, features.reshape(16, 128))
    got = lax.all_to_all(spread_out, PLANE, 0, 0, tiled=True)
    first = [line] + [lax.ppermute(line, AXES, plane_pairs(k, False)) for k in (1, 2, 3)]
    got, first = lax.optimization_barrier((got, first))
    first = jnp.stack(first)
    second = [first] + [lax.ppermute(first, AXES, plane_pairs(k, True)) for k in (2, 1, 3)]
    second = [second[0], second[2], second[1], second[3]]

    low, low_other, low_grad, gate_own, gate_other, down_all, up_half, terms = adapter_terms(
        core, got, rows, rows_other, cotangent, cot_other
    )
    terms = lax.all_to_all(terms, "z", 0, 0, tiled=True)
    terms = terms.astype(F32).sum(0).astype(BF)

    mixed_other, dx_other, mixed_own, dx_own = products(
        at, core, low_other, gate_other, low, gate_own, low_grad,
        up_half, down_all, *second, rows, rows_other, cotangent, cot_other,
    )
    dx_rest = other_core(dx_other)
    mixed_rest = other_core(mixed_other)
    mixed, dx = finish(core, mixed_own, mixed_rest, dx_own, dx_rest)
    mixed, dx, terms = lax.optimization_barrier((mixed, dx, terms))
    terms = jnp.broadcast_to(terms.reshape(1, 2, 72, 128), (8, 2, 72, 128)).reshape(16, 72, 128)
    terms = lax.all_to_all(terms, PLANE, 0, 0, tiled=True).astype(F32).sum(0)
    rest = other_core(terms)
    terms = jnp.stack([jnp.where(core == 0, terms, rest), jnp.where(core == 0, rest, terms)])
    grad_scale = 131072**-0.5
    down_grad = terms[:, :24].reshape(48, 128) * grad_scale
    up_grad = terms[:, 24:].reshape(96, 128).T * (SCALE * grad_scale)
    return mixed, dx, down_grad, up_grad


def solution(mesh):
    fine = Mesh(mesh.devices.reshape(SIZES), AXES)
    dp, fsdp = ("yh", "x", "core"), ("z", "yl")
    every = dp + fsdp
    in_specs = (
        P(every, None),
        P(every, None),
        P(fsdp, None),
        P(fsdp),
        P(fsdp, None),
        P(None, fsdp),
        P(fsdp, None),
        P(),
    )
    out_specs = (P(every, None), P(every, None), P(fsdp, None), P(None, fsdp))
    return jax.shard_map(
        per_device, mesh=fine, in_specs=in_specs, out_specs=out_specs, check_vma=False
    )
```

time: 168 us -> 153 us (0.911)
  local copies, waits for them, and re-layouts: 11.4 us -> 1.28 us
  starting transfers between devices: 75.2 us -> 66.2 us
  Pallas kernels: 15.7 us -> 24.4 us
  other arithmetic: 7.17 us -> 4.52 us
  waiting for transfers between devices: 43.7 us -> 42 us
    ppermute x6 -> x5, starting transfers between devices: 23.6 us -> 14.8 us  [other_core(): return lax.ppermute(v, 'core', [(0, 1), (1, 0)])]
    pallas_call x2 -> x4, Pallas kernels: 13 us -> 21.4 us  [the longest x1 11.6 us: products(): pl.pallas_call(products_kernel, out_shape=(half, half, jax.ShapeDtypeStru...]
    unnamed x40 -> x16, local copies, waits for them, and re-layouts: 8.21 us -> 0.94 us
    all_to_all x3, waiting for transfers between devices: 16.9 us -> 14.4 us  [the longest x1 14.4 us: per_device(): line = lax.all_to_all(line, 'z', 0, 0, tiled=True)]
    ppermute x3, waiting for transfers between devices: 14.5 us -> 16.2 us  [per_device(): lax.ppermute(line, AXES, plane_pairs(k, False))]
    ppermute x6 -> x5, waiting for transfers between devices: 4.63 us -> 5.03 us  [other_core(): return lax.ppermute(v, 'core', [(0, 1), (1, 0)])]
  transfers between devices with their start and end apart: 15 -> 14, of which waited for: 9 -> 10; matrix products, arithmetic and copies ran while one was open for 3% -> 1% of each run, Pallas kernels for 8% -> 14%
where the time goes in v4:
time: 153 us; the launch traced here: 152 us
  starting transfers between devices  66.2 us (43%)
  waiting for transfers between devices  42 us (27%)
  Pallas kernels  24.4 us (16%)
  blocking collectives  12.4 us (8%)
  other arithmetic  4.52 us (3%)
  between operations  1.71 us (1%)
    ppermute x3, waiting for transfers between devices, per_device(): lax.ppermute(line, AXES, plane_pairs(k, False))  16.2 us
    all_to_all x1, starting transfers between devices, per_device(): line = lax.all_to_all(line, 'z', 0, 0, tiled=True)  15.7 us
    ppermute x5, starting transfers between devices, other_core(): return lax.ppermute(v, 'core', [(0, 1), (1, 0)])  14.8 us
    all_to_all x1, waiting for transfers between devices, per_device(): line = lax.all_to_all(line, 'z', 0, 0, tiled=True)  14.4 us
    all_to_all x1, blocking collectives, per_device(): terms = lax.all_to_all(terms, PLANE, 0, 0, tiled=True).astype(F32).sum(0)  12.4 us
    pallas_call x1, Pallas kernels, products(): pl.pallas_call(products_kernel, out_shape=(half, half, jax.ShapeDtypeStru...  11.6 us
    all_to_all x1, starting transfers between devices, per_device(): terms = lax.all_to_all(terms, 'z', 0, 0, tiled=True)  10.9 us
    ppermute x3, starting transfers between devices, per_device(): lax.ppermute(first, AXES, plane_pairs(k, True))  8.98 us
  transfers between devices with their start and end apart: 14, of which 10 were waited for; matrix products, arithmetic and copies ran while one was open for 1% of the time, Pallas kernels for 14%

profile of v4, /device:TPU:1, one launch (start us, length us, event | category | flops | bytes accessed | tf_op | source)
XLA Modules:
  0.0 152.4 jit_solution(1385520035539790511)
XLA Ops:
  2.0 1.9 %pieces.1 = bf16[16,114,128]{2,1,0:T(8,128)(2,1)} custom-call(s32[3]{0:T(128)} %pad_add_fusion.1.at, bf16[48,3072]{1,0:T(8,128)(2,1)} %codes.1, bf16[1,1]{1,0:T(2,128)(2,1)} %bitcast.21.amax, bf16[48,128]{1,0:T(8,128)(2,1)} %down.1, bf16[96,128]{1,0:T(8,128)(2,1)} %bitcast.29, bf16[8,3072]{1,0:T(8,128)(2,1)} %gate.1), custom_call_target="tpu_custom_call" | custom-call | tf_op jit(solution)/shard_map/pieces/pallas_call | solution.py:321
  3.9 15.7 %all-to-all-start = ((bf16[16,114,128]{2,1,0:T(8,128)(2,1)}), bf16[16,114,128]{2,1,0:T(8,128)(2,1)S(1)}, u32[]{:S(2)}, u32[]{:S(2)}) async-start(bf16[16,114,128]{2,1,0:T(8,128)(2,1)} %pieces.1), calls=%async_computation | async-start | bytes 983040 | tf_op jit(solution)/shard_map/all_to_all | solution.py:386
  19.7 2.9 %collective-permute-start.1 = (bf16[256,3072]{1,0:T(8,128)(2,1)S(1)}, bf16[256,3072]{1,0:T(8,128)(2,1)}, u32[]{:S(2)}, u32[]{:S(2)}) collective-permute-start(bf16[256,3072]{1,0:T(8,128)(2,1)S(1)} %copy-done.1), channel_id=1, source_target_pairs={{0,32},{32,0},{1,33},{33,1},{2,34},{34,2},{3,35},{35,3},{4,36},{36... | collective-permute-start | bytes 4718600 | tf_op jit(solution)/shard_map/ppermute | solution.py:41
  22.6 1.9 %collective-permute-start = (bf16[256,1536]{1,0:T(8,128)(2,1)}, bf16[256,1536]{1,0:T(8,128)(2,1)S(1)}, u32[]{:S(2)}, u32[]{:S(2)}) collective-permute-start(bf16[256,1536]{1,0:T(8,128)(2,1)} %rows_hbm.3), channel_id=1, source_target_pairs={{0,32},{32,0},{1,33},{33,1},{2,34},{34,2},{3,35},{35,3},{4,36},{36... | collective-permute-start | bytes 2359304 | tf_op jit(solution)/shard_map/ppermute | solution.py:41
  25.2 1.7 %collective-permute-done.rows_other_hbm = bf16[256,1536]{1,0:T(8,128)(2,1)S(1)} collective-permute-done((bf16[256,1536]{1,0:T(8,128)(2,1)}, bf16[256,1536]{1,0:T(8,128)(2,1)S(1)}, u32[]{:S(2)}, u32[]{:S(2)}) %collective-permute-start) | collective-permute-done | bytes 786464 | tf_op jit(solution)/shard_map/ppermute | solution.py:41
  27.0 14.4 %all-to-all-done.line = bf16[16,114,128]{2,1,0:T(8,128)(2,1)S(1)} async-done(((bf16[16,114,128]{2,1,0:T(8,128)(2,1)}), bf16[16,114,128]{2,1,0:T(8,128)(2,1)S(1)}, u32[]{:S(2)}, u32[]{:S(2)}) %all-to-all-start) | async-done | bytes 466976 | tf_op jit(solution)/shard_map/all_to_all | solution.py:386
  41.3 1.3 spread.1
  42.7 6.8 %all-to-all-start.1 = ((bf16[16,300,128]{2,1,0:T(8,128)(2,1)}), bf16[16,300,128]{2,1,0:T(8,128)(2,1)S(1)}, u32[]{:S(2)}, u32[]{:S(2)}) async-start(bf16[16,300,128]{2,1,0:T(8,128)(2,1)} %get-tuple-element.32), calls=%async_computation.1 | async-start | bytes 2490368 | tf_op jit(solution)/shard_map/all_to_all | solution.py:403
  49.5 4.5 %collective-permute-start.4 = (bf16[16,24,384]{2,1,0:T(8,128)(2,1)S(1)}, bf16[16,24,384]{2,1,0:T(8,128)(2,1)S(1)}, u32[]{:S(2)}, u32[]{:S(2)}) collective-permute-start(bf16[16,24,384]{2,1,0:T(8,128)(2,1)S(1)} %get-tuple-element.44), channel_id=1, source_target_pairs={{0,192},{1,193},{2,194},{3,195},{4,196},{5,197},{6,198},{7,199},{8... | collective-permute-start | bytes 884744 | tf_op jit(solution)/shard_map/ppermute | solution.py:404
  53.9 2.5 %collective-permute-start.3 = (bf16[16,24,384]{2,1,0:T(8,128)(2,1)S(1)}, bf16[16,24,384]{2,1,0:T(8,128)(2,1)S(1)}, u32[]{:S(2)}, u32[]{:S(2)}) collective-permute-start(bf16[16,24,384]{2,1,0:T(8,128)(2,1)S(1)} %get-tuple-element.44), channel_id=1, source_target_pairs={{0,128},{1,129},{2,130},{3,131},{4,132},{5,133},{6,134},{7,135},{8... | collective-permute-start | bytes 884744 | tf_op jit(solution)/shard_map/ppermute | solution.py:404
  56.4 2.0 %collective-permute-start.2 = (bf16[16,24,384]{2,1,0:T(8,128)(2,1)S(1)}, bf16[16,24,384]{2,1,0:T(8,128)(2,1)}, u32[]{:S(2)}, u32[]{:S(2)}) collective-permute-start(bf16[16,24,384]{2,1,0:T(8,128)(2,1)S(1)} %get-tuple-element.44), channel_id=1, source_target_pairs={{0,64},{1,65},{2,66},{3,67},{4,68},{5,69},{6,70},{7,71},{8,72},{9,... | collective-permute-start | bytes 884744 | tf_op jit(solution)/shard_map/ppermute | solution.py:404
  58.5 14.2 %collective-permute-done.4 = bf16[16,24,384]{2,1,0:T(8,128)(2,1)S(1)} collective-permute-done((bf16[16,24,384]{2,1,0:T(8,128)(2,1)S(1)}, bf16[16,24,384]{2,1,0:T(8,128)(2,1)S(1)}, u32[]{:S(2)}, u32[]{:S(2)}) %collective-permute-start.4) | collective-permute-done | bytes 294944 | tf_op jit(solution)/shard_map/ppermute | solution.py:404
  73.0 1.7 %collective-permute-done.2 = bf16[16,24,384]{2,1,0:T(8,128)(2,1)} collective-permute-done((bf16[16,24,384]{2,1,0:T(8,128)(2,1)S(1)}, bf16[16,24,384]{2,1,0:T(8,128)(2,1)}, u32[]{:S(2)}, u32[]{:S(2)}) %collective-permute-start.2) | collective-permute-done | bytes 294944 | tf_op jit(solution)/shard_map/ppermute | solution.py:404
  74.7 1.3 pad_maximum_fusion.t0
  76.0 2.5 %collective-permute-start.7 = (bf16[4,16,24,384]{3,2,1,0:T(8,128)(2,1)S(1)}, bf16[4,16,24,384]{3,2,1,0:T(8,128)(2,1)}, u32[]{:S(2)}, u32[]{:S(2)}) collective-permute-start(bf16[4,16,24,384]{3,2,1,0:T(8,128)(2,1)S(1)} %pad_maximum_fusion.t0), channel_id=1, source_target_pairs={{0,257},{1,256},{2,259},{3,258},{4,261},{5,260},{6,263},{7,262},{8... | collective-permute-start | bytes 3538952 | tf_op jit(solution)/shard_map/ppermute | solution.py:407
  78.6 2.8 %collective-permute-start.6 = (bf16[4,16,24,384]{3,2,1,0:T(8,128)(2,1)S(1)}, bf16[4,16,24,384]{3,2,1,0:T(8,128)(2,1)S(1)}, u32[]{:S(2)}, u32[]{:S(2)}) collective-permute-start(bf16[4,16,24,384]{3,2,1,0:T(8,128)(2,1)S(1)} %pad_maximum_fusion.t0), channel_id=1, source_target_pairs={{0,256},{1,257},{2,258},{3,259},{4,260},{5,261},{6,262},{7,263},{8... | collective-permute-start | bytes 3538952 | tf_op jit(solution)/shard_map/ppermute | solution.py:407
  81.4 3.7 %collective-permute-start.5 = (bf16[4,16,24,384]{3,2,1,0:T(8,128)(2,1)S(1)}, bf16[4,16,24,384]{3,2,1,0:T(8,128)(2,1)}, u32[]{:S(2)}, u32[]{:S(2)}) collective-permute-start(bf16[4,16,24,384]{3,2,1,0:T(8,128)(2,1)S(1)} %pad_maximum_fusion.t0), channel_id=1, source_target_pairs={{0,1},{1,0},{2,3},{3,2},{4,5},{5,4},{6,7},{7,6},{8,9},{9,8},{10,11... | collective-permute-start | bytes 3538952 | tf_op jit(solution)/shard_map/ppermute | solution.py:407
  85.0 6.6 %adapter_terms.1 = (bf16[256,128]{1,0:T(8,128)(2,1)}, bf16[256,128]{1,0:T(8,128)(2,1)}, bf16[256,128]{1,0:T(8,128)(2,1)}, f32[1,1536]{1,0:T(1,128)}, f32[1,1536]...) custom-call(s32[1]{0:T(128)} %bitcast.core, ...), custom_call_target="tpu_custom_call" | custom-call | flops 1400000000 | bytes 200000000 | tf_op jit(solution)/shard_map/adapter_terms/pallas_call | solution.py:269
  91.6 10.9 %all-to-all-start.2 = ((bf16[16,144,128]{2,1,0:T(8,128)(2,1)}), bf16[16,144,128]{2,1,0:T(8,128)(2,1)S(1)}, u32[]{:S(2)}, u32[]{:S(2)}) async-start(bf16[16,144,128]{2,1,0:T(8,128)(2,1)} %get-tuple-element.54), calls=%async_computation.2 | async-start | bytes 1179648 | tf_op jit(solution)/shard_map/all_to_all | solution.py:413
  102.7 0.7 pad_add_fusion.at
  103.3 3.9 %collective-permute-done.7.t3 = bf16[4,16,24,384]{3,2,1,0:T(8,128)(2,1)} collective-permute-done((bf16[4,16,24,384]{3,2,1,0:T(8,128)(2,1)S(1)}, bf16[4,16,24,384]{3,2,1,0:T(8,128)(2,1)}, u32[]{:S(2)}, u32[]{:S(2)}) %collective-permute-start.7) | collective-permute-done | bytes 1179680 | tf_op jit(solution)/shard_map/ppermute | solution.py:407
  107.2 2.5 %collective-permute-done.5.t1 = bf16[4,16,24,384]{3,2,1,0:T(8,128)(2,1)} collective-permute-done((bf16[4,16,24,384]{3,2,1,0:T(8,128)(2,1)S(1)}, bf16[4,16,24,384]{3,2,1,0:T(8,128)(2,1)}, u32[]{:S(2)}, u32[]{:S(2)}) %collective-permute-start.5) | collective-permute-done | bytes 1179680 | tf_op jit(solution)/shard_map/ppermute | solution.py:407
  109.8 11.6 %products.1 = (bf16[256,1536]{1,0:T(8,128)(2,1)}, bf16[256,1536]{1,0:T(8,128)(2,1)}, bf16[256,3072]{1,0:T(8,128)(2,1)}, f32[256,1536]{1,0:T(8,128)}) custom-call(s32[32]{0:T(128)} %pad_add_fusion.at, s32[1]{0:T(128)} %bitcast.core, bf16[256,128]{1,0:T(8,128)(2,1)} %get-tuple-element.37.low_other, f32[1,1536]{1,0:T(1,128)} %get-tuple-element.38.gate_other, ...), custom_call_target="tpu_custom_call" | custom-call | flops 4831838208 | bytes 200000000 | tf_op jit(solution)/shard_map/products/pallas_call | solution.py:219
  121.4 3.5 %collective-permute-start.8 = (bf16[256,1536]{1,0:T(8,128)(2,1)}, bf16[256,1536]{1,0:T(8,128)(2,1)S(1)}, u32[]{:S(2)}, u32[]{:S(2)}) collective-permute-start(bf16[256,1536]{1,0:T(8,128)(2,1)} %get-tuple-element.49), channel_id=1, source_target_pairs={{0,32},{32,0},{1,33},{33,1},{2,34},{34,2},{3,35},{35,3},{4,36},{36... | collective-permute-start | bytes 2359304 | tf_op jit(solution)/shard_map/ppermute | solution.py:41
  124.9 1.9 %collective-permute-start.9 = (bf16[256,1536]{1,0:T(8,128)(2,1)}, bf16[256,1536]{1,0:T(8,128)(2,1)S(1)}, u32[]{:S(2)}, u32[]{:S(2)}) collective-permute-start(bf16[256,1536]{1,0:T(8,128)(2,1)} %get-tuple-element.51), channel_id=1, source_target_pairs={{0,32},{32,0},{1,33},{33,1},{2,34},{34,2},{3,35},{35,3},{4,36},{36... | collective-permute-start | bytes 2359304 | tf_op jit(solution)/shard_map/ppermute | solution.py:41
  127.0 2.3 %collective-permute-done.9.dx_rest_hbm = bf16[256,1536]{1,0:T(8,128)(2,1)S(1)} collective-permute-done((bf16[256,1536]{1,0:T(8,128)(2,1)}, bf16[256,1536]{1,0:T(8,128)(2,1)S(1)}, u32[]{:S(2)}, u32[]{:S(2)}) %collective-permute-start.9) | collective-permute-done | bytes 786464 | tf_op jit(solution)/shard_map/ppermute | solution.py:41
  129.3 0.9 copy-done.5
  130.2 2.9 %finish.1 = (bf16[256,3072]{1,0:T(8,128)(2,1)}, bf16[256,1536]{1,0:T(8,128)(2,1)}) custom-call(s32[1]{0:T(128)} %bitcast.core, bf16[256,3072]{1,0:T(8,128)(2,1)} %get-tuple-element.48.mixed_in, bf16[256,1536]{1,0:T(8,128)(2,1)} %copy-done.4, f32[256,1536]{1,0:T(8,128)} %get-tuple-element.50.dx_own_hbm, ...), custom_call_target="tpu_custom_call", output_to_operand_aliasing={{0}: (1, {})} | custom-call | flops 1000000 | bytes 7000000 | tf_op jit(solution)/shard_map/finish/pallas_call | solution.py:245
  133.3 12.4 %all_to_all.20 = bf16[16,72,128]{2,1,0:T(8,128)(2,1)S(1)} all-to-all(bf16[16,72,128]{2,1,0:T(8,128)(2,1)S(1)} %bitcast.23), channel_id=1, replica_groups=mesh['yh'=2,'x'=4,'core'=2,'z'=16,'yl'=2] {'yh','x','yl'}, dimensions={0} | all-to-all | bytes 589824 | tf_op jit(solution)/shard_map/all_to_all | solution.py:425
  145.7 4.6 %collective-permute-start.10 = (f32[72,128]{1,0:T(8,128)S(1)}, f32[72,128]{1,0:T(8,128)S(1)}, u32[]{:S(2)}, u32[]{:S(2)}) collective-permute-start(f32[72,128]{1,0:T(8,128)S(1)} %convert_reduce_fusion), channel_id=1, source_target_pairs={{0,32},{32,0},{1,33},{33,1},{2,34},{34,2},{3,35},{35,3},{4,36},{36... | collective-permute-start | bytes 110600 | tf_op jit(solution)/shard_map/ppermute | solution.py:41
  150.3 0.8 collective-permute-done.10
  151.8 0.6 fusion.2
  (37 shorter events, 2.7 us)
Async XLA Ops:
  0.6 19.1 %copy-start.1 = (bf16[256,3072]{1,0:T(8,128)(2,1)S(1)}, bf16[256,3072]{1,0:T(8,128)(2,1)}, u32[]{:S(2)}) copy-start(bf16[256,3072]{1,0:T(8,128)(2,1)} %cot_hbm.3) | copy-start | bytes 4718596
  0.6 23.9 %copy-start.6 = (s32[32]{0:T(128)S(1)}, s32[32]{0:T(128)}, u32[]{:S(2)}) copy-start(s32[32]{0:T(128)} %param.15) | copy-start | bytes 388
  3.9 37.4 %all-to-all-start = ((bf16[16,114,128]{2,1,0:T(8,128)(2,1)}), bf16[16,114,128]{2,1,0:T(8,128)(2,1)S(1)}, u32[]{:S(2)}, u32[]{:S(2)}) async-start(bf16[16,114,128]{2,1,0:T(8,128)(2,1)} %pieces.1), calls=%async_computation | async-start | bytes 983040 | tf_op jit(solution)/shard_map/all_to_all | solution.py:386
  19.7 7.3 %collective-permute-start.1 = (bf16[256,3072]{1,0:T(8,128)(2,1)S(1)}, bf16[256,3072]{1,0:T(8,128)(2,1)}, u32[]{:S(2)}, u32[]{:S(2)}) collective-permute-start(bf16[256,3072]{1,0:T(8,128)(2,1)S(1)} %copy-done.1), channel_id=1, source_target_pairs={{0,32},{32,0},{1,33},{33,1},{2,34},{34,2},{3,35},{35,3},{4,36},{36... | collective-permute-start | bytes 4718600 | tf_op jit(solution)/shard_map/ppermute | solution.py:41
  22.6 4.4 %collective-permute-start = (bf16[256,1536]{1,0:T(8,128)(2,1)}, bf16[256,1536]{1,0:T(8,128)(2,1)S(1)}, u32[]{:S(2)}, u32[]{:S(2)}) collective-permute-start(bf16[256,1536]{1,0:T(8,128)(2,1)} %rows_hbm.3), channel_id=1, source_target_pairs={{0,32},{32,0},{1,33},{33,1},{2,34},{34,2},{3,35},{35,3},{4,36},{36... | collective-permute-start | bytes 2359304 | tf_op jit(solution)/shard_map/ppermute | solution.py:41
  27.0 15.7 %copy-start.3 = (bf16[256,1536]{1,0:T(8,128)(2,1)}, bf16[256,1536]{1,0:T(8,128)(2,1)S(1)}, u32[]{:S(2)}) copy-start(bf16[256,1536]{1,0:T(8,128)(2,1)S(1)} %collective-permute-done.rows_other_hbm) | copy-start | bytes 2359300
  42.7 32.0 %all-to-all-start.1 = ((bf16[16,300,128]{2,1,0:T(8,128)(2,1)}), bf16[16,300,128]{2,1,0:T(8,128)(2,1)S(1)}, u32[]{:S(2)}, u32[]{:S(2)}) async-start(bf16[16,300,128]{2,1,0:T(8,128)(2,1)} %get-tuple-element.32), calls=%async_computation.1 | async-start | bytes 2490368 | tf_op jit(solution)/shard_map/all_to_all | solution.py:403
  49.5 23.2 %collective-permute-start.4 = (bf16[16,24,384]{2,1,0:T(8,128)(2,1)S(1)}, bf16[16,24,384]{2,1,0:T(8,128)(2,1)S(1)}, u32[]{:S(2)}, u32[]{:S(2)}) collective-permute-start(bf16[16,24,384]{2,1,0:T(8,128)(2,1)S(1)} %get-tuple-element.44), channel_id=1, source_target_pairs={{0,192},{1,193},{2,194},{3,195},{4,196},{5,197},{6,198},{7,199},{8... | collective-permute-start | bytes 884744 | tf_op jit(solution)/shard_map/ppermute | solution.py:404
  53.9 19.0 %collective-permute-start.3 = (bf16[16,24,384]{2,1,0:T(8,128)(2,1)S(1)}, bf16[16,24,384]{2,1,0:T(8,128)(2,1)S(1)}, u32[]{:S(2)}, u32[]{:S(2)}) collective-permute-start(bf16[16,24,384]{2,1,0:T(8,128)(2,1)S(1)} %get-tuple-element.44), channel_id=1, source_target_pairs={{0,128},{1,129},{2,130},{3,131},{4,132},{5,133},{6,134},{7,135},{8... | collective-permute-start | bytes 884744 | tf_op jit(solution)/shard_map/ppermute | solution.py:404
  56.4 18.2 %collective-permute-start.2 = (bf16[16,24,384]{2,1,0:T(8,128)(2,1)S(1)}, bf16[16,24,384]{2,1,0:T(8,128)(2,1)}, u32[]{:S(2)}, u32[]{:S(2)}) collective-permute-start(bf16[16,24,384]{2,1,0:T(8,128)(2,1)S(1)} %get-tuple-element.44), channel_id=1, source_target_pairs={{0,64},{1,65},{2,66},{3,67},{4,68},{5,69},{6,70},{7,71},{8,72},{9,... | collective-permute-start | bytes 884744 | tf_op jit(solution)/shard_map/ppermute | solution.py:404
  74.7 1.3 copy-start
  76.0 15.6 %copy-start.2 = (bf16[4,16,24,384]{3,2,1,0:T(8,128)(2,1)}, bf16[4,16,24,384]{3,2,1,0:T(8,128)(2,1)S(1)}, u32[]{:S(2)}) copy-start(bf16[4,16,24,384]{3,2,1,0:T(8,128)(2,1)S(1)} %pad_maximum_fusion.t0) | copy-start | bytes 3538948
  76.0 31.2 %collective-permute-start.7 = (bf16[4,16,24,384]{3,2,1,0:T(8,128)(2,1)S(1)}, bf16[4,16,24,384]{3,2,1,0:T(8,128)(2,1)}, u32[]{:S(2)}, u32[]{:S(2)}) collective-permute-start(bf16[4,16,24,384]{3,2,1,0:T(8,128)(2,1)S(1)} %pad_maximum_fusion.t0), channel_id=1, source_target_pairs={{0,257},{1,256},{2,259},{3,258},{4,261},{5,260},{6,263},{7,262},{8... | collective-permute-start | bytes 3538952 | tf_op jit(solution)/shard_map/ppermute | solution.py:407
  78.6 28.7 %collective-permute-start.6 = (bf16[4,16,24,384]{3,2,1,0:T(8,128)(2,1)S(1)}, bf16[4,16,24,384]{3,2,1,0:T(8,128)(2,1)S(1)}, u32[]{:S(2)}, u32[]{:S(2)}) collective-permute-start(bf16[4,16,24,384]{3,2,1,0:T(8,128)(2,1)S(1)} %pad_maximum_fusion.t0), channel_id=1, source_target_pairs={{0,256},{1,257},{2,258},{3,259},{4,260},{5,261},{6,262},{7,263},{8... | collective-permute-start | bytes 3538952 | tf_op jit(solution)/shard_map/ppermute | solution.py:407
  81.4 28.4 %collective-permute-start.5 = (bf16[4,16,24,384]{3,2,1,0:T(8,128)(2,1)S(1)}, bf16[4,16,24,384]{3,2,1,0:T(8,128)(2,1)}, u32[]{:S(2)}, u32[]{:S(2)}) collective-permute-start(bf16[4,16,24,384]{3,2,1,0:T(8,128)(2,1)S(1)} %pad_maximum_fusion.t0), channel_id=1, source_target_pairs={{0,1},{1,0},{2,3},{3,2},{4,5},{5,4},{6,7},{7,6},{8,9},{9,8},{10,11... | collective-permute-start | bytes 3538952 | tf_op jit(solution)/shard_map/ppermute | solution.py:407
  91.6 41.6 %all-to-all-start.2 = ((bf16[16,144,128]{2,1,0:T(8,128)(2,1)}), bf16[16,144,128]{2,1,0:T(8,128)(2,1)S(1)}, u32[]{:S(2)}, u32[]{:S(2)}) async-start(bf16[16,144,128]{2,1,0:T(8,128)(2,1)} %get-tuple-element.54), calls=%async_computation.2 | async-start | bytes 1179648 | tf_op jit(solution)/shard_map/all_to_all | solution.py:413
  107.2 2.5 %copy-start.7 = (bf16[4,16,24,384]{3,2,1,0:T(8,128)(2,1)}, bf16[4,16,24,384]{3,2,1,0:T(8,128)(2,1)S(1)}, u32[]{:S(2)}) copy-start(bf16[4,16,24,384]{3,2,1,0:T(8,128)(2,1)S(1)} %collective-permute-done.6.t2) | copy-start | bytes 3538948
  121.4 5.6 %collective-permute-start.8 = (bf16[256,1536]{1,0:T(8,128)(2,1)}, bf16[256,1536]{1,0:T(8,128)(2,1)S(1)}, u32[]{:S(2)}, u32[]{:S(2)}) collective-permute-start(bf16[256,1536]{1,0:T(8,128)(2,1)} %get-tuple-element.49), channel_id=1, source_target_pairs={{0,32},{32,0},{1,33},{33,1},{2,34},{34,2},{3,35},{35,3},{4,36},{36... | collective-permute-start | bytes 2359304 | tf_op jit(solution)/shard_map/ppermute | solution.py:41
  124.9 4.4 %collective-permute-start.9 = (bf16[256,1536]{1,0:T(8,128)(2,1)}, bf16[256,1536]{1,0:T(8,128)(2,1)S(1)}, u32[]{:S(2)}, u32[]{:S(2)}) collective-permute-start(bf16[256,1536]{1,0:T(8,128)(2,1)} %get-tuple-element.51), channel_id=1, source_target_pairs={{0,32},{32,0},{1,33},{33,1},{2,34},{34,2},{3,35},{35,3},{4,36},{36... | collective-permute-start | bytes 2359304 | tf_op jit(solution)/shard_map/ppermute | solution.py:41
  127.0 2.3 %copy-start.4 = (bf16[256,1536]{1,0:T(8,128)(2,1)}, bf16[256,1536]{1,0:T(8,128)(2,1)S(1)}, u32[]{:S(2)}) copy-start(bf16[256,1536]{1,0:T(8,128)(2,1)S(1)} %collective-permute-done.8.mixed_rest_hbm) | copy-start | bytes 2359300
  129.3 0.9 copy-start.5
  145.7 5.5 %collective-permute-start.10 = (f32[72,128]{1,0:T(8,128)S(1)}, f32[72,128]{1,0:T(8,128)S(1)}, u32[]{:S(2)}, u32[]{:S(2)}) collective-permute-start(f32[72,128]{1,0:T(8,128)S(1)} %convert_reduce_fusion), channel_id=1, source_target_pairs={{0,32},{32,0},{1,33},{33,1},{2,34},{34,2},{3,35},{35,3},{4,36},{36... | collective-permute-start | bytes 110600 | tf_op jit(solution)/shard_map/ppermute | solution.py:41

commit v5 on v4

--- a/solution.py
+++ b/solution.py
@@ -64,26 +64,28 @@
     up_hbm, down_hbm, t0, t1, t2, t3, rows_hbm, rows_other_hbm, cot_hbm, cot_other_hbm,
     mixed_other_hbm, dx_other_hbm, mixed_hbm, dx_hbm,
     blocks, wm, rows, rows_other, cot, cot_other, branch, branch_other, up, down,
-    mixed_other, dx_other, mixed, dx, sems,
+    mixed_other, dx_other, mixed, dx, side_other, side, sems,
 ):
-    pairs = []
+    half = pl.ds(pl.multiple_of(core[0] * 1536, 128), 1536)
+    pairs = [(cot_other_hbm.at[:, half], cot_other), (cot_hbm.at[:, half], cot)]
+    pairs += [(down_hbm, down), (up_hbm, up)]
     for k2, t in enumerate((t0, t1, t2, t3)):
         for k1 in range(4):
             b = k2 * 4 + k1
             col = pl.multiple_of(at[b] * 384, 128)
             pairs.append((t.at[k1], blocks.at[:, at[16 + b], :, pl.ds(col, 384)]))
-    half = pl.ds(pl.multiple_of(core[0] * 1536, 128), 1536)
-    pairs.append((cot_other_hbm.at[:, half], cot_other))
-    pairs.append((cot_hbm.at[:, half], cot))
-    pairs.append((down_hbm, down))
-    pairs.append((rows_other_hbm, rows_other))
-    pairs.append((rows_hbm, rows))
-    pairs.append((up_hbm, up))
+    pairs += [(rows_other_hbm, rows_other), (rows_hbm, rows)]
     copies = fetch(pairs, sems)
-    for copy in copies[:19]:
+    for copy in copies[:4]:
         copy.wait()
     branch_other[...] = (cot_other[...].astype(F32) * gate_other[...]).astype(BF)
     branch[...] = (cot[...].astype(F32) * gate[...]).astype(BF)
+    for s in STRIPS:
+        dx[:, s] = nt(low_grad[...], down[s, :])
+        side_other[:, s] = SCALE * nt(low_other[...], up[s, :])
+        side[:, s] = SCALE * nt(low[...], up[s, :])
+    for copy in copies[4:20]:
+        copy.wait()
 
     def pack(z, carry):
         part = blocks[z].astype(F32).reshape(96, 1536).astype(BF)
@@ -94,17 +96,17 @@
     for s in STRIPS:
         dx_other[:, s] = nt(branch_other[...], wm[s, :]).astype(BF)
     out = fetch([(dx_other, dx_other_hbm)], sems.at[pl.ds(22, 1)])
-    for copy in copies[19:]:
+    for copy in copies[20:]:
         copy.wait()
     for s in STRIPS:
-        p = nn(rows_other[...], wm[:, s]) + SCALE * nt(low_other[...], up[s, :])
+        p = nn(rows_other[...], wm[:, s]) + side_other[:, s]
         mixed_other[:, s] = (p * gate_other[:, s]).astype(BF)
     out += fetch([(mixed_other, mixed_other_hbm)], sems.at[pl.ds(23, 1)])
     for s in STRIPS:
-        dx[:, s] = nt(branch[...], wm[s, :]) + nt(low_grad[...], down[s, :])
+        dx[:, s] = nt(branch[...], wm[s, :]) + dx[:, s]
     out += fetch([(dx, dx_hbm)], sems.at[pl.ds(24, 1)])
     for s in STRIPS:
-        p = nn(rows[...], wm[:, s]) + SCALE * nt(low[...], up[s, :])
+        p = nn(rows[...], wm[:, s]) + side[:, s]
         mixed[:, s] = (p * gate[:, s]).astype(BF)
     out += fetch([(mixed, mixed_hbm.at[:, half])], sems.at[pl.ds(25, 1)])
     for copy in out:
@@ -133,26 +135,32 @@
 
 
 def adapter_kernel(
-    core, got_hbm, rows_hbm, rows_other_hbm, cot_hbm, cot_other_hbm,
+    core, got_hbm, got_other_hbm, rows_hbm, rows_other_hbm, cot_hbm, cot_other_hbm,
     low, low_other, low_grad, gate_own, gate_other, down_hbm, up_hbm, terms_hbm,
-    wide, down_wide, up_wide, down, up, gates, branch, td, tu, kept, terms,
-    rows, rows_other, cot, cot_other, got, sems,
+    wide, parts, down_wide, up_wide, down, up, gates, branch, td, tu, kept, terms,
+    rows, rows_other, cot, cot_other, got, got_other, sems,
 ):
-    load = fetch([(got_hbm, got)], sems.at[pl.ds(7, 1)])
+    load = fetch([(got_hbm, got), (got_other_hbm, got_other)], sems.at[pl.ds(7, 2)])
     copies = fetch(
         [(rows_hbm, rows), (rows_other_hbm, rows_other), (cot_hbm, cot), (cot_other_hbm, cot_other)],
         sems.at[pl.ds(0, 4)],
     )
-    load[0].wait()
+    for copy in load:
+        copy.wait()
+    first = core[0] == 0
     for s in range(16):
-        wide[s] = got[s].astype(F32)
+        mine, theirs = got[s].astype(F32), got_other[s].astype(F32)
+        wide[s] = mine
+        parts[0] = jnp.where(first, mine, theirs)
+        parts[1] = jnp.where(first, theirs, mine)
         j, yl = s // 2, s % 2
-        for z in range(16):
-            a, b = 96 * z + 48 * yl + 6 * j, 192 * z + 96 * yl + 12 * j
-            down_wide[a : a + 6] = wide[s, 18 * z : 18 * z + 6]
-            up_wide[b : b + 12] = wide[s, 18 * z + 6 : 18 * z + 18]
+        for c in range(2):
+            for z in range(16):
+                a, b = 96 * z + 48 * yl + 6 * j + 3 * c, 192 * z + 96 * yl + 12 * j + 6 * c
+                down_wide[a : a + 3] = parts[c, 9 * z : 9 * z + 3]
+                up_wide[b : b + 6] = parts[c, 9 * z + 3 : 9 * z + 9]
     for j in range(8):
-        part = wide[2 * j, 288:300] + wide[2 * j + 1, 288:300]
+        part = wide[2 * j, 144:156] + wide[2 * j + 1, 144:156]
         part = part[:6] + part[6:]
         for r in range(6):
             at = 384 * j + 128 * (r % 3)
@@ -161,7 +169,6 @@
     up[...] = up_wide[...].astype(BF)
     at = pl.multiple_of(core[0] * 1536, 128)
     out = fetch([(down, down_hbm), (up.at[pl.ds(at, 1536)], up_hbm)], sems.at[pl.ds(4, 2)])
-    first = core[0] == 0
     gate = jnp.where(first, gates[0:1], gates[1:2])
     gate_own[...] = jnp.where(first, gates[0:1, :1536], gates[1:2, 1536:])
     gate_other[...] = jnp.where(first, gates[1:2, :1536], gates[0:1, 1536:])
@@ -232,7 +239,7 @@
             *[pltpu.VMEM((256, 1536), BF)] * 6,
             *[pltpu.VMEM((1536, 128), BF)] * 2,
             *[pltpu.VMEM((256, 1536), BF)] * 3,
-            pltpu.VMEM((256, 1536), F32),
+            *[pltpu.VMEM((256, 1536), F32)] * 3,
             pltpu.SemaphoreType.DMA((26,)),
         ],
         compiler_params=PARAMS,
@@ -269,10 +276,11 @@
     return pl.pallas_call(
         adapter_kernel,
         out_shape=(thin, thin, thin, row, row, tall, tall, out(16, 144, 128)),
-        in_specs=[pl.BlockSpec(memory_space=pltpu.SMEM)] + hbm(5),
+        in_specs=[pl.BlockSpec(memory_space=pltpu.SMEM)] + hbm(6),
         out_specs=tuple(vmem(5) + hbm(3)),
         scratch_shapes=[
-            pltpu.VMEM((16, 300, 128), F32),
+            pltpu.VMEM((16, 156, 128), F32),
+            pltpu.VMEM((2, 156, 128), F32),
             pltpu.VMEM((1536, 128), F32),
             pltpu.VMEM((3072, 128), F32),
             pltpu.VMEM((1536, 128), BF),
@@ -285,8 +293,8 @@
             pltpu.VMEM((16, 144, 128), BF),
             *[pltpu.VMEM((256, 1536), BF)] * 2,
             *[pltpu.VMEM((256, 3072), BF)] * 2,
-            pltpu.VMEM((16, 300, 128), BF),
-            pltpu.SemaphoreType.DMA((8,)),
+            *[pltpu.VMEM((16, 156, 128), BF)] * 2,
+            pltpu.SemaphoreType.DMA((9,)),
         ],
         compiler_params=PARAMS,
         cost_estimate=pl.CostEstimate(flops=1400000000, bytes_accessed=200000000, transcendentals=0),
@@ -306,13 +314,15 @@
         wide[24 * k : 24 * k + 24] = weight[:, lanes]
         wide[72 + 8 * k : 80 + 8 * k] = gates[:, lanes]
 
+    i = 2 * j + core
+
     def pick(n, size):
         row = lax.broadcasted_iota(jnp.int32, (n, size), 0)
         col = lax.broadcasted_iota(jnp.int32, (n, size), 1)
-        return jnp.where(col == row + n * j, 1.0, 0.0).astype(BF)
-
-    wide[96:102] = nn(pick(6, 48), down[...])
-    wide[102:114] = nn(pick(12, 96), up[...])
+        return jnp.where(col == row + n * i, 1.0, 0.0).astype(BF)
+
+    wide[96:99] = nn(pick(3, 48), down[...])
+    wide[99:105] = nn(pick(6, 96), up[...])
     for d in range(16):
         out[d] = wide[...].astype(BF)
 
@@ -320,10 +330,10 @@
 def pieces(at, codes, amax, down, up, gate):
     return pl.pallas_call(
         pieces_kernel,
-        out_shape=jax.ShapeDtypeStruct((16, 114, 128), BF),
+        out_shape=jax.ShapeDtypeStruct((16, 105, 128), BF),
         in_specs=[pl.BlockSpec(memory_space=pltpu.SMEM)] + vmem(5),
         out_specs=vmem(1)[0],
-        scratch_shapes=[pltpu.VMEM((114, 128), F32)],
+        scratch_shapes=[pltpu.VMEM((105, 128), F32)],
         compiler_params=PARAMS,
         name="pieces",
     )(at, codes, amax, down, up, gate)
@@ -335,7 +345,7 @@
     copies = fetch([(weight, weight_hbm)], sems.at[pl.ds(0, 1)])
     wide[...] = line[...].astype(F32)
     for z in range(16):
-        maps[18 * z : 18 * z + 18] = wide[z, 96:114]
+        maps[9 * z : 9 * z + 9] = wide[z, 96:105]
     for k in range(3):
         block = wide[:, 72 + 8 * k : 80 + 8 * k].reshape(128, 128).astype(BF)
         part = nn(features[...], block)
@@ -348,15 +358,15 @@
                     pair[2 * j, r : r + 1] = row
                     pair[2 * j + 1, r : r + 1] = row
     for d in range(16):
-        out[d, :288] = maps[...].astype(BF)
-        out[d, 288:] = pair[d].astype(BF)
+        out[d, :144] = maps[...].astype(BF)
+        out[d, 144:] = pair[d].astype(BF)
     copies += fetch([(out, out_hbm)], sems.at[pl.ds(1, 1)])
     for copy in copies:
         copy.wait()
 
 
 def spread(line, features):
-    shapes = ((16, 114, 128), (16, 300, 128), (16, 24, 384))
+    shapes = ((16, 105, 128), (16, 156, 128), (16, 24, 384))
     return pl.pallas_call(
         spread_kernel,
         out_shape=tuple(jax.ShapeDtypeStruct(s, BF) for s in shapes[1:]),
@@ -364,7 +374,7 @@
         out_specs=tuple(hbm(2)),
         scratch_shapes=[
             pltpu.VMEM(shapes[0], F32),
-            pltpu.VMEM((288, 128), F32),
+            pltpu.VMEM((144, 128), F32),
             pltpu.VMEM((16, 12, 128), F32),
             pltpu.VMEM(shapes[1], BF),
             pltpu.VMEM(shapes[2], BF),
@@ -408,7 +418,7 @@
     second = [second[0], second[2], second[1], second[3]]
 
     low, low_other, low_grad, gate_own, gate_other, down_all, up_half, terms = adapter_terms(
-        core, got, rows, rows_other, cotangent, cot_other
+        core, got, other_core(got), rows, rows_other, cotangent, cot_other
     )
     terms = lax.all_to_all(terms, "z", 0, 0, tiled=True)
     terms = terms.astype(F32).sum(0).astype(BF)
@@ -419,8 +429,8 @@
     )
     dx_rest = other_core(dx_other)
     mixed_rest = other_core(mixed_other)
+    mixed_rest, dx_rest, terms = lax.optimization_barrier((mixed_rest, dx_rest, terms))
     mixed, dx = finish(core, mixed_own, mixed_rest, dx_own, dx_rest)
-    mixed, dx, terms = lax.optimization_barrier((mixed, dx, terms))
     terms = jnp.broadcast_to(terms.reshape(1, 2, 72, 128), (8, 2, 72, 128)).reshape(16, 72, 128)
     terms = lax.all_to_all(terms, PLANE, 0, 0, tiled=True).astype(F32).sum(0)
     rest = other_core(terms)

time: 153 us -> 151 us (0.987)
  waiting for transfers between devices: 42 us -> 37.3 us
  starting transfers between devices: 66.2 us -> 68.9 us
    ppermute x5 -> x6, starting transfers between devices: 14.8 us -> 22.6 us  [other_core(): return lax.ppermute(v, 'core', [(0, 1), (1, 0)])]
    ppermute x3, waiting for transfers between devices: 16.2 us -> 9.26 us  [per_device(): lax.ppermute(line, AXES, plane_pairs(k, False))]
    all_to_all x1, starting transfers between devices: 10.9 us -> 5.79 us  [per_device(): terms = lax.all_to_all(terms, 'z', 0, 0, tiled=True)]
    ppermute x3, waiting for transfers between devices: 6.42 us -> 10.3 us  [per_device(): lax.ppermute(first, AXES, plane_pairs(k, True))]
    ppermute x5 -> x6, waiting for transfers between devices: 5.03 us -> 4.23 us  [other_core(): return lax.ppermute(v, 'core', [(0, 1), (1, 0)])]
  transfers between devices with their start and end apart: 14 -> 15, of which waited for: 10 -> 8; matrix products, arithmetic and copies ran while one was open for 1% -> 2% of each run, Pallas kernels for 14% -> 14%
where the time goes in v5:
time: 151 us; the launch traced here: 150 us
  starting transfers between devices  68.9 us (46%)
  waiting for transfers between devices  37.3 us (25%)
  Pallas kernels  23.3 us (15%)
  blocking collectives  13.7 us (9%)
  other arithmetic  3.37 us (2%)
  between operations  1.76 us (1%)
  local copies, waits for them, and re-layouts  1.63 us (1%)
    ppermute x6, starting transfers between devices, other_core(): return lax.ppermute(v, 'core', [(0, 1), (1, 0)])  22.6 us
    all_to_all x1, starting transfers between devices, per_device(): line = lax.all_to_all(line, 'z', 0, 0, tiled=True)  15.7 us
    all_to_all x1, blocking collectives, per_device(): terms = lax.all_to_all(terms, PLANE, 0, 0, tiled=True).astype(F32).sum(0)  13.7 us
    all_to_all x1, waiting for transfers between devices, per_device(): line = lax.all_to_all(line, 'z', 0, 0, tiled=True)  13.4 us
    pallas_call x1, Pallas kernels, products(): pl.pallas_call(products_kernel, out_shape=(half, half, jax.ShapeDtypeStru...  10.7 us
    ppermute x3, waiting for transfers between devices, per_device(): lax.ppermute(first, AXES, plane_pairs(k, True))  10.3 us
    ppermute x3, waiting for transfers between devices, per_device(): lax.ppermute(line, AXES, plane_pairs(k, False))  9.26 us
    ppermute x3, starting transfers between devices, per_device(): lax.ppermute(first, AXES, plane_pairs(k, True))  8.98 us
  transfers between devices with their start and end apart: 15, of which 8 were waited for; matrix products, arithmetic and copies ran while one was open for 2% of the time, Pallas kernels for 14%

profile of v5, /device:TPU:1, one launch (start us, length us, event | category | flops | bytes accessed | tf_op | source)
XLA Modules:
  0.0 149.9 jit_solution(13248580698873712758)
XLA Ops:
  1.4 0.6 pad_add_fusion.1.at
  2.0 1.9 %pieces.1 = bf16[16,105,128]{2,1,0:T(8,128)(2,1)} custom-call(s32[3]{0:T(128)} %pad_add_fusion.1.at, bf16[48,3072]{1,0:T(8,128)(2,1)} %codes.1, bf16[1,1]{1,0:T(2,128)(2,1)} %bitcast.21.amax, bf16[48,128]{1,0:T(8,128)(2,1)} %down.1, bf16[96,128]{1,0:T(8,128)(2,1)} %bitcast.29, bf16[8,3072]{1,0:T(8,128)(2,1)} %gate.1), custom_call_target="tpu_custom_call" | custom-call | tf_op jit(solution)/shard_map/pieces/pallas_call | solution.py:331
  3.9 15.7 %all-to-all-start = ((bf16[16,105,128]{2,1,0:T(8,128)(2,1)}), bf16[16,105,128]{2,1,0:T(8,128)(2,1)S(1)}, u32[]{:S(2)}, u32[]{:S(2)}) async-start(bf16[16,105,128]{2,1,0:T(8,128)(2,1)} %pieces.1), calls=%async_computation | async-start | bytes 917504 | tf_op jit(solution)/shard_map/all_to_all | solution.py:396
  19.7 2.9 %collective-permute-start.1 = (bf16[256,3072]{1,0:T(8,128)(2,1)S(1)}, bf16[256,3072]{1,0:T(8,128)(2,1)}, u32[]{:S(2)}, u32[]{:S(2)}) collective-permute-start(bf16[256,3072]{1,0:T(8,128)(2,1)S(1)} %copy-done.1), channel_id=1, source_target_pairs={{0,32},{32,0},{1,33},{33,1},{2,34},{34,2},{3,35},{35,3},{4,36},{36... | collective-permute-start | bytes 4718600 | tf_op jit(solution)/shard_map/ppermute | solution.py:41
  22.6 1.9 %collective-permute-start = (bf16[256,1536]{1,0:T(8,128)(2,1)}, bf16[256,1536]{1,0:T(8,128)(2,1)}, u32[]{:S(2)}, u32[]{:S(2)}) collective-permute-start(bf16[256,1536]{1,0:T(8,128)(2,1)} %rows_hbm.3), channel_id=1, source_target_pairs={{0,32},{32,0},{1,33},{33,1},{2,34},{34,2},{3,35},{35,3},{4,36},{36... | collective-permute-start | bytes 2359304 | tf_op jit(solution)/shard_map/ppermute | solution.py:41
  25.2 1.9 %collective-permute-done.rows_other_hbm = bf16[256,1536]{1,0:T(8,128)(2,1)} collective-permute-done((bf16[256,1536]{1,0:T(8,128)(2,1)}, bf16[256,1536]{1,0:T(8,128)(2,1)}, u32[]{:S(2)}, u32[]{:S(2)}) %collective-permute-start) | collective-permute-done | bytes 786464 | tf_op jit(solution)/shard_map/ppermute | solution.py:41
  27.1 13.4 %all-to-all-done.line = bf16[16,105,128]{2,1,0:T(8,128)(2,1)S(1)} async-done(((bf16[16,105,128]{2,1,0:T(8,128)(2,1)}), bf16[16,105,128]{2,1,0:T(8,128)(2,1)S(1)}, u32[]{:S(2)}, u32[]{:S(2)}) %all-to-all-start) | async-done | bytes 430112 | tf_op jit(solution)/shard_map/all_to_all | solution.py:396
  40.5 1.1 spread.1
  41.7 6.8 %all-to-all-start.1 = ((bf16[16,156,128]{2,1,0:T(8,128)(2,1)}), bf16[16,156,128]{2,1,0:T(8,128)(2,1)S(1)}, u32[]{:S(2)}, u32[]{:S(2)}) async-start(bf16[16,156,128]{2,1,0:T(8,128)(2,1)} %get-tuple-element.32), calls=%async_computation.1 | async-start | bytes 1310720 | tf_op jit(solution)/shard_map/all_to_all | solution.py:413
  48.4 4.5 %collective-permute-start.4 = (bf16[16,24,384]{2,1,0:T(8,128)(2,1)S(1)}, bf16[16,24,384]{2,1,0:T(8,128)(2,1)S(1)}, u32[]{:S(2)}, u32[]{:S(2)}) collective-permute-start(bf16[16,24,384]{2,1,0:T(8,128)(2,1)S(1)} %get-tuple-element.44), channel_id=1, source_target_pairs={{0,192},{1,193},{2,194},{3,195},{4,196},{5,197},{6,198},{7,199},{8... | collective-permute-start | bytes 884744 | tf_op jit(solution)/shard_map/ppermute | solution.py:414
  52.9 2.5 %collective-permute-start.3 = (bf16[16,24,384]{2,1,0:T(8,128)(2,1)S(1)}, bf16[16,24,384]{2,1,0:T(8,128)(2,1)S(1)}, u32[]{:S(2)}, u32[]{:S(2)}) collective-permute-start(bf16[16,24,384]{2,1,0:T(8,128)(2,1)S(1)} %get-tuple-element.44), channel_id=1, source_target_pairs={{0,128},{1,129},{2,130},{3,131},{4,132},{5,133},{6,134},{7,135},{8... | collective-permute-start | bytes 884744 | tf_op jit(solution)/shard_map/ppermute | solution.py:414
  55.4 2.0 %collective-permute-start.2 = (bf16[16,24,384]{2,1,0:T(8,128)(2,1)S(1)}, bf16[16,24,384]{2,1,0:T(8,128)(2,1)S(1)}, u32[]{:S(2)}, u32[]{:S(2)}) collective-permute-start(bf16[16,24,384]{2,1,0:T(8,128)(2,1)S(1)} %get-tuple-element.44), channel_id=1, source_target_pairs={{0,64},{1,65},{2,66},{3,67},{4,68},{5,69},{6,70},{7,71},{8,72},{9,... | collective-permute-start | bytes 884744 | tf_op jit(solution)/shard_map/ppermute | solution.py:414
  57.4 9.1 %collective-permute-done.4 = bf16[16,24,384]{2,1,0:T(8,128)(2,1)S(1)} collective-permute-done((bf16[16,24,384]{2,1,0:T(8,128)(2,1)S(1)}, bf16[16,24,384]{2,1,0:T(8,128)(2,1)S(1)}, u32[]{:S(2)}, u32[]{:S(2)}) %collective-permute-start.4) | collective-permute-done | bytes 294944 | tf_op jit(solution)/shard_map/ppermute | solution.py:414
  67.0 7.2 %collective-permute-start.5 = (bf16[16,156,128]{2,0,1:T(8,128)(2,1)S(1)}, bf16[16,156,128]{2,0,1:T(8,128)(2,1)S(1)}, u32[]{:S(2)}, u32[]{:S(2)}) collective-permute-start(bf16[16,156,128]{2,0,1:T(8,128)(2,1)S(1)} %copy.18), channel_id=1, source_target_pairs={{0,32},{32,0},{1,33},{33,1},{2,34},{34,2},{3,35},{35,3},{4,36},{36... | collective-permute-start | bytes 1916936 | tf_op jit(solution)/shard_map/ppermute | solution.py:41
  74.4 4.1 %collective-permute-start.8 = (bf16[4,16,24,384]{3,2,1,0:T(8,128)(2,1)S(1)}, bf16[4,16,24,384]{3,2,1,0:T(8,128)(2,1)}, u32[]{:S(2)}, u32[]{:S(2)}) collective-permute-start(bf16[4,16,24,384]{3,2,1,0:T(8,128)(2,1)S(1)} %pad_maximum_fusion.t0), channel_id=1, source_target_pairs={{0,257},{1,256},{2,259},{3,258},{4,261},{5,260},{6,263},{7,262},{8... | collective-permute-start | bytes 3538952 | tf_op jit(solution)/shard_map/ppermute | solution.py:417
  78.5 2.5 %collective-permute-start.7 = (bf16[4,16,24,384]{3,2,1,0:T(8,128)(2,1)S(1)}, bf16[4,16,24,384]{3,2,1,0:T(8,128)(2,1)S(1)}, u32[]{:S(2)}, u32[]{:S(2)}) collective-permute-start(bf16[4,16,24,384]{3,2,1,0:T(8,128)(2,1)S(1)} %pad_maximum_fusion.t0), channel_id=1, source_target_pairs={{0,256},{1,257},{2,258},{3,259},{4,260},{5,261},{6,262},{7,263},{8... | collective-permute-start | bytes 3538952 | tf_op jit(solution)/shard_map/ppermute | solution.py:417
  81.0 2.4 %collective-permute-start.6 = (bf16[4,16,24,384]{3,2,1,0:T(8,128)(2,1)S(1)}, bf16[4,16,24,384]{3,2,1,0:T(8,128)(2,1)}, u32[]{:S(2)}, u32[]{:S(2)}) collective-permute-start(bf16[4,16,24,384]{3,2,1,0:T(8,128)(2,1)S(1)} %pad_maximum_fusion.t0), channel_id=1, source_target_pairs={{0,1},{1,0},{2,3},{3,2},{4,5},{5,4},{6,7},{7,6},{8,9},{9,8},{10,11... | collective-permute-start | bytes 3538952 | tf_op jit(solution)/shard_map/ppermute | solution.py:417
  83.4 1.0 copy.19.got_other_hbm
  84.4 6.7 %adapter_terms.1 = (bf16[256,128]{1,0:T(8,128)(2,1)}, bf16[256,128]{1,0:T(8,128)(2,1)}, bf16[256,128]{1,0:T(8,128)(2,1)}, f32[1,1536]{1,0:T(1,128)}, f32[1,1536]...) custom-call(s32[1]{0:T(128)} %bitcast.core, ...), custom_call_target="tpu_custom_call" | custom-call | flops 1400000000 | bytes 200000000 | tf_op jit(solution)/shard_map/adapter_terms/pallas_call | solution.py:276
  91.1 5.8 %all-to-all-start.2 = ((bf16[16,144,128]{2,1,0:T(8,128)(2,1)}), bf16[16,144,128]{2,1,0:T(8,128)(2,1)S(1)}, u32[]{:S(2)}, u32[]{:S(2)}) async-start(bf16[16,144,128]{2,1,0:T(8,128)(2,1)} %get-tuple-element.51), calls=%async_computation.2 | async-start | bytes 1179648 | tf_op jit(solution)/shard_map/all_to_all | solution.py:423
  97.1 0.7 pad_add_fusion.at
  97.8 7.8 %collective-permute-done.8.t3 = bf16[4,16,24,384]{3,2,1,0:T(8,128)(2,1)} collective-permute-done((bf16[4,16,24,384]{3,2,1,0:T(8,128)(2,1)S(1)}, bf16[4,16,24,384]{3,2,1,0:T(8,128)(2,1)}, u32[]{:S(2)}, u32[]{:S(2)}) %collective-permute-start.8) | collective-permute-done | bytes 1179680 | tf_op jit(solution)/shard_map/ppermute | solution.py:417
  105.6 2.5 %collective-permute-done.6.t1 = bf16[4,16,24,384]{3,2,1,0:T(8,128)(2,1)} collective-permute-done((bf16[4,16,24,384]{3,2,1,0:T(8,128)(2,1)S(1)}, bf16[4,16,24,384]{3,2,1,0:T(8,128)(2,1)}, u32[]{:S(2)}, u32[]{:S(2)}) %collective-permute-start.6) | collective-permute-done | bytes 1179680 | tf_op jit(solution)/shard_map/ppermute | solution.py:417
  108.2 10.7 %products.1 = (bf16[256,1536]{1,0:T(8,128)(2,1)}, bf16[256,1536]{1,0:T(8,128)(2,1)}, bf16[256,3072]{1,0:T(8,128)(2,1)}, f32[256,1536]{1,0:T(8,128)}) custom-call(s32[32]{0:T(128)} %pad_add_fusion.at, s32[1]{0:T(128)} %bitcast.core, bf16[256,128]{1,0:T(8,128)(2,1)} %get-tuple-element.37.low_other, f32[1,1536]{1,0:T(1,128)} %get-tuple-element.38.gate_other, ...), custom_call_target="tpu_custom_call" | custom-call | flops 4831838208 | bytes 200000000 | tf_op jit(solution)/shard_map/products/pallas_call | solution.py:226
  118.8 3.1 %collective-permute-start.9 = (bf16[256,1536]{1,0:T(8,128)(2,1)}, bf16[256,1536]{1,0:T(8,128)(2,1)S(1)}, u32[]{:S(2)}, u32[]{:S(2)}) collective-permute-start(bf16[256,1536]{1,0:T(8,128)(2,1)} %get-tuple-element.49), channel_id=1, source_target_pairs={{0,32},{32,0},{1,33},{33,1},{2,34},{34,2},{3,35},{35,3},{4,36},{36... | collective-permute-start | bytes 2359304 | tf_op jit(solution)/shard_map/ppermute | solution.py:41
  121.9 1.9 %collective-permute-start.10 = (bf16[256,1536]{1,0:T(8,128)(2,1)}, bf16[256,1536]{1,0:T(8,128)(2,1)S(1)}, u32[]{:S(2)}, u32[]{:S(2)}) collective-permute-start(bf16[256,1536]{1,0:T(8,128)(2,1)} %get-tuple-element.50), channel_id=1, source_target_pairs={{0,32},{32,0},{1,33},{33,1},{2,34},{34,2},{3,35},{35,3},{4,36},{36... | collective-permute-start | bytes 2359304 | tf_op jit(solution)/shard_map/ppermute | solution.py:41
  124.0 2.3 %collective-permute-done.10.dx_rest_hbm = bf16[256,1536]{1,0:T(8,128)(2,1)S(1)} collective-permute-done((bf16[256,1536]{1,0:T(8,128)(2,1)}, bf16[256,1536]{1,0:T(8,128)(2,1)S(1)}, u32[]{:S(2)}, u32[]{:S(2)}) %collective-permute-start.10) | collective-permute-done | bytes 786464 | tf_op jit(solution)/shard_map/ppermute | solution.py:41
  126.3 13.7 %all_to_all.20 = bf16[16,72,128]{2,1,0:T(8,128)(2,1)S(1)} all-to-all(bf16[16,72,128]{2,1,0:T(8,128)(2,1)S(1)} %bitcast.23), channel_id=1, replica_groups=mesh['yh'=2,'x'=4,'core'=2,'z'=16,'yl'=2] {'yh','x','yl'}, dimensions={0} | all-to-all | bytes 589824 | tf_op jit(solution)/shard_map/all_to_all | solution.py:435
  140.1 5.6 %collective-permute-start.11 = (f32[72,128]{1,0:T(8,128)S(1)}, f32[72,128]{1,0:T(8,128)S(1)}, u32[]{:S(2)}, u32[]{:S(2)}) collective-permute-start(f32[72,128]{1,0:T(8,128)S(1)} %convert_reduce_fusion), channel_id=1, source_target_pairs={{0,32},{32,0},{1,33},{33,1},{2,34},{34,2},{3,35},{35,3},{4,36},{36... | collective-permute-start | bytes 110600 | tf_op jit(solution)/shard_map/ppermute | solution.py:41
  145.7 2.9 %finish.1 = (bf16[256,3072]{1,0:T(8,128)(2,1)}, bf16[256,1536]{1,0:T(8,128)(2,1)}) custom-call(s32[1]{0:T(128)} %bitcast.core, bf16[256,3072]{1,0:T(8,128)(2,1)} %get-tuple-element.48.mixed_in, bf16[256,1536]{1,0:T(8,128)(2,1)} %copy-done.3, f32[256,1536]{1,0:T(8,128)} %get-tuple-element.53.dx_own_hbm, ...), custom_call_target="tpu_custom_call", output_to_operand_aliasing={{0}: (1, {})} | custom-call | flops 1000000 | bytes 7000000 | tf_op jit(solution)/shard_map/finish/pallas_call | solution.py:252
  148.7 0.6 maximum_multiply_fusion
  149.3 0.6 fusion.2
  (39 shorter events, 1.7 us)
Async XLA Ops:
  0.6 19.0 %copy-start.1 = (bf16[256,3072]{1,0:T(8,128)(2,1)S(1)}, bf16[256,3072]{1,0:T(8,128)(2,1)}, u32[]{:S(2)}) copy-start(bf16[256,3072]{1,0:T(8,128)(2,1)} %cot_hbm.3) | copy-start | bytes 4718596
  0.6 23.9 %copy-start.5 = (s32[32]{0:T(128)S(1)}, s32[32]{0:T(128)}, u32[]{:S(2)}) copy-start(s32[32]{0:T(128)} %param.15) | copy-start | bytes 388
  3.9 36.6 %all-to-all-start = ((bf16[16,105,128]{2,1,0:T(8,128)(2,1)}), bf16[16,105,128]{2,1,0:T(8,128)(2,1)S(1)}, u32[]{:S(2)}, u32[]{:S(2)}) async-start(bf16[16,105,128]{2,1,0:T(8,128)(2,1)} %pieces.1), calls=%async_computation | async-start | bytes 917504 | tf_op jit(solution)/shard_map/all_to_all | solution.py:396
  19.7 7.4 %collective-permute-start.1 = (bf16[256,3072]{1,0:T(8,128)(2,1)S(1)}, bf16[256,3072]{1,0:T(8,128)(2,1)}, u32[]{:S(2)}, u32[]{:S(2)}) collective-permute-start(bf16[256,3072]{1,0:T(8,128)(2,1)S(1)} %copy-done.1), channel_id=1, source_target_pairs={{0,32},{32,0},{1,33},{33,1},{2,34},{34,2},{3,35},{35,3},{4,36},{36... | collective-permute-start | bytes 4718600 | tf_op jit(solution)/shard_map/ppermute | solution.py:41
  22.6 4.5 %collective-permute-start = (bf16[256,1536]{1,0:T(8,128)(2,1)}, bf16[256,1536]{1,0:T(8,128)(2,1)}, u32[]{:S(2)}, u32[]{:S(2)}) collective-permute-start(bf16[256,1536]{1,0:T(8,128)(2,1)} %rows_hbm.3), channel_id=1, source_target_pairs={{0,32},{32,0},{1,33},{33,1},{2,34},{34,2},{3,35},{35,3},{4,36},{36... | collective-permute-start | bytes 2359304 | tf_op jit(solution)/shard_map/ppermute | solution.py:41
  41.7 25.0 %all-to-all-start.1 = ((bf16[16,156,128]{2,1,0:T(8,128)(2,1)}), bf16[16,156,128]{2,1,0:T(8,128)(2,1)S(1)}, u32[]{:S(2)}, u32[]{:S(2)}) async-start(bf16[16,156,128]{2,1,0:T(8,128)(2,1)} %get-tuple-element.32), calls=%async_computation.1 | async-start | bytes 1310720 | tf_op jit(solution)/shard_map/all_to_all | solution.py:413
  48.4 18.1 %collective-permute-start.4 = (bf16[16,24,384]{2,1,0:T(8,128)(2,1)S(1)}, bf16[16,24,384]{2,1,0:T(8,128)(2,1)S(1)}, u32[]{:S(2)}, u32[]{:S(2)}) collective-permute-start(bf16[16,24,384]{2,1,0:T(8,128)(2,1)S(1)} %get-tuple-element.44), channel_id=1, source_target_pairs={{0,192},{1,193},{2,194},{3,195},{4,196},{5,197},{6,198},{7,199},{8... | collective-permute-start | bytes 884744 | tf_op jit(solution)/shard_map/ppermute | solution.py:414
  52.9 13.6 %collective-permute-start.3 = (bf16[16,24,384]{2,1,0:T(8,128)(2,1)S(1)}, bf16[16,24,384]{2,1,0:T(8,128)(2,1)S(1)}, u32[]{:S(2)}, u32[]{:S(2)}) collective-permute-start(bf16[16,24,384]{2,1,0:T(8,128)(2,1)S(1)} %get-tuple-element.44), channel_id=1, source_target_pairs={{0,128},{1,129},{2,130},{3,131},{4,132},{5,133},{6,134},{7,135},{8... | collective-permute-start | bytes 884744 | tf_op jit(solution)/shard_map/ppermute | solution.py:414
  55.4 11.3 %collective-permute-start.2 = (bf16[16,24,384]{2,1,0:T(8,128)(2,1)S(1)}, bf16[16,24,384]{2,1,0:T(8,128)(2,1)S(1)}, u32[]{:S(2)}, u32[]{:S(2)}) collective-permute-start(bf16[16,24,384]{2,1,0:T(8,128)(2,1)S(1)} %get-tuple-element.44), channel_id=1, source_target_pairs={{0,64},{1,65},{2,66},{3,67},{4,68},{5,69},{6,70},{7,71},{8,72},{9,... | collective-permute-start | bytes 884744 | tf_op jit(solution)/shard_map/ppermute | solution.py:414
  66.7 7.7 %copy-start = (bf16[16,156,128]{2,1,0:T(8,128)(2,1)}, bf16[16,156,128]{2,1,0:T(8,128)(2,1)S(1)}, u32[]{:S(2)}) copy-start(bf16[16,156,128]{2,1,0:T(8,128)(2,1)S(1)} %all-to-all-done.1.got_hbm) | copy-start | bytes 1916932
  67.0 16.5 %collective-permute-start.5 = (bf16[16,156,128]{2,0,1:T(8,128)(2,1)S(1)}, bf16[16,156,128]{2,0,1:T(8,128)(2,1)S(1)}, u32[]{:S(2)}, u32[]{:S(2)}) collective-permute-start(bf16[16,156,128]{2,0,1:T(8,128)(2,1)S(1)} %copy.18), channel_id=1, source_target_pairs={{0,32},{32,0},{1,33},{33,1},{2,34},{34,2},{3,35},{35,3},{4,36},{36... | collective-permute-start | bytes 1916936 | tf_op jit(solution)/shard_map/ppermute | solution.py:41
  74.4 16.7 %copy-start.2 = (bf16[4,16,24,384]{3,2,1,0:T(8,128)(2,1)}, bf16[4,16,24,384]{3,2,1,0:T(8,128)(2,1)S(1)}, u32[]{:S(2)}) copy-start(bf16[4,16,24,384]{3,2,1,0:T(8,128)(2,1)S(1)} %pad_maximum_fusion.t0) | copy-start | bytes 3538948
  74.4 31.2 %collective-permute-start.8 = (bf16[4,16,24,384]{3,2,1,0:T(8,128)(2,1)S(1)}, bf16[4,16,24,384]{3,2,1,0:T(8,128)(2,1)}, u32[]{:S(2)}, u32[]{:S(2)}) collective-permute-start(bf16[4,16,24,384]{3,2,1,0:T(8,128)(2,1)S(1)} %pad_maximum_fusion.t0), channel_id=1, source_target_pairs={{0,257},{1,256},{2,259},{3,258},{4,261},{5,260},{6,263},{7,262},{8... | collective-permute-start | bytes 3538952 | tf_op jit(solution)/shard_map/ppermute | solution.py:417
  78.5 27.1 %collective-permute-start.7 = (bf16[4,16,24,384]{3,2,1,0:T(8,128)(2,1)S(1)}, bf16[4,16,24,384]{3,2,1,0:T(8,128)(2,1)S(1)}, u32[]{:S(2)}, u32[]{:S(2)}) collective-permute-start(bf16[4,16,24,384]{3,2,1,0:T(8,128)(2,1)S(1)} %pad_maximum_fusion.t0), channel_id=1, source_target_pairs={{0,256},{1,257},{2,258},{3,259},{4,260},{5,261},{6,262},{7,263},{8... | collective-permute-start | bytes 3538952 | tf_op jit(solution)/shard_map/ppermute | solution.py:417
  81.0 27.2 %collective-permute-start.6 = (bf16[4,16,24,384]{3,2,1,0:T(8,128)(2,1)S(1)}, bf16[4,16,24,384]{3,2,1,0:T(8,128)(2,1)}, u32[]{:S(2)}, u32[]{:S(2)}) collective-permute-start(bf16[4,16,24,384]{3,2,1,0:T(8,128)(2,1)S(1)} %pad_maximum_fusion.t0), channel_id=1, source_target_pairs={{0,1},{1,0},{2,3},{3,2},{4,5},{5,4},{6,7},{7,6},{8,9},{9,8},{10,11... | collective-permute-start | bytes 3538952 | tf_op jit(solution)/shard_map/ppermute | solution.py:417
  91.1 32.7 %all-to-all-start.2 = ((bf16[16,144,128]{2,1,0:T(8,128)(2,1)}), bf16[16,144,128]{2,1,0:T(8,128)(2,1)S(1)}, u32[]{:S(2)}, u32[]{:S(2)}) async-start(bf16[16,144,128]{2,1,0:T(8,128)(2,1)} %get-tuple-element.51), calls=%async_computation.2 | async-start | bytes 1179648 | tf_op jit(solution)/shard_map/all_to_all | solution.py:423
  105.6 2.5 %copy-start.6 = (bf16[4,16,24,384]{3,2,1,0:T(8,128)(2,1)}, bf16[4,16,24,384]{3,2,1,0:T(8,128)(2,1)S(1)}, u32[]{:S(2)}) copy-start(bf16[4,16,24,384]{3,2,1,0:T(8,128)(2,1)S(1)} %collective-permute-done.7.t2) | copy-start | bytes 3538948
  118.8 5.2 %collective-permute-start.9 = (bf16[256,1536]{1,0:T(8,128)(2,1)}, bf16[256,1536]{1,0:T(8,128)(2,1)S(1)}, u32[]{:S(2)}, u32[]{:S(2)}) collective-permute-start(bf16[256,1536]{1,0:T(8,128)(2,1)} %get-tuple-element.49), channel_id=1, source_target_pairs={{0,32},{32,0},{1,33},{33,1},{2,34},{34,2},{3,35},{35,3},{4,36},{36... | collective-permute-start | bytes 2359304 | tf_op jit(solution)/shard_map/ppermute | solution.py:41
  121.9 4.4 %collective-permute-start.10 = (bf16[256,1536]{1,0:T(8,128)(2,1)}, bf16[256,1536]{1,0:T(8,128)(2,1)S(1)}, u32[]{:S(2)}, u32[]{:S(2)}) collective-permute-start(bf16[256,1536]{1,0:T(8,128)(2,1)} %get-tuple-element.50), channel_id=1, source_target_pairs={{0,32},{32,0},{1,33},{33,1},{2,34},{34,2},{3,35},{35,3},{4,36},{36... | collective-permute-start | bytes 2359304 | tf_op jit(solution)/shard_map/ppermute | solution.py:41
  124.0 21.7 %copy-start.3 = (bf16[256,1536]{1,0:T(8,128)(2,1)}, bf16[256,1536]{1,0:T(8,128)(2,1)S(1)}, u32[]{:S(2)}) copy-start(bf16[256,1536]{1,0:T(8,128)(2,1)S(1)} %collective-permute-done.9.mixed_rest_hbm) | copy-start | bytes 2359300
  126.3 19.4 %copy-start.4 = (bf16[256,1536]{1,0:T(8,128)(2,1)}, bf16[256,1536]{1,0:T(8,128)(2,1)S(1)}, u32[]{:S(2)}) copy-start(bf16[256,1536]{1,0:T(8,128)(2,1)S(1)} %collective-permute-done.10.dx_rest_hbm) | copy-start | bytes 2359300
  140.1 8.6 %collective-permute-start.11 = (f32[72,128]{1,0:T(8,128)S(1)}, f32[72,128]{1,0:T(8,128)S(1)}, u32[]{:S(2)}, u32[]{:S(2)}) collective-permute-start(f32[72,128]{1,0:T(8,128)S(1)} %convert_reduce_fusion), channel_id=1, source_target_pairs={{0,32},{32,0},{1,33},{33,1},{2,34},{34,2},{3,35},{35,3},{4,36},{36... | collective-permute-start | bytes 110600 | tf_op jit(solution)/shard_map/ppermute | solution.py:41

commit v6 on v5

--- a/solution.py
+++ b/solution.py
@@ -150,7 +150,7 @@
     first = core[0] == 0
     for s in range(16):
         mine, theirs = got[s].astype(F32), got_other[s].astype(F32)
-        wide[s] = mine
+        wide[s] = mine + theirs
         parts[0] = jnp.where(first, mine, theirs)
         parts[1] = jnp.where(first, theirs, mine)
         j, yl = s // 2, s % 2
@@ -309,10 +309,11 @@
     weight = codes[:, pl.ds(col, 384)].astype(F32) * amax[...].astype(F32)
     weight = jnp.where(yh == 0, weight[:24], weight[24:]).astype(BF).astype(F32)
     gates = gate[:, pl.ds(pl.multiple_of(j * 384, 128), 384)].astype(F32)
+    gates = jnp.where(core == 0, gates[:4], gates[4:])
     for k in range(3):
         lanes = slice(128 * k, 128 * k + 128)
         wide[24 * k : 24 * k + 24] = weight[:, lanes]
-        wide[72 + 8 * k : 80 + 8 * k] = gates[:, lanes]
+        wide[72 + 4 * k : 76 + 4 * k] = gates[:, lanes]
 
     i = 2 * j + core
 
@@ -321,8 +322,8 @@
         col = lax.broadcasted_iota(jnp.int32, (n, size), 1)
         return jnp.where(col == row + n * i, 1.0, 0.0).astype(BF)
 
-    wide[96:99] = nn(pick(3, 48), down[...])
-    wide[99:105] = nn(pick(6, 96), up[...])
+    wide[84:87] = nn(pick(3, 48), down[...])
+    wide[87:93] = nn(pick(6, 96), up[...])
     for d in range(16):
         out[d] = wide[...].astype(BF)
 
@@ -330,25 +331,26 @@
 def pieces(at, codes, amax, down, up, gate):
     return pl.pallas_call(
         pieces_kernel,
-        out_shape=jax.ShapeDtypeStruct((16, 105, 128), BF),
+        out_shape=jax.ShapeDtypeStruct((16, 93, 128), BF),
         in_specs=[pl.BlockSpec(memory_space=pltpu.SMEM)] + vmem(5),
         out_specs=vmem(1)[0],
-        scratch_shapes=[pltpu.VMEM((105, 128), F32)],
+        scratch_shapes=[pltpu.VMEM((93, 128), F32)],
         compiler_params=PARAMS,
         name="pieces",
     )(at, codes, amax, down, up, gate)
 
 
-def spread_kernel(line, features, out_hbm, weight_hbm, wide, maps, pair, out, weight, sems):
+def spread_kernel(line, features, out_hbm, weight_hbm, wide, maps, blocks, pair, out, weight, sems):
     for k in range(3):
         weight[:, :, 128 * k : 128 * k + 128] = line[:, 24 * k : 24 * k + 24]
     copies = fetch([(weight, weight_hbm)], sems.at[pl.ds(0, 1)])
     wide[...] = line[...].astype(F32)
     for z in range(16):
-        maps[9 * z : 9 * z + 9] = wide[z, 96:105]
+        maps[9 * z : 9 * z + 9] = wide[z, 84:93]
+        for k in range(3):
+            blocks[k, 4 * z : 4 * z + 4] = wide[z, 72 + 4 * k : 76 + 4 * k]
     for k in range(3):
-        block = wide[:, 72 + 8 * k : 80 + 8 * k].reshape(128, 128).astype(BF)
-        part = nn(features[...], block)
+        part = nn(features[...], blocks[k].astype(BF))
         high = part.astype(BF).astype(F32)
         for h, v in enumerate((high, part - high)):
             for c in range(2):
@@ -366,7 +368,7 @@
 
 
 def spread(line, features):
-    shapes = ((16, 105, 128), (16, 156, 128), (16, 24, 384))
+    shapes = ((16, 93, 128), (16, 156, 128), (16, 24, 384))
     return pl.pallas_call(
         spread_kernel,
         out_shape=tuple(jax.ShapeDtypeStruct(s, BF) for s in shapes[1:]),
@@ -375,6 +377,7 @@
         scratch_shapes=[
             pltpu.VMEM(shapes[0], F32),
             pltpu.VMEM((144, 128), F32),
+            pltpu.VMEM((3, 64, 128), F32),
             pltpu.VMEM((16, 12, 128), F32),
             pltpu.VMEM(shapes[1], BF),
             pltpu.VMEM(shapes[2], BF),
@@ -408,8 +411,9 @@
     steps = lax.dynamic_slice(timesteps.reshape(16, 2), (0, z // 8), (16, 1))
     phase = steps.astype(F32) * frequency[None, :]
     features = jnp.concatenate([jnp.cos(phase), jnp.sin(phase)], axis=1).astype(BF)
-    features = lax.dynamic_slice(features.reshape(16, 16, 2, 8), (0, 0, yl, 0), (16, 16, 1, 8))
-    spread_out, line = spread(line, features.reshape(16, 128))
+    features = features.reshape(16, 16, 2, 2, 4)
+    features = lax.dynamic_slice(features, (0, 0, yl, core, 0), (16, 16, 1, 1, 4))
+    spread_out, line = spread(line, features.reshape(16, 64))
     got = lax.all_to_all(spread_out, PLANE, 0, 0, tiled=True)
     first = [line] + [lax.ppermute(line, AXES, plane_pairs(k, False)) for k in (1, 2, 3)]
     got, first = lax.optimization_barrier((got, first))

time: 151 us -> 151 us (level)
  starting transfers between devices: 68.9 us -> 66.8 us
  waiting for transfers between devices: 37.3 us -> 39 us
    all_to_all x1, starting transfers between devices: 15.7 us -> 9.54 us  [per_device(): line = lax.all_to_all(line, 'z', 0, 0, tiled=True)]
    ppermute x6, starting transfers between devices: 22.6 us -> 27.1 us  [other_core(): return lax.ppermute(v, 'core', [(0, 1), (1, 0)])]
  transfers between devices with their start and end apart: 15 -> 15, of which waited for: 8 -> 8; matrix products, arithmetic and copies ran while one was open for 2% -> 2% of each run, Pallas kernels for 14% -> 15%
where the time goes in v6:
time: 151 us; the launch traced here: 150 us
  starting transfers between devices  66.8 us (44%)
  waiting for transfers between devices  39 us (26%)
  Pallas kernels  23.5 us (16%)
  blocking collectives  13.6 us (9%)
  other arithmetic  3.6 us (2%)
  local copies, waits for them, and re-layouts  1.63 us (1%)
  between operations  1.63 us (1%)
    ppermute x6, starting transfers between devices, other_core(): return lax.ppermute(v, 'core', [(0, 1), (1, 0)])  27.1 us
    all_to_all x1, waiting for transfers between devices, per_device(): line = lax.all_to_all(line, 'z', 0, 0, tiled=True)  14.8 us
    all_to_all x1, blocking collectives, per_device(): terms = lax.all_to_all(terms, PLANE, 0, 0, tiled=True).astype(F32).sum(0)  13.6 us
    ppermute x3, waiting for transfers between devices, per_device(): lax.ppermute(first, AXES, plane_pairs(k, True))  10.8 us
    pallas_call x1, Pallas kernels, products(): pl.pallas_call(products_kernel, out_shape=(half, half, jax.ShapeDtypeStru...  10.7 us
    ppermute x3, waiting for transfers between devices, per_device(): lax.ppermute(line, AXES, plane_pairs(k, False))  9.71 us
    all_to_all x1, starting transfers between devices, per_device(): line = lax.all_to_all(line, 'z', 0, 0, tiled=True)  9.54 us
    ppermute x3, starting transfers between devices, per_device(): lax.ppermute(first, AXES, plane_pairs(k, True))  8.98 us
  transfers between devices with their start and end apart: 15, of which 8 were waited for; matrix products, arithmetic and copies ran while one was open for 2% of the time, Pallas kernels for 15%

profile of v6, /device:TPU:1, one launch (start us, length us, event | category | flops | bytes accessed | tf_op | source)
XLA Modules:
  0.0 149.8 jit_solution(9082461661421671150)
XLA Ops:
  0.6 8.8 %collective-permute-start.1 = (bf16[256,3072]{1,0:T(8,128)(2,1)}, bf16[256,3072]{1,0:T(8,128)(2,1)S(1)}, u32[]{:S(2)}, u32[]{:S(2)}) collective-permute-start(bf16[256,3072]{1,0:T(8,128)(2,1)} %cot_hbm.3), channel_id=1, source_target_pairs={{0,32},{32,0},{1,33},{33,1},{2,34},{34,2},{3,35},{35,3},{4,36},{36... | collective-permute-start | bytes 4718600 | tf_op jit(solution)/shard_map/ppermute | solution.py:41
  10.7 1.9 %pieces.1 = bf16[16,93,128]{2,1,0:T(8,128)(2,1)} custom-call(s32[3]{0:T(128)} %pad_add_fusion.1.at, bf16[48,3072]{1,0:T(8,128)(2,1)} %codes.1, bf16[1,1]{1,0:T(2,128)(2,1)} %bitcast.20.amax, bf16[48,128]{1,0:T(8,128)(2,1)} %down.1, bf16[96,128]{1,0:T(8,128)(2,1)} %bitcast.29, bf16[8,3072]{1,0:T(8,128)(2,1)} %gate.1), custom_call_target="tpu_custom_call" | custom-call | tf_op jit(solution)/shard_map/pieces/pallas_call | solution.py:332
  12.6 9.5 %all-to-all-start = ((bf16[16,93,128]{2,1,0:T(8,128)(2,1)}), bf16[16,93,128]{2,1,0:T(8,128)(2,1)S(1)}, u32[]{:S(2)}, u32[]{:S(2)}) async-start(bf16[16,93,128]{2,1,0:T(8,128)(2,1)} %pieces.1), calls=%async_computation | async-start | bytes 786432 | tf_op jit(solution)/shard_map/all_to_all | solution.py:399
  22.1 2.2 %collective-permute-start = (bf16[256,1536]{1,0:T(8,128)(2,1)}, bf16[256,1536]{1,0:T(8,128)(2,1)}, u32[]{:S(2)}, u32[]{:S(2)}) collective-permute-start(bf16[256,1536]{1,0:T(8,128)(2,1)} %rows_hbm.3), channel_id=1, source_target_pairs={{0,32},{32,0},{1,33},{33,1},{2,34},{34,2},{3,35},{35,3},{4,36},{36... | collective-permute-start | bytes 2359304 | tf_op jit(solution)/shard_map/ppermute | solution.py:41
  25.3 1.3 collective-permute-done.rows_other_hbm
  26.6 14.8 %all-to-all-done.line = bf16[16,93,128]{2,1,0:T(8,128)(2,1)S(1)} async-done(((bf16[16,93,128]{2,1,0:T(8,128)(2,1)}), bf16[16,93,128]{2,1,0:T(8,128)(2,1)S(1)}, u32[]{:S(2)}, u32[]{:S(2)}) %all-to-all-start) | async-done | bytes 380960 | tf_op jit(solution)/shard_map/all_to_all | solution.py:399
  41.5 1.4 spread.1
  42.8 6.8 %all-to-all-start.1 = ((bf16[16,156,128]{2,1,0:T(8,128)(2,1)}), bf16[16,156,128]{2,1,0:T(8,128)(2,1)S(1)}, u32[]{:S(2)}, u32[]{:S(2)}) async-start(bf16[16,156,128]{2,1,0:T(8,128)(2,1)} %get-tuple-element.32), calls=%async_computation.1 | async-start | bytes 1310720 | tf_op jit(solution)/shard_map/all_to_all | solution.py:417
  49.6 4.5 %collective-permute-start.4 = (bf16[16,24,384]{2,1,0:T(8,128)(2,1)S(1)}, bf16[16,24,384]{2,1,0:T(8,128)(2,1)S(1)}, u32[]{:S(2)}, u32[]{:S(2)}) collective-permute-start(bf16[16,24,384]{2,1,0:T(8,128)(2,1)S(1)} %get-tuple-element.44), channel_id=1, source_target_pairs={{0,192},{1,193},{2,194},{3,195},{4,196},{5,197},{6,198},{7,199},{8... | collective-permute-start | bytes 884744 | tf_op jit(solution)/shard_map/ppermute | solution.py:418
  54.1 2.5 %collective-permute-start.3 = (bf16[16,24,384]{2,1,0:T(8,128)(2,1)S(1)}, bf16[16,24,384]{2,1,0:T(8,128)(2,1)S(1)}, u32[]{:S(2)}, u32[]{:S(2)}) collective-permute-start(bf16[16,24,384]{2,1,0:T(8,128)(2,1)S(1)} %get-tuple-element.44), channel_id=1, source_target_pairs={{0,128},{1,129},{2,130},{3,131},{4,132},{5,133},{6,134},{7,135},{8... | collective-permute-start | bytes 884744 | tf_op jit(solution)/shard_map/ppermute | solution.py:418
  56.6 2.0 %collective-permute-start.2 = (bf16[16,24,384]{2,1,0:T(8,128)(2,1)S(1)}, bf16[16,24,384]{2,1,0:T(8,128)(2,1)S(1)}, u32[]{:S(2)}, u32[]{:S(2)}) collective-permute-start(bf16[16,24,384]{2,1,0:T(8,128)(2,1)S(1)} %get-tuple-element.44), channel_id=1, source_target_pairs={{0,64},{1,65},{2,66},{3,67},{4,68},{5,69},{6,70},{7,71},{8,72},{9,... | collective-permute-start | bytes 884744 | tf_op jit(solution)/shard_map/ppermute | solution.py:418
  58.6 8.8 %collective-permute-done.4 = bf16[16,24,384]{2,1,0:T(8,128)(2,1)S(1)} collective-permute-done((bf16[16,24,384]{2,1,0:T(8,128)(2,1)S(1)}, bf16[16,24,384]{2,1,0:T(8,128)(2,1)S(1)}, u32[]{:S(2)}, u32[]{:S(2)}) %collective-permute-start.4) | collective-permute-done | bytes 294944 | tf_op jit(solution)/shard_map/ppermute | solution.py:418
  67.4 0.9 collective-permute-done.2
  68.6 6.3 %collective-permute-start.5 = (bf16[16,156,128]{2,0,1:T(8,128)(2,1)S(1)}, bf16[16,156,128]{2,0,1:T(8,128)(2,1)S(1)}, u32[]{:S(2)}, u32[]{:S(2)}) collective-permute-start(bf16[16,156,128]{2,0,1:T(8,128)(2,1)S(1)} %copy.18), channel_id=1, source_target_pairs={{0,32},{32,0},{1,33},{33,1},{2,34},{34,2},{3,35},{35,3},{4,36},{36... | collective-permute-start | bytes 1916936 | tf_op jit(solution)/shard_map/ppermute | solution.py:41
  75.1 4.1 %collective-permute-start.8 = (bf16[4,16,24,384]{3,2,1,0:T(8,128)(2,1)S(1)}, bf16[4,16,24,384]{3,2,1,0:T(8,128)(2,1)}, u32[]{:S(2)}, u32[]{:S(2)}) collective-permute-start(bf16[4,16,24,384]{3,2,1,0:T(8,128)(2,1)S(1)} %pad_maximum_fusion.t0), channel_id=1, source_target_pairs={{0,257},{1,256},{2,259},{3,258},{4,261},{5,260},{6,263},{7,262},{8... | collective-permute-start | bytes 3538952 | tf_op jit(solution)/shard_map/ppermute | solution.py:421
  79.2 2.5 %collective-permute-start.7 = (bf16[4,16,24,384]{3,2,1,0:T(8,128)(2,1)S(1)}, bf16[4,16,24,384]{3,2,1,0:T(8,128)(2,1)}, u32[]{:S(2)}, u32[]{:S(2)}) collective-permute-start(bf16[4,16,24,384]{3,2,1,0:T(8,128)(2,1)S(1)} %pad_maximum_fusion.t0), channel_id=1, source_target_pairs={{0,256},{1,257},{2,258},{3,259},{4,260},{5,261},{6,262},{7,263},{8... | collective-permute-start | bytes 3538952 | tf_op jit(solution)/shard_map/ppermute | solution.py:421
  81.7 2.4 %collective-permute-start.6 = (bf16[4,16,24,384]{3,2,1,0:T(8,128)(2,1)S(1)}, bf16[4,16,24,384]{3,2,1,0:T(8,128)(2,1)}, u32[]{:S(2)}, u32[]{:S(2)}) collective-permute-start(bf16[4,16,24,384]{3,2,1,0:T(8,128)(2,1)S(1)} %pad_maximum_fusion.t0), channel_id=1, source_target_pairs={{0,1},{1,0},{2,3},{3,2},{4,5},{5,4},{6,7},{7,6},{8,9},{9,8},{10,11... | collective-permute-start | bytes 3538952 | tf_op jit(solution)/shard_map/ppermute | solution.py:421
  84.1 1.0 copy.19.got_other_hbm
  85.1 6.7 %adapter_terms.1 = (bf16[256,128]{1,0:T(8,128)(2,1)}, bf16[256,128]{1,0:T(8,128)(2,1)}, bf16[256,128]{1,0:T(8,128)(2,1)}, f32[1,1536]{1,0:T(1,128)}, f32[1,1536]...) custom-call(s32[1]{0:T(128)} %bitcast.core, ...), custom_call_target="tpu_custom_call" | custom-call | flops 1400000000 | bytes 200000000 | tf_op jit(solution)/shard_map/adapter_terms/pallas_call | solution.py:276
  91.8 5.4 %all-to-all-start.2 = ((bf16[16,144,128]{2,1,0:T(8,128)(2,1)}), bf16[16,144,128]{2,1,0:T(8,128)(2,1)S(1)}, u32[]{:S(2)}, u32[]{:S(2)}) async-start(bf16[16,144,128]{2,1,0:T(8,128)(2,1)} %get-tuple-element.51), calls=%async_computation.2 | async-start | bytes 1179648 | tf_op jit(solution)/shard_map/all_to_all | solution.py:427
  97.4 0.7 pad_add_fusion.at
  98.0 8.3 %collective-permute-done.8.t3 = bf16[4,16,24,384]{3,2,1,0:T(8,128)(2,1)} collective-permute-done((bf16[4,16,24,384]{3,2,1,0:T(8,128)(2,1)S(1)}, bf16[4,16,24,384]{3,2,1,0:T(8,128)(2,1)}, u32[]{:S(2)}, u32[]{:S(2)}) %collective-permute-start.8) | collective-permute-done | bytes 1179680 | tf_op jit(solution)/shard_map/ppermute | solution.py:421
  106.3 2.5 %collective-permute-done.6.t1 = bf16[4,16,24,384]{3,2,1,0:T(8,128)(2,1)} collective-permute-done((bf16[4,16,24,384]{3,2,1,0:T(8,128)(2,1)S(1)}, bf16[4,16,24,384]{3,2,1,0:T(8,128)(2,1)}, u32[]{:S(2)}, u32[]{:S(2)}) %collective-permute-start.6) | collective-permute-done | bytes 1179680 | tf_op jit(solution)/shard_map/ppermute | solution.py:421
  108.8 10.7 %products.1 = (bf16[256,1536]{1,0:T(8,128)(2,1)}, bf16[256,1536]{1,0:T(8,128)(2,1)}, bf16[256,3072]{1,0:T(8,128)(2,1)}, f32[256,1536]{1,0:T(8,128)}) custom-call(s32[32]{0:T(128)} %pad_add_fusion.at, s32[1]{0:T(128)} %bitcast.core, bf16[256,128]{1,0:T(8,128)(2,1)} %get-tuple-element.37.low_other, f32[1,1536]{1,0:T(1,128)} %get-tuple-element.38.gate_other, ...), custom_call_target="tpu_custom_call" | custom-call | flops 4831838208 | bytes 200000000 | tf_op jit(solution)/shard_map/products/pallas_call | solution.py:226
  119.5 3.1 %collective-permute-start.9 = (bf16[256,1536]{1,0:T(8,128)(2,1)}, bf16[256,1536]{1,0:T(8,128)(2,1)S(1)}, u32[]{:S(2)}, u32[]{:S(2)}) collective-permute-start(bf16[256,1536]{1,0:T(8,128)(2,1)} %get-tuple-element.49), channel_id=1, source_target_pairs={{0,32},{32,0},{1,33},{33,1},{2,34},{34,2},{3,35},{35,3},{4,36},{36... | collective-permute-start | bytes 2359304 | tf_op jit(solution)/shard_map/ppermute | solution.py:41
  122.5 1.9 %collective-permute-start.10 = (bf16[256,1536]{1,0:T(8,128)(2,1)}, bf16[256,1536]{1,0:T(8,128)(2,1)S(1)}, u32[]{:S(2)}, u32[]{:S(2)}) collective-permute-start(bf16[256,1536]{1,0:T(8,128)(2,1)} %get-tuple-element.50), channel_id=1, source_target_pairs={{0,32},{32,0},{1,33},{33,1},{2,34},{34,2},{3,35},{35,3},{4,36},{36... | collective-permute-start | bytes 2359304 | tf_op jit(solution)/shard_map/ppermute | solution.py:41
  124.6 2.3 %collective-permute-done.10.dx_rest_hbm = bf16[256,1536]{1,0:T(8,128)(2,1)S(1)} collective-permute-done((bf16[256,1536]{1,0:T(8,128)(2,1)}, bf16[256,1536]{1,0:T(8,128)(2,1)S(1)}, u32[]{:S(2)}, u32[]{:S(2)}) %collective-permute-start.10) | collective-permute-done | bytes 786464 | tf_op jit(solution)/shard_map/ppermute | solution.py:41
  127.0 13.6 %all_to_all.20 = bf16[16,72,128]{2,1,0:T(8,128)(2,1)S(1)} all-to-all(bf16[16,72,128]{2,1,0:T(8,128)(2,1)S(1)} %bitcast.22), channel_id=1, replica_groups=mesh['yh'=2,'x'=4,'core'=2,'z'=16,'yl'=2] {'yh','x','yl'}, dimensions={0} | all-to-all | bytes 589824 | tf_op jit(solution)/shard_map/all_to_all | solution.py:439
  140.7 4.9 %collective-permute-start.11 = (f32[72,128]{1,0:T(8,128)S(1)}, f32[72,128]{1,0:T(8,128)S(1)}, u32[]{:S(2)}, u32[]{:S(2)}) collective-permute-start(f32[72,128]{1,0:T(8,128)S(1)} %convert_reduce_fusion), channel_id=1, source_target_pairs={{0,32},{32,0},{1,33},{33,1},{2,34},{34,2},{3,35},{35,3},{4,36},{36... | collective-permute-start | bytes 110600 | tf_op jit(solution)/shard_map/ppermute | solution.py:41
  145.6 2.9 %finish.1 = (bf16[256,3072]{1,0:T(8,128)(2,1)}, bf16[256,1536]{1,0:T(8,128)(2,1)}) custom-call(s32[1]{0:T(128)} %bitcast.core, bf16[256,3072]{1,0:T(8,128)(2,1)} %get-tuple-element.48.mixed_in, bf16[256,1536]{1,0:T(8,128)(2,1)} %copy-done.3, f32[256,1536]{1,0:T(8,128)} %get-tuple-element.53.dx_own_hbm, ...), custom_call_target="tpu_custom_call", output_to_operand_aliasing={{0}: (1, {})} | custom-call | flops 1000000 | bytes 7000000 | tf_op jit(solution)/shard_map/finish/pallas_call | solution.py:252
  148.6 0.6 maximum_multiply_fusion
  149.2 0.6 fusion.2
  (37 shorter events, 2.4 us)
Async XLA Ops:
  0.6 23.7 %copy-start.5 = (s32[32]{0:T(128)S(1)}, s32[32]{0:T(128)}, u32[]{:S(2)}) copy-start(s32[32]{0:T(128)} %param.15) | copy-start | bytes 388
  0.6 40.8 %collective-permute-start.1 = (bf16[256,3072]{1,0:T(8,128)(2,1)}, bf16[256,3072]{1,0:T(8,128)(2,1)S(1)}, u32[]{:S(2)}, u32[]{:S(2)}) collective-permute-start(bf16[256,3072]{1,0:T(8,128)(2,1)} %cot_hbm.3), channel_id=1, source_target_pairs={{0,32},{32,0},{1,33},{33,1},{2,34},{34,2},{3,35},{35,3},{4,36},{36... | collective-permute-start | bytes 4718600 | tf_op jit(solution)/shard_map/ppermute | solution.py:41
  12.6 28.9 %all-to-all-start = ((bf16[16,93,128]{2,1,0:T(8,128)(2,1)}), bf16[16,93,128]{2,1,0:T(8,128)(2,1)S(1)}, u32[]{:S(2)}, u32[]{:S(2)}) async-start(bf16[16,93,128]{2,1,0:T(8,128)(2,1)} %pieces.1), calls=%async_computation | async-start | bytes 786432 | tf_op jit(solution)/shard_map/all_to_all | solution.py:399
  22.1 4.5 %collective-permute-start = (bf16[256,1536]{1,0:T(8,128)(2,1)}, bf16[256,1536]{1,0:T(8,128)(2,1)}, u32[]{:S(2)}, u32[]{:S(2)}) collective-permute-start(bf16[256,1536]{1,0:T(8,128)(2,1)} %rows_hbm.3), channel_id=1, source_target_pairs={{0,32},{32,0},{1,33},{33,1},{2,34},{34,2},{3,35},{35,3},{4,36},{36... | collective-permute-start | bytes 2359304 | tf_op jit(solution)/shard_map/ppermute | solution.py:41
  41.5 27.1 %copy-start.1 = (bf16[256,3072]{1,0:T(8,128)(2,1)}, bf16[256,3072]{1,0:T(8,128)(2,1)S(1)}, u32[]{:S(2)}) copy-start(bf16[256,3072]{1,0:T(8,128)(2,1)S(1)} %collective-permute-done.1.cot_other_hbm) | copy-start | bytes 4718596
  42.8 25.5 %all-to-all-start.1 = ((bf16[16,156,128]{2,1,0:T(8,128)(2,1)}), bf16[16,156,128]{2,1,0:T(8,128)(2,1)S(1)}, u32[]{:S(2)}, u32[]{:S(2)}) async-start(bf16[16,156,128]{2,1,0:T(8,128)(2,1)} %get-tuple-element.32), calls=%async_computation.1 | async-start | bytes 1310720 | tf_op jit(solution)/shard_map/all_to_all | solution.py:417
  49.6 17.8 %collective-permute-start.4 = (bf16[16,24,384]{2,1,0:T(8,128)(2,1)S(1)}, bf16[16,24,384]{2,1,0:T(8,128)(2,1)S(1)}, u32[]{:S(2)}, u32[]{:S(2)}) collective-permute-start(bf16[16,24,384]{2,1,0:T(8,128)(2,1)S(1)} %get-tuple-element.44), channel_id=1, source_target_pairs={{0,192},{1,193},{2,194},{3,195},{4,196},{5,197},{6,198},{7,199},{8... | collective-permute-start | bytes 884744 | tf_op jit(solution)/shard_map/ppermute | solution.py:418
  54.1 13.3 %collective-permute-start.3 = (bf16[16,24,384]{2,1,0:T(8,128)(2,1)S(1)}, bf16[16,24,384]{2,1,0:T(8,128)(2,1)S(1)}, u32[]{:S(2)}, u32[]{:S(2)}) collective-permute-start(bf16[16,24,384]{2,1,0:T(8,128)(2,1)S(1)} %get-tuple-element.44), channel_id=1, source_target_pairs={{0,128},{1,129},{2,130},{3,131},{4,132},{5,133},{6,134},{7,135},{8... | collective-permute-start | bytes 884744 | tf_op jit(solution)/shard_map/ppermute | solution.py:418
  56.6 11.7 %collective-permute-start.2 = (bf16[16,24,384]{2,1,0:T(8,128)(2,1)S(1)}, bf16[16,24,384]{2,1,0:T(8,128)(2,1)S(1)}, u32[]{:S(2)}, u32[]{:S(2)}) collective-permute-start(bf16[16,24,384]{2,1,0:T(8,128)(2,1)S(1)} %get-tuple-element.44), channel_id=1, source_target_pairs={{0,64},{1,65},{2,66},{3,67},{4,68},{5,69},{6,70},{7,71},{8,72},{9,... | collective-permute-start | bytes 884744 | tf_op jit(solution)/shard_map/ppermute | solution.py:418
  68.3 6.7 %copy-start = (bf16[16,156,128]{2,1,0:T(8,128)(2,1)}, bf16[16,156,128]{2,1,0:T(8,128)(2,1)S(1)}, u32[]{:S(2)}) copy-start(bf16[16,156,128]{2,1,0:T(8,128)(2,1)S(1)} %all-to-all-done.1.got_hbm) | copy-start | bytes 1916932
  68.6 15.5 %collective-permute-start.5 = (bf16[16,156,128]{2,0,1:T(8,128)(2,1)S(1)}, bf16[16,156,128]{2,0,1:T(8,128)(2,1)S(1)}, u32[]{:S(2)}, u32[]{:S(2)}) collective-permute-start(bf16[16,156,128]{2,0,1:T(8,128)(2,1)S(1)} %copy.18), channel_id=1, source_target_pairs={{0,32},{32,0},{1,33},{33,1},{2,34},{34,2},{3,35},{35,3},{4,36},{36... | collective-permute-start | bytes 1916936 | tf_op jit(solution)/shard_map/ppermute | solution.py:41
  75.1 16.7 %copy-start.2 = (bf16[4,16,24,384]{3,2,1,0:T(8,128)(2,1)}, bf16[4,16,24,384]{3,2,1,0:T(8,128)(2,1)S(1)}, u32[]{:S(2)}) copy-start(bf16[4,16,24,384]{3,2,1,0:T(8,128)(2,1)S(1)} %pad_maximum_fusion.t0) | copy-start | bytes 3538948
  75.1 31.2 %collective-permute-start.8 = (bf16[4,16,24,384]{3,2,1,0:T(8,128)(2,1)S(1)}, bf16[4,16,24,384]{3,2,1,0:T(8,128)(2,1)}, u32[]{:S(2)}, u32[]{:S(2)}) collective-permute-start(bf16[4,16,24,384]{3,2,1,0:T(8,128)(2,1)S(1)} %pad_maximum_fusion.t0), channel_id=1, source_target_pairs={{0,257},{1,256},{2,259},{3,258},{4,261},{5,260},{6,263},{7,262},{8... | collective-permute-start | bytes 3538952 | tf_op jit(solution)/shard_map/ppermute | solution.py:421
  79.2 27.1 %collective-permute-start.7 = (bf16[4,16,24,384]{3,2,1,0:T(8,128)(2,1)S(1)}, bf16[4,16,24,384]{3,2,1,0:T(8,128)(2,1)}, u32[]{:S(2)}, u32[]{:S(2)}) collective-permute-start(bf16[4,16,24,384]{3,2,1,0:T(8,128)(2,1)S(1)} %pad_maximum_fusion.t0), channel_id=1, source_target_pairs={{0,256},{1,257},{2,258},{3,259},{4,260},{5,261},{6,262},{7,263},{8... | collective-permute-start | bytes 3538952 | tf_op jit(solution)/shard_map/ppermute | solution.py:421
  81.7 27.2 %collective-permute-start.6 = (bf16[4,16,24,384]{3,2,1,0:T(8,128)(2,1)S(1)}, bf16[4,16,24,384]{3,2,1,0:T(8,128)(2,1)}, u32[]{:S(2)}, u32[]{:S(2)}) collective-permute-start(bf16[4,16,24,384]{3,2,1,0:T(8,128)(2,1)S(1)} %pad_maximum_fusion.t0), channel_id=1, source_target_pairs={{0,1},{1,0},{2,3},{3,2},{4,5},{5,4},{6,7},{7,6},{8,9},{9,8},{10,11... | collective-permute-start | bytes 3538952 | tf_op jit(solution)/shard_map/ppermute | solution.py:421
  91.8 32.7 %all-to-all-start.2 = ((bf16[16,144,128]{2,1,0:T(8,128)(2,1)}), bf16[16,144,128]{2,1,0:T(8,128)(2,1)S(1)}, u32[]{:S(2)}, u32[]{:S(2)}) async-start(bf16[16,144,128]{2,1,0:T(8,128)(2,1)} %get-tuple-element.51), calls=%async_computation.2 | async-start | bytes 1179648 | tf_op jit(solution)/shard_map/all_to_all | solution.py:427
  119.5 5.2 %collective-permute-start.9 = (bf16[256,1536]{1,0:T(8,128)(2,1)}, bf16[256,1536]{1,0:T(8,128)(2,1)S(1)}, u32[]{:S(2)}, u32[]{:S(2)}) collective-permute-start(bf16[256,1536]{1,0:T(8,128)(2,1)} %get-tuple-element.49), channel_id=1, source_target_pairs={{0,32},{32,0},{1,33},{33,1},{2,34},{34,2},{3,35},{35,3},{4,36},{36... | collective-permute-start | bytes 2359304 | tf_op jit(solution)/shard_map/ppermute | solution.py:41
  122.5 4.4 %collective-permute-start.10 = (bf16[256,1536]{1,0:T(8,128)(2,1)}, bf16[256,1536]{1,0:T(8,128)(2,1)S(1)}, u32[]{:S(2)}, u32[]{:S(2)}) collective-permute-start(bf16[256,1536]{1,0:T(8,128)(2,1)} %get-tuple-element.50), channel_id=1, source_target_pairs={{0,32},{32,0},{1,33},{33,1},{2,34},{34,2},{3,35},{35,3},{4,36},{36... | collective-permute-start | bytes 2359304 | tf_op jit(solution)/shard_map/ppermute | solution.py:41
  124.6 20.9 %copy-start.3 = (bf16[256,1536]{1,0:T(8,128)(2,1)}, bf16[256,1536]{1,0:T(8,128)(2,1)S(1)}, u32[]{:S(2)}) copy-start(bf16[256,1536]{1,0:T(8,128)(2,1)S(1)} %collective-permute-done.9.mixed_rest_hbm) | copy-start | bytes 2359300
  126.9 18.6 %copy-start.4 = (bf16[256,1536]{1,0:T(8,128)(2,1)}, bf16[256,1536]{1,0:T(8,128)(2,1)S(1)}, u32[]{:S(2)}) copy-start(bf16[256,1536]{1,0:T(8,128)(2,1)S(1)} %collective-permute-done.10.dx_rest_hbm) | copy-start | bytes 2359300
  140.7 7.9 %collective-permute-start.11 = (f32[72,128]{1,0:T(8,128)S(1)}, f32[72,128]{1,0:T(8,128)S(1)}, u32[]{:S(2)}, u32[]{:S(2)}) collective-permute-start(f32[72,128]{1,0:T(8,128)S(1)} %convert_reduce_fusion), channel_id=1, source_target_pairs={{0,32},{32,0},{1,33},{33,1},{2,34},{34,2},{3,35},{35,3},{4,36},{36... | collective-permute-start | bytes 110600 | tf_op jit(solution)/shard_map/ppermute | solution.py:41
